TPU v7x, 32 devices: a whole 2x2x4 slice. The times are simulated.
32 devices in a mesh: groups: 2 (over y), gx: 8 (over z, x), gy: 2 (over core).
Axes of the slice: x: 2, y: 2, z: 4, core: 2. Of those that a mesh axis runs over, the one named last changes fastest.
Arguments:
- positions: float32 [16, 2, 3, 384], P(('groups', 'gx'), 'gy'), parts along dimension 0, may hold values from -1 to 17, as said below
- species: int32 [16, 2, 384], P(('groups', 'gx'), 'gy'), parts along dimension 0, may hold values from 0 to 4
- neighbours: int32 [16, 2, 32, 384], P(('groups', 'gx'), 'gy'), parts along dimension 0, may hold values from 0 to 1440, as said below
- send_x: int32 [16, 2, 2, 384], P(('groups', 'gx'), 'gy'), parts along dimension 0, may hold values from 0 to 383
- send_y: int32 [16, 2, 2, 144], P(('groups', 'gx'), 'gy'), parts along dimension 0, may hold values from 0 to 1151, as said below
- two_weight: float32 [18, 128], replicated, may hold values from -1.5 to 1.5
- two_bias: float32 [128], replicated, may hold values from -3 to 3
- env_weight: float32 [2, 128, 32], replicated, may hold values from -0.5 to 0.5
- value_weight: float32 [2, 128, 32], replicated, may hold values from -0.5 to 0.5
- latent_weight: float32 [2, 224, 128], replicated, may hold values from -0.375 to 0.375
- latent_bias: float32 [2, 128], replicated, may hold values from -3 to 3
- out_weight: float32 [128], replicated, may hold values from -0.5 to 0.5
- species_shift: float32 [5], replicated, may hold values from -1 to 1
Outputs:
- atom_energy: float32 [16, 2, 384], P(('groups', 'gx'), 'gy'), parts along dimension 0
- forces: float32 [16, 2, 3, 384], P(('groups', 'gx'), 'gy'), parts along dimension 0
- mean_energy: float32 [2], P('groups'), parts along dimension 0
There are 2 independent parts, one for each index of `groups`. A program takes and returns all parts, laid end to end along the dimension named above; an argument that names none is the same for every part. Nothing has to cross between parts.
Inputs may be any that keep to these rules, and one draw needn't show every extreme that they name: `neighbours`: entries equal to 1440 point to the padding slot. `send_y`: the two rows of a box hold distinct entries. `positions`: lattice sites jittered: two atoms of the extended list are at least 0.4 apart.
All inputs are finite; a program needn't handle non-finite values.
Results may differ from a plain program's by a relative error of at most 0.0003.
Values sent between devices are 32-bit elements; how exact they have to be, the bound alone decides.
No kernel may reach another device: no remote copies, remote signals or barrier semaphores. Data moves between devices by JAX's collectives and lax.ppermute only.
A program may use at most 256 MiB of HBM per device.

v0:
```python
from functools import partial
import math

import jax
import jax.numpy as jnp
from jax import lax
from jax.sharding import PartitionSpec as P

BASIS = 8
SPECIES = 5
LAYERS = 2
SITES_X = 2
SITES_Y = 16


cutoff_radius = 2.5


def passed_along(value, axis, by):
    count = lax.axis_size(axis)
    return lax.ppermute(value, axis, [(i, (i + by) % count) for i in range(count)])


def harmonics(unit):
    ux, uy, uz = (unit[0], unit[1], unit[2])
    root = math.sqrt(3.0)
    return jnp.stack(
        [
            jnp.ones_like(ux),
            ux,
            uy,
            uz,
            root * ux * uy,
            root * uy * uz,
            0.5 * (3.0 * uz * uz - 1.0),
            root * ux * uz,
            0.5 * root * (ux * ux - uy * uy),
        ]
    )


def geometry(ext_pos, nbrs):
    count, atoms = nbrs.shape
    index = nbrs.reshape(-1)
    other = jnp.take(ext_pos, index, axis=1)
    centre = jnp.tile(ext_pos[:, :atoms], (1, count))
    vector = other - centre
    dist = jnp.sqrt(jnp.sum(vector * vector, axis=0))
    unit = vector / dist
    scaled = jnp.minimum(dist / cutoff_radius, 1.0)
    envelope = 1.0 - 28.0 * scaled**6 + 48.0 * scaled**7 - 21.0 * scaled**8
    orders = (jnp.arange(BASIS) + 1).astype(jnp.float32)[:, None]
    radial = (
        math.sqrt(2.0 / cutoff_radius)
        * jnp.sin(orders * math.pi * dist / cutoff_radius)
        / dist
        * envelope
    )
    return (harmonics(unit), envelope, radial)


def pair_latent(radial, ext_spec, nbrs, two_weight, two_bias):
    count, atoms = nbrs.shape
    kinds = jnp.arange(SPECIES).astype(jnp.float32)[:, None]
    spec_centre = jnp.tile(ext_spec[:atoms], (count,))
    spec_other = jnp.take(ext_spec, nbrs.reshape(-1))
    onehot_c = (spec_centre[None] == kinds).astype(jnp.float32)
    onehot_o = (spec_other[None] == kinds).astype(jnp.float32)
    features = jnp.concatenate([onehot_c, onehot_o, radial], 0)
    pre = jnp.dot(two_weight.T, features, precision=lax.Precision.HIGHEST) + two_bias[:, None]
    return jax.nn.silu(pre)


def environment(latent, sph, envelope, weight, count, atoms):
    embed = jnp.dot(weight.T, latent, precision=lax.Precision.HIGHEST) * envelope
    width = embed.shape[0]
    product = sph[:, None, :] * embed[None]
    return product.reshape(9 * width, count, atoms).sum(1) / math.sqrt(count)


def advance(latent, sph, env_own, ghost_env, nbrs, value_w, latent_w, latent_b):
    count, atoms = nbrs.shape
    width = value_w.shape[1]
    value = jnp.dot(value_w.T, latent, precision=lax.Precision.HIGHEST)
    ext_env = jnp.concatenate([env_own, ghost_env], 1)
    env_centre = jnp.tile(env_own, (1, count))
    env_other = jnp.take(ext_env, nbrs.reshape(-1), axis=1)
    mixed = (env_centre + env_other).reshape(9, width, -1) * sph[:, None, :] * value[None]
    scalars = jnp.concatenate([mixed[0], mixed[1:4].sum(0), mixed[4:9].sum(0)], 0)
    joined = jnp.concatenate([latent, scalars], 0)
    pre = jnp.dot(latent_w.T, joined, precision=lax.Precision.HIGHEST) + latent_b[:, None]
    return latent + jax.nn.silu(pre)


def readout(latent, envelope, own_spec, nbrs, out_weight, species_shift):
    count, atoms = nbrs.shape
    edge = (
        jnp.dot(out_weight, latent, precision=lax.Precision.HIGHEST) * envelope / math.sqrt(count)
    )
    kinds = jnp.arange(SPECIES).astype(jnp.float32)[:, None]
    onehot = (own_spec[None] == kinds).astype(jnp.float32)
    offset = jnp.dot(species_shift, onehot, precision=lax.Precision.HIGHEST)
    return edge.reshape(count, atoms).sum(0) + offset


def extend_local(rows, lend_x, lend_y, off_x, off_y, padding):
    low = jnp.take(rows, lend_x[0], axis=1)
    high = jnp.take(rows, lend_x[1], axis=1)
    from_below = passed_along(high, "gx", 1) - off_x
    from_above = passed_along(low, "gx", -1) + off_x
    wide = jnp.concatenate([rows, from_below, from_above], 1)
    low_y = jnp.take(wide, lend_y[0], axis=1)
    high_y = jnp.take(wide, lend_y[1], axis=1)
    below_y = passed_along(high_y, "gy", 1)
    above_y = passed_along(low_y, "gy", -1)
    return jnp.concatenate([wide, below_y - off_y, above_y + off_y, padding], 1)


def return_ghosts(ghost_grad, atoms, lend_x, lend_y):
    depth = ghost_grad.shape[0]
    face_x = lend_x.shape[1]
    face_y = lend_y.shape[1]
    below_y = ghost_grad[:, 2 * face_x : 2 * face_x + face_y]
    above_y = ghost_grad[:, 2 * face_x + face_y : 2 * face_x + 2 * face_y]
    to_high = passed_along(below_y, "gy", -1)
    to_low = passed_along(above_y, "gy", 1)
    wide = jnp.concatenate([jnp.zeros((depth, atoms), jnp.float32), ghost_grad[:, : 2 * face_x]], 1)
    wide = wide.at[:, lend_y[0]].add(to_low).at[:, lend_y[1]].add(to_high)
    below_x = wide[:, atoms : atoms + face_x]
    above_x = wide[:, atoms + face_x : atoms + 2 * face_x]
    to_high_x = passed_along(below_x, "gx", -1)
    to_low_x = passed_along(above_x, "gx", 1)
    return wide[:, :atoms].at[:, lend_x[0]].add(to_low_x).at[:, lend_x[1]].add(to_high_x)


def first_section(ext_pos, ext_spec, nbrs, two_weight, two_bias, weight):
    count, atoms = nbrs.shape
    sph, envelope, radial = geometry(ext_pos, nbrs)
    latent = pair_latent(radial, ext_spec, nbrs, two_weight, two_bias)
    return (sph, envelope, latent, environment(latent, sph, envelope, weight, count, atoms))


def middle_section(
    sph, envelope, latent, env, ghost, nbrs, value_w, latent_w, latent_b, next_env_w
):
    count, atoms = nbrs.shape
    fresh = advance(latent, sph, env, ghost, nbrs, value_w, latent_w, latent_b)
    return (fresh, environment(fresh, sph, envelope, next_env_w, count, atoms))


def last_section(
    sph,
    envelope,
    latent,
    env,
    ghost,
    nbrs,
    value_w,
    latent_w,
    latent_b,
    own_spec,
    out_weight,
    species_shift,
):
    fresh = advance(latent, sph, env, ghost, nbrs, value_w, latent_w, latent_b)
    return readout(fresh, envelope, own_spec, nbrs, out_weight, species_shift)


def per_device(
    positions,
    species,
    neighbours,
    send_x,
    send_y,
    two_weight,
    two_bias,
    env_weight,
    value_weight,
    latent_weight,
    latent_bias,
    out_weight,
    species_shift,
):
    coords = positions[0, 0]
    nbrs = neighbours[0, 0]
    lend_x = send_x[0, 0]
    lend_y = send_y[0, 0]
    atoms = coords.shape[1]
    rows = jnp.concatenate([coords, species[0, 0][None].astype(jnp.float32)], 0)
    off_x = jnp.array([SITES_X, 0.0, 0.0, 0.0], jnp.float32)[:, None]
    off_y = jnp.array([0.0, SITES_Y, 0.0, 0.0], jnp.float32)[:, None]
    padding = jnp.array([0.0, 0.0, -1000.0, -1.0], jnp.float32)[:, None]
    extended = extend_local(rows, lend_x, lend_y, off_x, off_y, padding)
    ext_pos = extended[:3]
    ext_spec = extended[3]
    start = partial(
        first_section,
        ext_spec=ext_spec,
        nbrs=nbrs,
        two_weight=two_weight,
        two_bias=two_bias,
        weight=env_weight[0],
    )
    (sph, envelope, latent, env), pull_first = jax.vjp(start, ext_pos)
    zero = jnp.zeros((env.shape[0], 1), jnp.float32)
    pulls = []
    energies = None
    for layer in range(LAYERS):
        ghost = extend_local(env, lend_x, lend_y, zero, zero, zero)[:, atoms:]
        if layer + 1 < LAYERS:
            section = partial(
                middle_section,
                nbrs=nbrs,
                value_w=value_weight[layer],
                latent_w=latent_weight[layer],
                latent_b=latent_bias[layer],
                next_env_w=env_weight[layer + 1],
            )
            (latent, env), pull = jax.vjp(section, sph, envelope, latent, env, ghost)
        else:
            section = partial(
                last_section,
                nbrs=nbrs,
                value_w=value_weight[layer],
                latent_w=latent_weight[layer],
                latent_b=latent_bias[layer],
                own_spec=ext_spec[:atoms],
                out_weight=out_weight,
                species_shift=species_shift,
            )
            energies, pull = jax.vjp(section, sph, envelope, latent, env, ghost)
        pulls.append(pull)
    d_sph, d_cut, d_lat, d_env, d_ghost = pulls[LAYERS - 1](jnp.ones_like(energies))
    for layer in range(LAYERS - 1, -1, -1):
        d_env = d_env + return_ghosts(d_ghost, atoms, lend_x, lend_y)
        if layer > 0:
            g_sph, g_cut, d_lat, d_env, d_ghost = pulls[layer - 1]((d_lat, d_env))
            d_sph = d_sph + g_sph
            d_cut = d_cut + g_cut
    (d_ext,) = pull_first((d_sph, d_cut, d_lat, d_env))
    grad_own = d_ext[:, :atoms] + return_ghosts(d_ext[:, atoms:], atoms, lend_x, lend_y)
    total = lax.psum(jnp.sum(energies), ("gx", "gy"))
    mean_energy = total / (atoms * lax.axis_size("gx") * lax.axis_size("gy"))
    return (energies[None, None], (-grad_own)[None, None], mean_energy.reshape(1))


def solution(mesh):
    placed = (
        P(("groups", "gx"), "gy", None, None),
        P(("groups", "gx"), "gy", None),
        P(("groups", "gx"), "gy", None, None),
        P(("groups", "gx"), "gy", None, None),
        P(("groups", "gx"), "gy", None, None),
        P(),
        P(),
        P(),
        P(),
        P(),
        P(),
        P(),
        P(),
    )
    return jax.shard_map(
        per_device,
        mesh=mesh,
        in_specs=placed,
        out_specs=(
            P(("groups", "gx"), "gy", None),
            P(("groups", "gx"), "gy", None, None),
            P("groups"),
        ),
        check_vma=False,
    )
```

profile of v0, /device:TPU:0, one launch (start us, length us, event | category | flops | bytes accessed | tf_op | source)
XLA Modules:
  0.0 1145.6 jit_solution(12849989894226010347)
XLA Ops:
  24.8 68.0 %gather_fusion = f32[12288]{0:T(1024)S(1)} fusion(f32[1441]{0:T(1024)S(1)} %slice_reduce_fusion.4, s32[12288]{0:T(1024)S(1)} %broadcast_clamp_fusion.1), kind=kCustom, calls=%fused_computation.14 | custom fusion | bytes 147456 | tf_op jit(solution)/shard_map/jvp(jit(_take))/gather | solution.py:66
  93.2 41.0 %gather_fusion.1 = f32[12288,3]{1,0:T(8,128)} fusion(f32[3,1441]{0,1:T(8,128)S(1)} %copy.221, s32[12288]{0:T(1024)S(1)} %broadcast_clamp_fusion.1), kind=kCustom, calls=%fused_computation.15 | custom fusion | bytes 344064 | tf_op jit(solution)/shard_map/jvp(jit(_take))/gather | solution.py:45
  163.0 12.8 %copy.270 = f32[36,8,32,384]{3,2,1,0:T(8,128)} copy(f32[36,8,32,384]{3,1,2,0:T(8,128)} %bitcast.255) | data formatting | bytes 28311552
  202.8 9.4 collective-permute-done.5
  228.9 47.9 %gather_fusion.10 = f32[12288,288]{1,0:T(8,128)} fusion(f32[288,1441]{0,1:T(8,128)S(1)} %dynamic-update-slice.11, s32[12288]{0:T(1024)S(1)} %get-tuple-element.97), kind=kCustom, calls=%fused_computation.4.clone | custom fusion | bytes 28360704 | tf_op jit(solution)/shard_map/jvp(jit(_take))/gather | solution.py:87
  276.9 20.6 %bitcast_add_fusion.1 = f32[288,12288]{0,1:T(8,128)} fusion(f32[12288,288]{1,0:T(8,128)} %gather_fusion.10, f32[288,384]{0,1:T(8,128)S(1)} %get-tuple-element.86, pred[12288]{0:T(1024)(128)(4,1)S(1)} %get-tuple-element.59), kind=kLoop, calls=%fused_computation.36 | loop fusion | flops 7077888 | bytes 28766208 | tf_op jit(solution)/shard_map/jvp()/add | solution.py:88
  297.5 17.6 %copy.231 = f32[288,12288]{1,0:T(8,128)} copy(f32[288,12288]{0,1:T(8,128)} %bitcast_add_fusion.1) | data formatting | bytes 28311552 | tf_op jit(solution)/shard_map/jvp()/add | solution.py:88
  324.6 14.3 %multiply_add_fusion = (f32[128,12288]{1,0:T(8,128)}, f32[128,12288]{1,0:T(8,128)}) fusion(f32[128,12288]{1,0:T(8,128)} %copy-done.6, f32[128]{0:T(128)S(1)} %copy-done.57, f32[2,224,128]{2,1,0:T(8,128)S(1)} %copy-done.59, f32[32,12288]{1,0:T(8,128)S(1)} %slice_reduce_fusion.1, f32[32,12288]{1,0:T(8,128)} %slice_reduce_fusion.3, ...), kind=kOutput, calls=%fused_computation.117 | convolution fusion | flops 4245553152 | bytes 29999616 | tf_op jit(solution)/shard_map/jvp()/dot_general | solution.py:91
  352.3 12.7 %copy.271 = f32[36,8,32,384]{3,2,1,0:T(8,128)} copy(f32[36,8,32,384]{3,1,2,0:T(8,128)} %bitcast.256) | data formatting | bytes 28311552
  392.1 9.4 collective-permute-done.9
  418.4 47.7 %gather_fusion.15 = f32[12288,288]{1,0:T(8,128)} fusion(f32[288,1441]{0,1:T(8,128)S(1)} %dynamic-update-slice.5, s32[12288]{0:T(1024)S(1)} %get-tuple-element.97), kind=kCustom, calls=%fused_computation.13.clone | custom fusion | bytes 28360704 | tf_op jit(solution)/shard_map/jvp(jit(_take))/gather | solution.py:87
  466.1 20.6 %bitcast_add_fusion = f32[288,12288]{0,1:T(8,128)} fusion(f32[12288,288]{1,0:T(8,128)} %gather_fusion.15, f32[288,384]{0,1:T(8,128)S(1)} %get-tuple-element.84, pred[12288]{0:T(1024)(128)(4,1)S(1)} %get-tuple-element.59), kind=kLoop, calls=%fused_computation.35 | loop fusion | flops 7077888 | bytes 28766208 | tf_op jit(solution)/shard_map/jvp()/add | solution.py:88
  486.8 17.5 %copy.239 = f32[288,12288]{1,0:T(8,128)} copy(f32[288,12288]{0,1:T(8,128)} %bitcast_add_fusion) | data formatting | bytes 28311552 | tf_op jit(solution)/shard_map/jvp()/add | solution.py:88
  515.0 10.3 fusion.8
  525.3 16.4 %convolution_bitcast_fusion.1 = f32[224,12288]{1,0:T(8,128)} fusion(f32[128,12288]{1,0:T(8,128)} %fusion.8, f32[128]{0:T(128)S(1)} %copy-done.53, f32[12288]{0:T(1024)S(1)} %copy-done.35, f32[2,224,128]{2,1,0:T(8,128)S(1)} %copy-done.60), kind=kOutput, calls=%fused_computation.38 | convolution fusion | flops 4243587072 | bytes 17465856 | tf_op jit(solution)/shard_map/transpose(jvp())/dot_general | solution.py:91
  549.1 11.3 multiply_reduce_fusion.7
  560.3 12.7 %copy.272 = f32[36,8,32,384]{3,2,1,0:T(8,128)} copy(f32[36,8,32,384]{3,1,2,0:T(8,128)} %bitcast.245) | data formatting | bytes 28311552
  573.0 16.8 %copy.241 = f32[288,12288]{0,1:T(8,128)} copy(f32[288,12288]{1,0:T(8,128)} %bitcast.246) | data formatting | bytes 28311552 | tf_op jit(solution)/shard_map/transpose(jvp())/reshape | solution.py:88
  589.8 75.6 %scatter_custom_fusion = f32[288,1441]{0,1:T(8,128)} fusion(s32[12288]{0:T(1024)} %get-tuple-element.96, f32[288,12288]{0,1:T(8,128)} %copy.241, f32[]{:T(128)} %constant.84.clone.1), kind=kCustom, calls=%fused_computation.33 | custom fusion | flops 3538944 | bytes 20534912 | tf_op jit(solution)/shard_map/transpose(jvp(jit(_take)))/scatter-add | solution.py:87
  693.4 14.4 %collective-permute-done.14 = f32[288,384]{1,0:T(8,128)S(1)} collective-permute-done((f32[288,384]{1,0:T(8,128)S(1)}, f32[288,384]{1,0:T(8,128)S(1)}, u32[]{:S(2)}, u32[]{:S(2)}) %collective-permute-start.14) | collective-permute-done | bytes 442400 | tf_op jit(solution)/shard_map/ppermute | solution.py:21
  724.0 15.1 %reshape.428 = f32[9,32,12288]{2,1,0:T(8,128)} reshape(f32[288,32,384]{2,1,0:T(8,128)} %broadcast_in_dim.164) | data formatting | bytes 28311552 | tf_op jit(solution)/shard_map/transpose(jvp())/reshape | solution.py:78
  739.0 9.5 multiply_reduce_fusion.6
  753.8 8.8 fusion.5
  762.7 11.6 %convolution_bitcast_fusion = f32[224,12288]{1,0:T(8,128)S(1)} fusion(f32[128,12288]{1,0:T(8,128)S(1)} %bitcast.284, f32[128,12288]{1,0:T(8,128)S(1)} %fusion.5, f32[2,224,128]{2,1,0:T(8,128)S(1)} %copy-done.61), kind=kOutput, calls=%fused_computation.37 | convolution fusion | flops 4242014208 | bytes 23707648 | tf_op jit(solution)/shard_map/transpose(jvp())/dot_general | solution.py:91
  788.3 12.7 %copy.273 = f32[36,8,32,384]{3,2,1,0:T(8,128)} copy(f32[36,8,32,384]{3,1,2,0:T(8,128)} %bitcast.253) | data formatting | bytes 28311552
  801.0 16.8 %copy.250 = f32[288,12288]{0,1:T(8,128)} copy(f32[288,12288]{1,0:T(8,128)} %bitcast.254) | data formatting | bytes 28311552 | tf_op jit(solution)/shard_map/transpose(jvp())/reshape | solution.py:88
  817.8 75.6 %scatter_custom_fusion.5 = f32[288,1441]{0,1:T(8,128)} fusion(s32[12288]{0:T(1024)} %get-tuple-element.96, f32[288,12288]{0,1:T(8,128)} %copy.250, f32[]{:T(128)} %constant.84.clone.1), kind=kCustom, calls=%fused_computation.31 | custom fusion | flops 3538944 | bytes 20534912 | tf_op jit(solution)/shard_map/transpose(jvp(jit(_take)))/scatter-add | solution.py:87
  927.8 8.5 fusion.42
  962.1 15.2 %reshape.431 = f32[9,32,12288]{2,1,0:T(8,128)} reshape(f32[288,32,384]{2,1,0:T(8,128)} %broadcast_in_dim.168) | data formatting | bytes 28311552 | tf_op jit(solution)/shard_map/transpose(jvp())/reshape | solution.py:78
  977.3 16.1 %multiply_reduce_fusion.1 = (f32[32,12288]{1,0:T(8,128)S(1)}, f32[9,12288]{1,0:T(8,128)S(1)}, f32[9,12288]{1,0:T(8,128)S(1)}, f32[32,12288]{1,0:T(8,128)S(1)}) fusion(f32[1,32,12288]{2,1,0:T(8,128)} %copy-done.13, f32[3,32,12288]{2,1,0:T(8,128)} %copy-done.5, f32[5,32,12288]{2,1,0:T(8,128)} %copy-done.1, f32[9,32,12288]{2,1,0:T(8,128)} %bitcast.248, ...), kind=kLoop, calls=%fused_computation.58 | loop fusion | flops 41459712 | bytes 50085888 | tf_op jit(solution)/shard_map/transpose(jvp())/reduce_sum | solution.py:88
  1023.6 66.2 %scatter_fusion.4 = f32[3,1441]{0,1:T(8,128)S(1)} fusion(f32[3,1441]{0,1:T(8,128)S(1)} %pad.42, s32[12288]{0:T(1024)S(1)} %bitcast.267, f32[12288,3]{1,0:T(8,128)} %copy.260), kind=kCustom, calls=%fused_computation.26 | custom fusion | flops 36864 | bytes 491520 | tf_op jit(solution)/shard_map/transpose(jvp(jit(_take)))/scatter-add | solution.py:45
  1102.4 34.2 %psum.7 = f32[]{:T(128)} all-reduce(f32[]{:T(128)} %get-tuple-element.50), channel_id=1, replica_groups=mesh['groups'=2,'gx'=8,'gy'=2] {'gx','gy'}, use_global_device_ids=true, to_apply=%region_41.47 | all-reduce | flops 1 | bytes 8 | tf_op jit(solution)/shard_map/psum | solution.py:242
  (392 shorter events, 353.8 us)
Async XLA Ops:
  0.6 141.5 %copy-start = (f32[18,128]{1,0:T(8,128)S(1)}, f32[18,128]{1,0:T(8,128)}, u32[]{:S(2)}) copy-start(f32[18,128]{1,0:T(8,128)} %param.31) | copy-start | bytes 27652
  4.3 12.8 %collective-permute-start = (f32[4,384]{0,1:T(8,128)S(1)}, f32[4,384]{0,1:T(8,128)S(1)}, u32[]{:S(2)}, u32[]{:S(2)}) collective-permute-start(f32[4,384]{0,1:T(8,128)S(1)} %select_bitcast_fusion.9), channel_id=1, source_target_pairs={{0,2},{2,4},{4,6},{6,8},{8,10},{10,12},{12,14},{14,0},{1,3},{3,5},... | collective-permute-start | bytes 18440 | tf_op jit(solution)/shard_map/ppermute | solution.py:21
  8.5 10.6 collective-permute-start.1
  12.1 128.5 %copy-start.51 = (f32[8]{0:T(128)}, f32[8]{0:T(128)S(1)}, u32[]{:S(2)}) copy-start(f32[8]{0:T(128)S(1)} %get-tuple-element.120) | copy-start | bytes 100
  13.6 210.3 %copy-start.47 = (pred[144]{0:T(512)(128)(4,1)}, pred[144]{0:T(512)(128)(4,1)S(1)}, u32[]{:S(2)}) copy-start(pred[144]{0:T(512)(128)(4,1)S(1)} %compare_and_fusion.3) | copy-start | bytes 436
  16.9 125.1 %copy-start.54 = (f32[5]{0:T(128)}, f32[5]{0:T(128)S(1)}, u32[]{:S(2)}) copy-start(f32[5]{0:T(128)S(1)} %iota_convert_fusion) | copy-start | bytes 64
  21.4 1.2 collective-permute-start.2
  21.6 1.7 collective-permute-start.3
  139.6 199.4 %copy-start.21 = (f32[12288]{0:T(1024)}, f32[12288]{0:T(1024)S(1)}, u32[]{:S(2)}) copy-start(f32[12288]{0:T(1024)S(1)} %get-tuple-element.55) | copy-start | bytes 147460
  190.1 22.0 %collective-permute-start.5 = (f32[288,384]{1,0:T(8,128)}, f32[288,384]{1,0:T(8,128)}, u32[]{:S(2)}, u32[]{:S(2)}) collective-permute-start(f32[288,384]{1,0:T(8,128)} %copy.226), channel_id=1, source_target_pairs={{0,14},{2,0},{4,2},{6,4},{8,6},{10,8},{12,10},{14,12},{1,15},{3,1}... | collective-permute-start | bytes 1327112 | tf_op jit(solution)/shard_map/ppermute | solution.py:21
  195.0 18.4 %collective-permute-start.4 = (f32[288,384]{1,0:T(8,128)}, f32[288,384]{1,0:T(8,128)}, u32[]{:S(2)}, u32[]{:S(2)}) collective-permute-start(f32[288,384]{1,0:T(8,128)} %copy.225), channel_id=1, source_target_pairs={{0,2},{2,4},{4,6},{6,8},{8,10},{10,12},{12,14},{14,0},{1,3},{3,5},... | collective-permute-start | bytes 1327112 | tf_op jit(solution)/shard_map/ppermute | solution.py:21
  226.0 1.8 collective-permute-start.6
  227.2 1.7 collective-permute-start.7
  379.3 22.2 %collective-permute-start.9 = (f32[288,384]{1,0:T(8,128)}, f32[288,384]{1,0:T(8,128)}, u32[]{:S(2)}, u32[]{:S(2)}) collective-permute-start(f32[288,384]{1,0:T(8,128)} %copy.234), channel_id=1, source_target_pairs={{0,14},{2,0},{4,2},{6,4},{8,6},{10,8},{12,10},{14,12},{1,15},{3,1}... | collective-permute-start | bytes 1327112 | tf_op jit(solution)/shard_map/ppermute | solution.py:21
  385.6 17.2 %collective-permute-start.8 = (f32[288,384]{1,0:T(8,128)}, f32[288,384]{1,0:T(8,128)}, u32[]{:S(2)}, u32[]{:S(2)}) collective-permute-start(f32[288,384]{1,0:T(8,128)} %copy.233), channel_id=1, source_target_pairs={{0,2},{2,4},{4,6},{6,8},{8,10},{10,12},{12,14},{14,0},{1,3},{3,5},... | collective-permute-start | bytes 1327112 | tf_op jit(solution)/shard_map/ppermute | solution.py:21
  415.5 1.8 collective-permute-start.10
  416.6 1.7 collective-permute-start.11
  667.2 14.4 %collective-permute-start.13 = (f32[288,144]{0,1:T(8,128)S(1)}, f32[288,144]{0,1:T(8,128)}, u32[]{:S(2)}, u32[]{:S(2)}) collective-permute-start(f32[288,144]{0,1:T(8,128)S(1)} %get-tuple-element.69), channel_id=1, source_target_pairs={{0,1},{1,0},{2,3},{3,2},{4,5},{5,4},{6,7},{7,6},{8,9},{9,8},{10,11... | collective-permute-start | bytes 497672 | tf_op jit(solution)/shard_map/ppermute | solution.py:21
  667.6 9.3 collective-permute-start.12
  688.1 19.7 %collective-permute-start.14 = (f32[288,384]{1,0:T(8,128)S(1)}, f32[288,384]{1,0:T(8,128)S(1)}, u32[]{:S(2)}, u32[]{:S(2)}) collective-permute-start(f32[288,384]{1,0:T(8,128)S(1)} %copy.243), channel_id=1, source_target_pairs={{0,2},{2,4},{4,6},{6,8},{8,10},{10,12},{12,14},{14,0},{1,3},{3,5},... | collective-permute-start | bytes 1327112 | tf_op jit(solution)/shard_map/ppermute | solution.py:21
  688.4 22.0 %collective-permute-start.15 = (f32[288,384]{1,0:T(8,128)S(1)}, f32[288,384]{1,0:T(8,128)}, u32[]{:S(2)}, u32[]{:S(2)}) collective-permute-start(f32[288,384]{1,0:T(8,128)S(1)} %copy.245), channel_id=1, source_target_pairs={{0,14},{2,0},{4,2},{6,4},{8,6},{10,8},{12,10},{14,12},{1,15},{3,1}... | collective-permute-start | bytes 1327112 | tf_op jit(solution)/shard_map/ppermute | solution.py:21
  894.5 17.5 %collective-permute-start.17 = (f32[288,144]{0,1:T(8,128)S(1)}, f32[288,144]{0,1:T(8,128)}, u32[]{:S(2)}, u32[]{:S(2)}) collective-permute-start(f32[288,144]{0,1:T(8,128)S(1)} %get-tuple-element.67), channel_id=1, source_target_pairs={{0,1},{1,0},{2,3},{3,2},{4,5},{5,4},{6,7},{7,6},{8,9},{9,8},{10,11... | collective-permute-start | bytes 497672 | tf_op jit(solution)/shard_map/ppermute | solution.py:21
  894.6 12.9 %collective-permute-start.16 = (f32[288,144]{0,1:T(8,128)S(1)}, f32[288,144]{0,1:T(8,128)}, u32[]{:S(2)}, u32[]{:S(2)}) collective-permute-start(f32[288,144]{0,1:T(8,128)S(1)} %get-tuple-element.68), channel_id=1, source_target_pairs={{0,1},{1,0},{2,3},{3,2},{4,5},{5,4},{6,7},{7,6},{8,9},{9,8},{10,11... | collective-permute-start | bytes 497672 | tf_op jit(solution)/shard_map/ppermute | solution.py:21
  922.9 19.8 %collective-permute-start.18 = (f32[288,384]{1,0:T(8,128)}, f32[288,384]{1,0:T(8,128)}, u32[]{:S(2)}, u32[]{:S(2)}) collective-permute-start(f32[288,384]{1,0:T(8,128)} %copy.252), channel_id=1, source_target_pairs={{0,2},{2,4},{4,6},{6,8},{8,10},{10,12},{12,14},{14,0},{1,3},{3,5},... | collective-permute-start | bytes 1327112 | tf_op jit(solution)/shard_map/ppermute | solution.py:21
  923.0 21.7 %collective-permute-start.19 = (f32[288,384]{1,0:T(8,128)S(1)}, f32[288,384]{1,0:T(8,128)}, u32[]{:S(2)}, u32[]{:S(2)}) collective-permute-start(f32[288,384]{1,0:T(8,128)S(1)} %copy.254), channel_id=1, source_target_pairs={{0,14},{2,0},{4,2},{6,4},{8,6},{10,8},{12,10},{14,12},{1,15},{3,1}... | collective-permute-start | bytes 1327112 | tf_op jit(solution)/shard_map/ppermute | solution.py:21
  1019.2 71.3 %copy-start.45 = (f32[384]{0:T(512)S(1)}, f32[384]{0:T(512)}, u32[]{:S(2)}) copy-start(f32[384]{0:T(512)} %copy-done.44) | copy-start | bytes 4612
  1019.2 71.3 %copy-start.55 = (f32[5]{0:T(128)S(1)}, f32[5]{0:T(128)}, u32[]{:S(2)}) copy-start(f32[5]{0:T(128)} %copy-done.54) | copy-start | bytes 64
  1019.2 71.3 %copy-start.63 = (f32[5]{0:T(128)S(1)}, f32[5]{0:T(128)}, u32[]{:S(2)}) copy-start(f32[5]{0:T(128)} %param.38) | copy-start | bytes 64
  1089.9 3.1 collective-permute-start.21
  1090.0 1.4 collective-permute-start.20
  1094.6 46.1 %collective-permute-start.23 = (f32[3,384]{0,1:T(8,128)S(1)}, f32[3,384]{0,1:T(8,128)S(1)}, u32[]{:S(2)}, u32[]{:S(2)}) collective-permute-start(f32[3,384]{0,1:T(8,128)S(1)} %get-tuple-element.81), channel_id=1, source_target_pairs={{0,14},{2,0},{4,2},{6,4},{8,6},{10,8},{12,10},{14,12},{1,15},{3,1}... | collective-permute-start | bytes 13832 | tf_op jit(solution)/shard_map/ppermute | solution.py:21
  1101.8 36.0 %collective-permute-start.22 = (f32[3,384]{0,1:T(8,128)S(1)}, f32[3,384]{0,1:T(8,128)S(1)}, u32[]{:S(2)}, u32[]{:S(2)}) collective-permute-start(f32[3,384]{0,1:T(8,128)S(1)} %get-tuple-element.82), channel_id=1, source_target_pairs={{0,2},{2,4},{4,6},{6,8},{8,10},{10,12},{12,14},{14,0},{1,3},{3,5},... | collective-permute-start | bytes 13832 | tf_op jit(solution)/shard_map/ppermute | solution.py:21
  (67 other events, 723.7 us)
where the time goes:
time: 1160 us; the launch traced here: 1150 us
  local copies, waits for them, and re-layouts  460 us (40%)
  other arithmetic  438 us (38%)
  matrix products  130 us (11%)
  waiting for transfers between devices  46 us (4%)
  blocking collectives  34.2 us (3%)
  starting transfers between devices  33.5 us (3%)
    scatter-add x2, other arithmetic, advance(): env_other = jnp.take(ext_env, nbrs.reshape(-1), axis=1)  151 us
    gather x2, local copies, waits for them, and re-layouts, advance(): env_other = jnp.take(ext_env, nbrs.reshape(-1), axis=1)  95.7 us
    gather x1, local copies, waits for them, and re-layouts, pair_latent(): spec_other = jnp.take(ext_spec, nbrs.reshape(-1))  68 us
    scatter-add x1, other arithmetic, geometry(): other = jnp.take(ext_pos, index, axis=1)  66.2 us
    unnamed x165, local copies, waits for them, and re-layouts  61.8 us
    dot_general x4, matrix products, advance(): jnp.dot(latent_w.T, joined, precision=lax.Precision.HIGHEST)  52.6 us
    ppermute x24, waiting for transfers between devices, passed_along(): lax.ppermute(value, axis, [(i, (i + by) % count) for i in range(count)])  46 us
    gather x2, local copies, waits for them, and re-layouts, geometry(): other = jnp.take(ext_pos, index, axis=1)  45.4 us
  transfers between devices with their start and end apart: 24, of which 10 were waited for; matrix products, arithmetic and copies ran while one was open for 7% of the time, Pallas kernels for 0%

commit v1 on v0

v1 whole, which is shorter than its diff:
```python
from functools import partial
import math

import jax
import jax.numpy as jnp
from jax import lax
from jax.experimental import pallas as pl
from jax.experimental.pallas import tpu as pltpu
from jax.sharding import PartitionSpec as P

BASIS = 8
SPECIES = 5
SITES_X = 2
SITES_Y = 16
CUTOFF = 2.5
LATENT = 128
TENSORS = 32
HARM = 9
ROOT3 = math.sqrt(3.0)
DEGREE = (0, 1, 1, 1, 2, 2, 2, 2, 2)
F32 = jnp.float32
BF16 = jnp.bfloat16
WHOLE = pl.BlockSpec(memory_space=pltpu.VMEM)
SCALARS = pl.BlockSpec(memory_space=pltpu.SMEM)


def params():
    return pltpu.CompilerParams(vmem_limit_bytes=60 << 20)


def passed_along(value, axis, by):
    count = lax.axis_size(axis)
    return lax.ppermute(value, axis, [(i, (i + by) % count) for i in range(count)])


def dot(a, b):
    return jnp.dot(a, b, preferred_element_type=F32)


def dot_nt(a, b):
    return lax.dot_general(a, b, (((1,), (1,)), ((), ())), preferred_element_type=F32)


def halves(value):
    high = value.astype(BF16)
    return high, (value - high.astype(F32)).astype(BF16)


def stacked(value):
    return jnp.concatenate(halves(value), 0)


def product(weights, value):
    rows = weights.shape[0] // 2
    both = dot(weights, stacked(value))
    return both[:rows] + both[rows:]


def rounded(value):
    high = value.astype(BF16).astype(F32)
    return high, value - high


def weights_kernel(two, bias, env, val, lat, lat_bias, out_w, *outs):
    two_out, mix_out, s_out, back_out, ev_out, rad_out, cols = outs

    def depth_stack(piece):
        high, low = rounded(piece)
        top = jnp.concatenate([high, high], 0)
        bottom = jnp.concatenate([low, jnp.zeros_like(low)], 0)
        return top.T, bottom.T

    def join(pieces):
        tops, bottoms = zip(*[depth_stack(p) for p in pieces])
        return jnp.concatenate(list(tops) + list(bottoms), 0).astype(BF16)

    def wide_stack(piece):
        high, low = rounded(piece)
        top = jnp.concatenate([high, high], 1)
        bottom = jnp.concatenate([low, jnp.zeros_like(low)], 1)
        return jnp.concatenate([top, bottom], 0).astype(BF16)

    width = two.shape[1]
    first = jnp.concatenate(
        [
            two[0:SPECIES, :],
            bias[...],
            jnp.zeros((2, width), F32),
            two[SPECIES : 2 * SPECIES, :],
            jnp.zeros((3, width), F32),
            two[2 * SPECIES :, :],
        ],
        0,
    )
    two_out[...] = join([first])
    rad_out[...] = wide_stack(two[2 * SPECIES :, :])
    for layer in range(env.shape[0]):
        latent = lat[layer]
        mix_out[layer] = join([env[layer], val[layer], latent[:width]])
        s_out[layer] = join([latent[width:]])
        back_out[layer] = wide_stack(latent)
        high = [rounded(env[layer].T), rounded(val[layer].T)]
        top = jnp.concatenate([high[0][0], high[1][0]] * 2, 0).T
        bottom = jnp.concatenate([high[0][1], high[1][1]] + [jnp.zeros_like(high[0][1])] * 2, 0).T
        ev_out[layer] = jnp.concatenate([top, bottom], 0).astype(BF16)
    columns = jnp.concatenate(
        [lat_bias[...], out_w[...], jnp.zeros((8 - lat_bias.shape[0] - 1, width), F32)], 0
    )
    cols[...] = columns.T


def prepare_weights(two, bias, env, val, lat, lat_bias, out_w):
    layers = env.shape[0]
    shapes = [
        (2 * LATENT, 48),
        (layers, 2 * (LATENT + 2 * TENSORS), 2 * LATENT),
        (layers, 2 * LATENT, 6 * TENSORS),
        (layers, 2 * (LATENT + 3 * TENSORS), 2 * LATENT),
        (layers, 2 * LATENT, 4 * TENSORS),
        (2 * BASIS, 2 * LATENT),
    ]
    out_shape = [jax.ShapeDtypeStruct(s, BF16) for s in shapes]
    out_shape.append(jax.ShapeDtypeStruct((LATENT, 8), F32))
    return pl.pallas_call(
        weights_kernel,
        out_shape=out_shape,
        in_specs=[WHOLE] * 7,
        out_specs=[WHOLE] * 7,
        compiler_params=params(),
        name="prepare_weights",
    )(two, bias[None], env, val, lat, lat_bias, out_w[None])


def shifted(rows, by_x, by_y):
    lane_row = lax.broadcasted_iota(jnp.int32, rows.shape, 0)
    return rows + jnp.where(lane_row == 0, by_x, jnp.where(lane_row == 1, by_y, 0.0))


def lane_pick(table, row, index, blocks):
    low = index & 127
    high = lax.shift_right_arithmetic(index, 7)
    found = jnp.zeros(index.shape, F32)
    for block in range(blocks):
        span = slice(block * 128, block * 128 + 128)
        source = table[...][:, span] if row is None else table[row : row + 1, span]
        source = jnp.broadcast_to(source, index.shape)
        taken = jnp.take_along_axis(source, low, axis=1)
        found = jnp.where(high == block, taken, found)
    return found


def fill_wide(own, below, above, table, remap):
    atoms = own.shape[1]
    table[:, 0:atoms] = own[...]
    table[:, atoms : 2 * atoms] = shifted(below[...], -float(SITES_X), 0.0)
    table[:, 2 * atoms : 3 * atoms] = shifted(above[...], float(SITES_X), 0.0)
    lanes = lax.broadcasted_iota(jnp.int32, (1, atoms), 1).astype(F32)
    remap[:, 0:atoms] = lanes
    remap[:, atoms : 2 * atoms] = below[5:6, :] + float(atoms)
    remap[:, 2 * atoms : 3 * atoms] = above[4:5, :] + float(2 * atoms)


def lend_kernel(own, below, above, wanted, rows_out, wanted_out, table, remap):
    atoms = own.shape[1]
    blocks = 3 * atoms // 128
    fill_wide(own, below, above, table, remap)
    for tile in range(wanted.shape[1] // 128):
        span = slice(tile * 128, tile * 128 + 128)
        index = jnp.broadcast_to(wanted[:, span], (8, 128))
        place = lane_pick(remap, 0, index, blocks).astype(jnp.int32)
        place = jnp.where(index < 0, -1, place)
        wanted_out[:, span] = place[0:1]
        rows_out[:, span] = lane_pick(table, None, place, blocks)


def lend_rows(own, below, above, wanted):
    atoms = own.shape[1]
    return pl.pallas_call(
        lend_kernel,
        out_shape=[
            jax.ShapeDtypeStruct(wanted.shape[:0] + (8, wanted.shape[1]), F32),
            jax.ShapeDtypeStruct(wanted.shape, jnp.int32),
        ],
        in_specs=[WHOLE] * 4,
        out_specs=[WHOLE] * 2,
        scratch_shapes=[pltpu.VMEM((8, 3 * atoms), F32), pltpu.VMEM((1, 3 * atoms), F32)],
        compiler_params=params(),
        name="lend_rows",
    )(own, below, above, wanted)


def distances(vx, vy, vz):
    dist = jnp.sqrt(vx * vx + vy * vy + vz * vz)
    inverse = 1.0 / dist
    scaled = jnp.minimum(dist * (1.0 / CUTOFF), 1.0)
    second = scaled * scaled
    fourth = second * second
    sixth = fourth * second
    cut = 1.0 - 28.0 * sixth + 48.0 * (sixth * scaled) - 21.0 * (sixth * second)
    rest = 1.0 - scaled
    slope = (-168.0 / CUTOFF) * (fourth * scaled) * (rest * rest)
    angle = scaled * math.pi
    return inverse, cut, slope, jnp.sin(angle), jnp.cos(angle)


def geometry_kernel(
    own, below, above, across, nbrs, shift, vec_out, geo_out, nbr_out, base_out, table, remap, face
):
    atoms = own.shape[1]
    slots = nbrs.shape[0]
    blocks = table.shape[1] // 128
    fill_wide(own, below, above, table, remap)
    lanes = lax.broadcasted_iota(jnp.int32, (8, atoms), 1)
    rows = lax.broadcasted_iota(jnp.int32, (8, atoms), 0)
    moved = across[...] + jnp.where(
        rows == 1, jnp.where(lanes < face, -float(SITES_Y), float(SITES_Y)), 0.0
    )
    empty = jnp.where(rows == 2, -1000.0, jnp.where(rows == 3, -1.0, 0.0))
    table[:, 3 * atoms : 4 * atoms] = jnp.where(lanes < 2 * face, moved, empty)
    remap[:, 3 * atoms : 4 * atoms] = (
        lax.broadcasted_iota(jnp.int32, (1, atoms), 1) + 3 * atoms
    ).astype(F32)
    base = jnp.zeros((1, atoms), F32)
    for kind in range(SPECIES):
        base = base + jnp.where(own[3:4, :] == float(kind), shift[kind], 0.0)
    base_out[...] = base
    for group in range(slots // 8):
        for tile in range(atoms // 128):
            up = slice(group * 8, group * 8 + 8)
            span = slice(tile * 128, tile * 128 + 128)
            index = nbrs[up, span]
            index = lane_pick(remap, 0, index, blocks).astype(jnp.int32)
            nbr_out[up, span] = index
            vx = lane_pick(table, 0, index, blocks) - own[0:1, span]
            vy = lane_pick(table, 1, index, blocks) - own[1:2, span]
            vz = lane_pick(table, 2, index, blocks) - own[2:3, span]
            kind = lane_pick(table, 3, index, blocks)
            vec_out[0, up, span] = vx
            vec_out[1, up, span] = vy
            vec_out[2, up, span] = vz
            inverse, cut, _, sine, cosine = distances(vx, vy, vz)
            ux, uy, uz = vx * inverse, vy * inverse, vz * inverse
            harm = [
                ux,
                uy,
                uz,
                ROOT3 * ux * uy,
                ROOT3 * uy * uz,
                0.5 * (3.0 * uz * uz - 1.0),
                ROOT3 * ux * uz,
                0.5 * ROOT3 * (ux * ux - uy * uy),
            ]
            geo_out[0, up, span] = cut
            for number, value in enumerate(harm):
                geo_out[1 + number, up, span] = value
            scale = math.sqrt(2.0 / CUTOFF) * inverse * cut
            before, now = jnp.zeros_like(sine), sine
            for number in range(BASIS):
                geo_out[9 + number, up, span] = now * scale
                before, now = now, 2.0 * cosine * now - before
            geo_out[17, up, span] = kind


def geometry(own, below, above, across, nbrs, shift, face):
    slots, atoms = nbrs.shape
    return pl.pallas_call(
        partial(geometry_kernel, face=face),
        out_shape=[
            jax.ShapeDtypeStruct((3, slots, atoms), F32),
            jax.ShapeDtypeStruct((18, slots, atoms), F32),
            jax.ShapeDtypeStruct((slots, atoms), jnp.int32),
            jax.ShapeDtypeStruct((1, atoms), F32),
        ],
        in_specs=[WHOLE] * 5 + [SCALARS],
        out_specs=[WHOLE] * 4,
        scratch_shapes=[pltpu.VMEM((8, 4 * atoms), F32), pltpu.VMEM((1, 4 * atoms), F32)],
        compiler_params=params(),
        name="geometry",
    )(own, below, above, across, nbrs, shift)


def silu_pair(pre):
    gate = 1.0 / (1.0 + jnp.exp(-pre))
    value = pre * gate
    return value, gate + value * (1.0 - gate)


def first_kernel(
    geo, own, two_w, mix_w, cols, x_out, slope_out, emb_out, val_out, lx_out, env_out, *, group
):
    step = pl.program_id(0)
    atoms = own.shape[1]
    norm = 1.0 / math.sqrt(geo.shape[1])
    kinds = lax.broadcasted_iota(jnp.int32, (8, atoms), 0)
    kinds_f = kinds.astype(F32)
    centre = jnp.where((own[3:4, :] == kinds_f) & (kinds < SPECIES), 1.0, 0.0)
    centre = jnp.where(kinds == SPECIES, 1.0, centre)
    parts = []
    for q in range(group):
        k = step * group + q
        other = jnp.where(geo[17, pl.ds(k, 1), :] == kinds_f, 1.0, 0.0)
        radial = [geo[9 + n, pl.ds(k, 1), :] for n in range(BASIS)]
        parts.append(jnp.concatenate([centre, other] + radial, 0))
    features = jnp.concatenate(parts, 1)
    x, slope = silu_pair(product(two_w[...], features))
    x_out[...] = x
    slope_out[...] = slope
    mixed = product(mix_w[0], x)
    emb_out[...] = mixed[:TENSORS]
    val_out[...] = mixed[TENSORS : 2 * TENSORS]
    lx_out[...] = mixed[2 * TENSORS :] + cols[:, 0:1]

    @pl.when(step == 0)
    def _():
        env_out[...] = jnp.zeros_like(env_out)

    add_env(geo, step, group, mixed, env_out, atoms, norm)


def add_env(geo, step, group, embed, env_out, atoms, norm):
    for m in range(HARM):
        total = env_out[m * TENSORS : (m + 1) * TENSORS, :]
        for q in range(group):
            k = step * group + q
            cut = geo[0, pl.ds(k, 1), :] * norm
            factor = cut if m == 0 else cut * geo[m, pl.ds(k, 1), :]
            total = total + embed[:TENSORS, q * atoms : (q + 1) * atoms] * factor
        env_out[m * TENSORS : (m + 1) * TENSORS, :] = total


def edge_spec(rows, width):
    return pl.BlockSpec((rows, width), lambda i: (0, i))


def edge_shape(rows, edges):
    return jax.ShapeDtypeStruct((rows, edges), F32)


def first_pass(geo, own, two_w, mix_w, cols, group):
    _, slots, atoms = geo.shape
    width = group * atoms
    edges = slots * atoms
    rows = (LATENT, LATENT, TENSORS, TENSORS, LATENT)
    return pl.pallas_call(
        partial(first_kernel, group=group),
        grid=(slots // group,),
        out_shape=[edge_shape(r, edges) for r in rows] + [edge_shape(HARM * TENSORS, atoms)],
        in_specs=[WHOLE] * 5,
        out_specs=[edge_spec(r, width) for r in rows] + [WHOLE],
        compiler_params=params(),
        name="first_pass",
    )(geo, own, two_w, mix_w, cols)


def lend_env_kernel(own, below, above, wanted, out):
    atoms = own.shape[1]
    total = jnp.zeros(out.shape, F32)
    for number, block in enumerate((own, below, above)):
        rows = lax.broadcasted_iota(jnp.int32, (atoms, wanted.shape[1]), 0) + number * atoms
        chosen = (rows == wanted[...]).astype(F32).astype(BF16)
        both = dot(stacked(block[...]), chosen)
        total = total + both[: out.shape[0]] + both[out.shape[0] :]
    out[...] = total


def lend_env(own, below, above, wanted):
    return pl.pallas_call(
        lend_env_kernel,
        out_shape=jax.ShapeDtypeStruct(own.shape, F32),
        in_specs=[WHOLE] * 4,
        out_specs=WHOLE,
        compiler_params=params(),
        name="lend_env",
    )(own, below, above, wanted)


def take_back_kernel(returned, wanted, below, above, own, own_out, below_out, above_out):
    atoms = own.shape[1]
    rows_total = returned.shape[0]
    value = stacked(returned[...])
    for number, (block, out) in enumerate(((own, own_out), (below, below_out), (above, above_out))):
        rows = lax.broadcasted_iota(jnp.int32, (atoms, wanted.shape[1]), 0) + number * atoms
        chosen = (rows == wanted[...]).astype(F32).astype(BF16)
        both = dot_nt(value, chosen)
        out[...] = block[...] + both[:rows_total] + both[rows_total:]


def take_back(returned, wanted, own, below, above):
    return pl.pallas_call(
        take_back_kernel,
        out_shape=[jax.ShapeDtypeStruct(own.shape, F32)] * 3,
        in_specs=[WHOLE] * 5,
        out_specs=[WHOLE] * 3,
        compiler_params=params(),
        name="take_back",
    )(returned, wanted, below, above, own)


def chosen_columns(nbrs, step, group, columns):
    parts = []
    for q in range(group):
        index = nbrs[pl.ds(step * group + q, 1), :]
        rows = lax.broadcasted_iota(jnp.int32, (columns, index.shape[1]), 0)
        parts.append((rows == index).astype(F32).astype(BF16))
    return jnp.concatenate(parts, 1)


def fill_split(own, below, above, across, split):
    atoms = own.shape[1]
    rows = own.shape[0]
    for number, block in enumerate((own, below, above, across)):
        span = slice(number * atoms, (number + 1) * atoms)
        high, low = halves(block[...])
        split[:rows, span] = high
        split[rows:, span] = low


def gathered(split, chosen, own, g, group):
    rows = HARM * TENSORS
    atoms = own.shape[1]
    both = dot(split[...], chosen)
    for q in range(group):
        span = slice(q * atoms, (q + 1) * atoms)
        g[:, span] = both[:rows, span] + both[rows:, span] + own[...]


def contracted(geo, step, group, g, value, atoms):
    columns = []
    for q in range(group):
        k = step * group + q
        span = slice(q * atoms, (q + 1) * atoms)
        sums = [g[0:TENSORS, span], None, None]
        for m in range(1, HARM):
            term = g[m * TENSORS : (m + 1) * TENSORS, span] * geo[m, pl.ds(k, 1), :]
            d = DEGREE[m]
            sums[d] = term if sums[d] is None else sums[d] + term
        columns.append(jnp.concatenate(sums, 0))
    sums = jnp.concatenate(columns, 1)
    return sums, sums * jnp.concatenate([value] * 3, 0)


def middle_kernel(
    geo, nbrs, own, below, above, across, x, lx, val, s_w, mix_w, cols,
    g, slope_out, x_out, emb_out, val_out, lx_out, env_out, split, *, group,
):
    step = pl.program_id(0)
    atoms = own.shape[1]
    norm = 1.0 / math.sqrt(geo.shape[1])

    @pl.when(step == 0)
    def _():
        fill_split(own, below, above, across, split)
        env_out[...] = jnp.zeros_like(env_out)

    chosen = chosen_columns(nbrs, step, group, split.shape[1])
    gathered(split, chosen, own, g, group)
    _, s = contracted(geo, step, group, g, val[...], atoms)
    update, slope = silu_pair(lx[...] + product(s_w[0], s))
    slope_out[...] = slope
    fresh = x[...] + update
    x_out[...] = fresh
    mixed = product(mix_w[1], fresh)
    emb_out[...] = mixed[:TENSORS]
    val_out[...] = mixed[TENSORS : 2 * TENSORS]
    lx_out[...] = mixed[2 * TENSORS :] + cols[:, 1:2]
    add_env(geo, step, group, mixed, env_out, atoms, norm)


def middle_pass(geo, nbrs, blocks, x, lx, val, s_w, mix_w, cols, group):
    _, slots, atoms = geo.shape
    width = group * atoms
    edges = slots * atoms
    rows = (HARM * TENSORS, LATENT, LATENT, TENSORS, TENSORS, LATENT)
    return pl.pallas_call(
        partial(middle_kernel, group=group),
        grid=(slots // group,),
        out_shape=[edge_shape(r, edges) for r in rows] + [edge_shape(HARM * TENSORS, atoms)],
        in_specs=[WHOLE] * 6
        + [edge_spec(r, width) for r in (LATENT, LATENT, TENSORS)]
        + [WHOLE] * 3,
        out_specs=[edge_spec(r, width) for r in rows] + [WHOLE],
        scratch_shapes=[pltpu.VMEM((2 * HARM * TENSORS, 4 * atoms), BF16)],
        compiler_params=params(),
        name="middle_pass",
    )(geo, nbrs, *blocks, x, lx, val, s_w, mix_w, cols)


def pull_mixed(geo, step, group, g, value, ds, chosen, dgeo, d_own, d_wide, dg, atoms):
    columns = []
    for q in range(group):
        k = step * group + q
        span = slice(q * atoms, (q + 1) * atoms)
        part = value[:, span]
        pulled = [ds[d * TENSORS : (d + 1) * TENSORS, span] for d in range(3)]
        scaled = [p * part for p in pulled]
        total = None
        for m in range(HARM):
            rows = slice(m * TENSORS, (m + 1) * TENSORS)
            d = DEGREE[m]
            source = g[rows, span]
            if m == 0:
                total = source * pulled[0]
                grad = scaled[0]
            else:
                harm = geo[m, pl.ds(k, 1), :]
                total = total + source * pulled[d] * harm
                dgeo[m, pl.ds(k, 1), :] += jnp.sum(source * scaled[d], axis=0, keepdims=True)
                grad = scaled[d] * harm
            d_own[rows, :] += grad
            high, low = halves(grad)
            dg[rows, span] = high
            dg[slice(HARM * TENSORS + m * TENSORS, HARM * TENSORS + (m + 1) * TENSORS), span] = low
        columns.append(total)
    both = dot_nt(dg[...], chosen)
    rows = HARM * TENSORS
    for number, out in enumerate(d_wide):
        span = slice(number * atoms, (number + 1) * atoms)
        out[...] += both[:rows, span] + both[rows:, span]
    return jnp.concatenate(columns, 1)


def last_kernel(
    geo, nbrs, own, below, above, across, x, lx, val, s_w, back_w, cols, base,
    energy, dx_out, dval_out, dgeo, d_own, d_below, d_above, d_across, split, g, dg, *, group,
):
    step = pl.program_id(0)
    atoms = own.shape[1]
    norm = 1.0 / math.sqrt(geo.shape[1])

    @pl.when(step == 0)
    def _():
        fill_split(own, below, above, across, split)
        energy[...] = base[...]
        dgeo[...] = jnp.zeros_like(dgeo)
        for out in (d_own, d_below, d_above, d_across):
            out[...] = jnp.zeros_like(out)

    chosen = chosen_columns(nbrs, step, group, split.shape[1])
    gathered(split, chosen, own, g, group)
    value = val[...]
    _, s = contracted(geo, step, group, g, value, atoms)
    update, slope = silu_pair(lx[...] + product(s_w[1], s))
    fresh = x[...] + update
    weight = cols[:, 2:3]
    read = jnp.sum(fresh * weight, axis=0, keepdims=True) * norm
    cuts = []
    for q in range(group):
        k = step * group + q
        span = slice(q * atoms, (q + 1) * atoms)
        cut = geo[0, pl.ds(k, 1), :]
        cuts.append(cut)
        energy[...] += read[:, span] * cut
        dgeo[0, pl.ds(k, 1), :] = read[:, span]
    d_fresh = weight * (jnp.concatenate(cuts, 1) * norm)
    pulled = product(back_w[1], d_fresh * slope)
    dx_out[...] = d_fresh + pulled[:LATENT]
    dval_out[...] = pull_mixed(
        geo, step, group, g, value, pulled[LATENT:], chosen, dgeo, d_own,
        (d_own, d_below, d_above, d_across), dg, atoms,
    )


def last_pass(geo, nbrs, blocks, x, lx, val, s_w, back_w, cols, base, group):
    _, slots, atoms = geo.shape
    width = group * atoms
    edges = slots * atoms
    rows = HARM * TENSORS
    return pl.pallas_call(
        partial(last_kernel, group=group),
        grid=(slots // group,),
        out_shape=[
            jax.ShapeDtypeStruct((1, atoms), F32),
            edge_shape(LATENT, edges),
            edge_shape(TENSORS, edges),
            jax.ShapeDtypeStruct((HARM, slots, atoms), F32),
        ]
        + [edge_shape(rows, atoms)] * 4,
        in_specs=[WHOLE] * 6
        + [edge_spec(r, width) for r in (LATENT, LATENT, TENSORS)]
        + [WHOLE] * 4,
        out_specs=[WHOLE, edge_spec(LATENT, width), edge_spec(TENSORS, width)] + [WHOLE] * 5,
        scratch_shapes=[
            pltpu.VMEM((2 * rows, 4 * atoms), BF16),
            pltpu.VMEM((rows, width), F32),
            pltpu.VMEM((2 * rows, width), BF16),
        ],
        compiler_params=params(),
        name="last_pass",
    )(geo, nbrs, *blocks, x, lx, val, s_w, back_w, cols, base)


def pull_env(geo, step, group, total, emb, dgeo, atoms, norm):
    columns = []
    for q in range(group):
        k = step * group + q
        span = slice(q * atoms, (q + 1) * atoms)
        part = emb[:, span]
        cut = geo[0, pl.ds(k, 1), :] * norm
        grad = None
        for m in range(HARM):
            source = total[m * TENSORS : (m + 1) * TENSORS, :]
            if m == 0:
                grad = source
            else:
                grad = grad + source * geo[m, pl.ds(k, 1), :]
                dgeo[m, pl.ds(k, 1), :] += cut * jnp.sum(source * part, axis=0, keepdims=True)
        dgeo[0, pl.ds(k, 1), :] += norm * jnp.sum(grad * part, axis=0, keepdims=True)
        columns.append(grad * cut)
    return jnp.concatenate(columns, 1)


def middle_back_kernel(
    geo, nbrs, own, low, high, dgeo_in, dx, dval, emb, g, slope, val, ev_w, back_w,
    dx_out, dval_out, dgeo, d_own, d_below, d_above, d_across, total, dg, *, group,
):
    step = pl.program_id(0)
    atoms = own.shape[1]
    norm = 1.0 / math.sqrt(geo.shape[1])

    @pl.when(step == 0)
    def _():
        total[...] = own[...] + low[...] + high[...]
        dgeo[...] = dgeo_in[...]
        for out in (d_own, d_below, d_above, d_across):
            out[...] = jnp.zeros_like(out)

    chosen = chosen_columns(nbrs, step, group, 4 * atoms)
    demb = pull_env(geo, step, group, total, emb, dgeo, atoms, norm)
    d_fresh = dx[...] + product(ev_w[1], jnp.concatenate([demb, dval[...]], 0))
    pulled = product(back_w[0], d_fresh * slope[...])
    dx_out[...] = d_fresh + pulled[:LATENT]
    dval_out[...] = pull_mixed(
        geo, step, group, g, val[...], pulled[LATENT:], chosen, dgeo, d_own,
        (d_own, d_below, d_above, d_across), dg, atoms,
    )


def middle_back(geo, nbrs, grads, dgeo, dx, dval, emb, g, slope, val, ev_w, back_w, group):
    _, slots, atoms = geo.shape
    width = group * atoms
    edges = slots * atoms
    rows = HARM * TENSORS
    return pl.pallas_call(
        partial(middle_back_kernel, group=group),
        grid=(slots // group,),
        out_shape=[
            edge_shape(LATENT, edges),
            edge_shape(TENSORS, edges),
            jax.ShapeDtypeStruct((HARM, slots, atoms), F32),
        ]
        + [edge_shape(rows, atoms)] * 4,
        in_specs=[WHOLE] * 6
        + [edge_spec(r, width) for r in (LATENT, TENSORS, TENSORS, rows, LATENT, TENSORS)]
        + [WHOLE] * 2,
        out_specs=[edge_spec(LATENT, width), edge_spec(TENSORS, width)] + [WHOLE] * 5,
        scratch_shapes=[pltpu.VMEM((rows, atoms), F32), pltpu.VMEM((2 * rows, width), BF16)],
        compiler_params=params(),
        name="middle_back",
    )(geo, nbrs, *grads, dgeo, dx, dval, emb, g, slope, val, ev_w, back_w)


def first_back_kernel(
    geo, own, low, high, dgeo_in, dx, dval, emb, slope, ev_w, rad_w, dgeo, total, *, group
):
    step = pl.program_id(0)
    atoms = own.shape[1]
    norm = 1.0 / math.sqrt(geo.shape[1])

    @pl.when(step == 0)
    def _():
        total[...] = own[...] + low[...] + high[...]
        dgeo[0:HARM] = dgeo_in[...]

    demb = pull_env(geo, step, group, total, emb, dgeo, atoms, norm)
    d_fresh = dx[...] + product(ev_w[0], jnp.concatenate([demb, dval[...]], 0))
    radial = product(rad_w[...], d_fresh * slope[...])
    for q in range(group):
        k = step * group + q
        for n in range(BASIS):
            dgeo[HARM + n, pl.ds(k, 1), :] = radial[n : n + 1, q * atoms : (q + 1) * atoms]


def first_back(geo, grads, dgeo, dx, dval, emb, slope, ev_w, rad_w, group):
    _, slots, atoms = geo.shape
    width = group * atoms
    return pl.pallas_call(
        partial(first_back_kernel, group=group),
        grid=(slots // group,),
        out_shape=jax.ShapeDtypeStruct((HARM + BASIS, slots, atoms), F32),
        in_specs=[WHOLE] * 5
        + [edge_spec(r, width) for r in (LATENT, TENSORS, TENSORS, LATENT)]
        + [WHOLE] * 2,
        out_specs=WHOLE,
        scratch_shapes=[pltpu.VMEM((HARM * TENSORS, atoms), F32)],
        compiler_params=params(),
        name="first_back",
    )(geo, *grads, dgeo, dx, dval, emb, slope, ev_w, rad_w)


def geometry_back_kernel(vec, dgeo, nbrs, own_out, below_out, above_out, across_out, dvec):
    _, slots, atoms = vec.shape
    for group in range(slots // 8):
        for tile in range(atoms // 128):
            up = slice(group * 8, group * 8 + 8)
            span = slice(tile * 128, tile * 128 + 128)
            vx, vy, vz = (vec[axis, up, span] for axis in range(3))
            inverse, cut, slope, sine, cosine = distances(vx, vy, vz)
            ux, uy, uz = vx * inverse, vy * inverse, vz * inverse
            _, h1, h2, h3, h4, h5, h6, h7, h8 = (dgeo[m, up, span] for m in range(HARM))
            dux = h1 + ROOT3 * (uy * h4 + uz * h7 + ux * h8)
            duy = h2 + ROOT3 * (ux * h4 + uz * h5 - uy * h8)
            duz = h3 + ROOT3 * (uy * h5 + ux * h7) + 3.0 * uz * h6
            along = ux * dux + uy * duy + uz * duz
            scale = math.sqrt(2.0 / CUTOFF) * inverse
            by_wave = jnp.zeros_like(sine)
            by_angle = jnp.zeros_like(sine)
            before, now = jnp.zeros_like(sine), sine
            before_c, now_c = jnp.ones_like(sine), cosine
            for n in range(BASIS):
                pulled = dgeo[HARM + n, up, span]
                by_wave = by_wave + pulled * now
                by_angle = by_angle + (n + 1.0) * (pulled * now_c)
                before, now = now, 2.0 * cosine * now - before
                before_c, now_c = now_c, 2.0 * cosine * now_c - before_c
            d_dist = slope * dgeo[0, up, span] + scale * (
                (math.pi / CUTOFF) * by_angle * cut + by_wave * (slope - inverse * cut)
            )
            dvec[0, up, span] = (dux - ux * along) * inverse + ux * d_dist
            dvec[1, up, span] = (duy - uy * along) * inverse + uy * d_dist
            dvec[2, up, span] = (duz - uz * along) * inverse + uz * d_dist
    blocks = 4 * atoms // 128
    total = jnp.zeros((2 * 48, 128), F32)
    for k in range(slots):
        index = nbrs[k : k + 1, :]
        block = lax.shift_right_arithmetic(index, 7)
        rows = lax.broadcasted_iota(jnp.int32, (16, atoms), 0)
        here = rows == block
        spread = jnp.concatenate(
            [jnp.where(here, dvec[axis, k : k + 1, :], 0.0) for axis in range(3)], 0
        )
        lane = lax.broadcasted_iota(jnp.int32, (128, atoms), 0)
        chosen = (lane == (index & 127)).astype(F32).astype(BF16)
        total = total + dot_nt(stacked(spread), chosen)
    total = total[:48] + total[48:]
    outs = (own_out, below_out, above_out, across_out)
    for out in outs:
        out[...] = jnp.zeros_like(out)
    per = atoms // 128
    for axis in range(3):
        for block in range(blocks):
            row = axis * 16 + block
            span = slice(block % per * 128, block % per * 128 + 128)
            outs[block // per][axis : axis + 1, span] = total[row : row + 1]
        own_out[axis : axis + 1, :] -= jnp.sum(dvec[axis], axis=0, keepdims=True)


def geometry_back(vec, dgeo, nbrs):
    _, slots, atoms = vec.shape
    return pl.pallas_call(
        geometry_back_kernel,
        out_shape=[jax.ShapeDtypeStruct((8, atoms), F32)] * 4,
        in_specs=[WHOLE] * 3,
        out_specs=[WHOLE] * 4,
        scratch_shapes=[pltpu.VMEM((3, slots, atoms), F32)],
        compiler_params=params(),
        name="geometry_back",
    )(vec, dgeo, nbrs)


def swap_y(rows, face):
    if lax.axis_size("gy") == 2:
        return passed_along(rows, "gy", 1)
    up = passed_along(rows[:, :face], "gy", 1)
    down = passed_along(rows[:, face:], "gy", -1)
    return jnp.concatenate([up, down], 1)


def return_y(rows, face):
    if lax.axis_size("gy") == 2:
        return passed_along(rows, "gy", 1)
    up = passed_along(rows[:, :face], "gy", -1)
    down = passed_along(rows[:, face:], "gy", 1)
    return jnp.concatenate([up, down], 1)


def ghost_env(env, wanted, face):
    below = passed_along(env, "gx", 1)
    above = passed_along(env, "gx", -1)
    across = swap_y(lend_env(env, below, above, wanted), face)
    return env, below, above, across


def owned_grads(own, below, above, across, wanted, face):
    returned = return_y(across, face)
    own, below, above = take_back(returned, wanted, own, below, above)
    return own, passed_along(below, "gx", -1), passed_along(above, "gx", 1)


def per_device(
    positions,
    species,
    neighbours,
    send_x,
    send_y,
    two_weight,
    two_bias,
    env_weight,
    value_weight,
    latent_weight,
    latent_bias,
    out_weight,
    species_shift,
):
    group = 4
    nbrs = neighbours[0, 0]
    atoms = nbrs.shape[1]
    face = send_y.shape[3]
    rows = jnp.concatenate(
        [
            positions[0, 0],
            species[0, 0][None].astype(F32),
            send_x[0, 0].astype(F32),
            jnp.zeros((2, atoms), F32),
        ],
        0,
    )
    wanted = jnp.concatenate(
        [
            send_y[0, 0, 1],
            send_y[0, 0, 0],
            jnp.full((atoms - 2 * face,), -1, jnp.int32),
        ]
    )[None]
    below = passed_along(rows, "gx", 1)
    above = passed_along(rows, "gx", -1)
    two_w, mix_w, s_w, back_w, ev_w, rad_w, cols = prepare_weights(
        two_weight, two_bias, env_weight, value_weight, latent_weight, latent_bias, out_weight
    )
    lent, wanted = lend_rows(rows, below, above, wanted)
    across = swap_y(lent, face)
    vec, geo, nbrs, base = geometry(rows, below, above, across, nbrs, species_shift, face)
    x0, slope_a, emb0, val0, lx0, env0 = first_pass(geo, rows, two_w, mix_w, cols, group)
    blocks = ghost_env(env0, wanted, face)
    g0, slope0, x1, emb1, val1, lx1, env1 = middle_pass(
        geo, nbrs, blocks, x0, lx0, val0, s_w, mix_w, cols, group
    )
    blocks = ghost_env(env1, wanted, face)
    energy, dx, dval, dgeo, *grads = last_pass(
        geo, nbrs, blocks, x1, lx1, val1, s_w, back_w, cols, base, group
    )
    total = lax.psum(jnp.sum(energy), ("gx", "gy"))
    mean_energy = total / (atoms * lax.axis_size("gx") * lax.axis_size("gy"))
    grads = owned_grads(*grads, wanted, face)
    dx, dval, dgeo, *grads = middle_back(
        geo, nbrs, grads, dgeo, dx, dval, emb1, g0, slope0, val0, ev_w, back_w, group
    )
    grads = owned_grads(*grads, wanted, face)
    dgeo = first_back(geo, grads, dgeo, dx, dval, emb0, slope_a, ev_w, rad_w, group)
    grads = owned_grads(*geometry_back(vec, dgeo, nbrs), wanted, face)
    forces = -(grads[0] + grads[1] + grads[2])[:3]
    return (energy[None], forces[None, None], mean_energy.reshape(1))


def solution(mesh):
    placed = (
        P(("groups", "gx"), "gy", None, None),
        P(("groups", "gx"), "gy", None),
        P(("groups", "gx"), "gy", None, None),
        P(("groups", "gx"), "gy", None, None),
        P(("groups", "gx"), "gy", None, None),
        P(),
        P(),
        P(),
        P(),
        P(),
        P(),
        P(),
        P(),
    )
    return jax.shard_map(
        per_device,
        mesh=mesh,
        in_specs=placed,
        out_specs=(
            P(("groups", "gx"), "gy", None),
            P(("groups", "gx"), "gy", None, None),
            P("groups"),
        ),
        check_vma=False,
    )
```

time: 1160 us -> 349 us (0.30); the launches traced: 1150 us -> 349 us
  local copies, waits for them, and re-layouts: 460 us -> 14.9 us
  other arithmetic: 438 us -> 2.84 us
  Pallas kernels: 0 us -> 185 us
  matrix products: 130 us -> 0 us
  waiting for transfers between devices: 46 us -> 94.1 us
  starting transfers between devices: 33.5 us -> 16.5 us
    scatter-add x15 -> x0, other arithmetic: 258 us -> none  [the longest x2 151 us: advance(): env_other = jnp.take(ext_env, nbrs.reshape(-1), axis=1)]
    gather x19 -> x0, local copies, waits for them, and re-layouts: 234 us -> none  [the longest x2 95.7 us: advance(): env_other = jnp.take(ext_env, nbrs.reshape(-1), axis=1)]
    pallas_call x0 -> x14, Pallas kernels: none -> 185 us  [the longest x1 61.7 us: last_pass(): pl.pallas_call(partial(last_kernel, group=group), grid=(slots // group,),...]
    dot_general x16 -> x0, matrix products: 130 us -> none  [the longest x4 52.6 us: advance(): jnp.dot(latent_w.T, joined, precision=lax.Precision.HIGHEST)]
    reduce_sum x19 -> x1, other arithmetic: 75.8 us -> 0.6 us  [per_device(): total = lax.psum(jnp.sum(energy), ('gx', 'gy'))]
    reshape x5 -> x0, local copies, waits for them, and re-layouts: 63.9 us -> none  [the longest x2 33.6 us: advance(): (env_centre + env_other).reshape(9, width, -1) * sph[:, None, :]]
    unnamed x165 -> x40, local copies, waits for them, and re-layouts: 61.8 us -> 13.5 us
    ppermute x24 -> x18, waiting for transfers between devices: 46 us -> 94.1 us  [passed_along(): lax.ppermute(value, axis, [(i, (i + by) % count) for i in range(count)])]
  transfers between devices with their start and end apart: 24 -> 18, of which waited for: 10 -> 10; matrix products, arithmetic and copies ran while one was open for 7% -> 1% of each run, Pallas kernels for 0% -> 1%
where the time goes in v1:
time: 349 us
  Pallas kernels  185 us (53%)
  waiting for transfers between devices  94.1 us (27%)
  blocking collectives  32.4 us (9%)
  starting transfers between devices  16.5 us (5%)
  local copies, waits for them, and re-layouts  14.9 us (4%)
    ppermute x18, waiting for transfers between devices, passed_along(): lax.ppermute(value, axis, [(i, (i + by) % count) for i in range(count)])  94.1 us
    pallas_call x1, Pallas kernels, last_pass(): pl.pallas_call(partial(last_kernel, group=group), grid=(slots // group,),...  61.7 us
    pallas_call x1, Pallas kernels, middle_back(): pl.pallas_call(partial(middle_back_kernel, group=group), grid=(slots // g...  38.7 us
    pallas_call x1, Pallas kernels, middle_pass(): pl.pallas_call(partial(middle_kernel, group=group), grid=(slots // group,...  34.9 us
    psum x1, blocking collectives, per_device(): total = lax.psum(jnp.sum(energy), ('gx', 'gy'))  32.4 us
    ppermute x18, starting transfers between devices, passed_along(): lax.ppermute(value, axis, [(i, (i + by) % count) for i in range(count)])  16.5 us
    unnamed x40, local copies, waits for them, and re-layouts  13.5 us
    pallas_call x1, Pallas kernels, first_back(): pl.pallas_call(partial(first_back_kernel, group=group), grid=(slots // gr...  12.5 us
  transfers between devices with their start and end apart: 18, of which 10 were waited for; matrix products, arithmetic and copies ran while one was open for 1% of the time, Pallas kernels for 1%

profile of v1, /device:TPU:0, one launch (start us, length us, event | category | flops | bytes accessed | tf_op | source)
XLA Modules:
  0.0 348.5 jit_solution(17365598037074475164)
XLA Ops:
  2.8 6.0 %collective-permute-start.1 = (f32[8,384]{1,0:T(8,128)S(1)}, f32[8,384]{1,0:T(8,128)S(1)}, u32[]{:S(2)}, u32[]{:S(2)}) collective-permute-start(f32[8,384]{1,0:T(8,128)S(1)} %maximum_maximum_fusion.own), channel_id=1, source_target_pairs={{0,14},{2,0},{4,2},{6,4},{8,6},{10,8},{12,10},{14,12},{1,15},{3,1}... | collective-permute-start | bytes 36872 | tf_op jit(solution)/shard_map/ppermute | solution.py:33
  10.2 5.0 %collective-permute-done.below = f32[8,384]{1,0:T(8,128)S(1)} collective-permute-done((f32[8,384]{1,0:T(8,128)S(1)}, f32[8,384]{1,0:T(8,128)S(1)}, u32[]{:S(2)}, u32[]{:S(2)}) %collective-permute-start) | collective-permute-done | bytes 12320 | tf_op jit(solution)/shard_map/ppermute | solution.py:33
  15.8 1.6 lend_rows.1
  17.4 1.5 copy.16.env
  18.9 1.5 copy.17.val
  20.4 2.4 prepare_weights.1
  23.4 3.5 %geometry.1 = (f32[3,32,384]{2,1,0:T(8,128)}, f32[18,32,384]{2,1,0:T(8,128)}, s32[32,384]{1,0:T(8,128)}, f32[1,384]{1,0:T(1,128)}) custom-call(f32[8,384]{1,0:T(8,128)} %copy-done.12, f32[8,384]{1,0:T(8,128)} %copy-done.14, f32[8,384]{1,0:T(8,128)} %copy-done.13, f32[8,384]{1,0:T(8,128)} %copy-done.15, s32[32,384]{1,0:T(8,128)} %bitcast.16, f32[5]{0:T(128)} %shift.1), custom_call_target="tpu_custom_call" | custom-call | tf_op jit(solution)/shard_map/geometry/pallas_call | solution.py:266
  27.0 12.0 %first_pass.1 = (f32[128,12288]{1,0:T(8,128)}, f32[128,12288]{1,0:T(8,128)}, f32[32,12288]{1,0:T(8,128)}, f32[32,12288]{1,0:T(8,128)}, f32[128,12288]{1,0:T(8,128)}, /*index=5*/f32[288,384]{1,0:T(8,128)}) custom-call(f32[18,32,384]{2,1,0:T(8,128)} %get-tuple-element.58.geo, f32[8,384]{1,0:T(8,128)} %copy-done.12, bf16[256,48]{1,0:T(8,128)(2,1)} %get-tuple-element.60.two_w, ...), custom_call_target="tpu_custom_call" | custom-call | tf_op jit(solution)/shard_map/first_pass/pallas_call | solution.py:344
  39.6 1.4 collective-permute-start.3
  41.1 20.2 %collective-permute-done.4.above = f32[288,384]{1,0:T(8,128)S(1)} collective-permute-done((f32[288,384]{1,0:T(8,128)}, f32[288,384]{1,0:T(8,128)S(1)}, u32[]{:S(2)}, u32[]{:S(2)}) %collective-permute-start.4) | collective-permute-done | bytes 442400 | tf_op jit(solution)/shard_map/ppermute | solution.py:33
  62.2 3.0 lend_env.2
  65.3 2.0 collective-permute-done.5.across
  68.0 34.9 %middle_pass.1 = (f32[288,12288]{1,0:T(8,128)}, f32[128,12288]{1,0:T(8,128)}, f32[128,12288]{1,0:T(8,128)}, f32[32,12288]{1,0:T(8,128)}, f32[32,12288]{1,0:T(8,1...) custom-call(f32[18,32,384]{2,1,0:T(8,128)} %get-tuple-element.58.geo, s32[32,384]{1,0:T(8,128)} %get-tuple-element.59.nbrs, ...), custom_call_target="tpu_custom_call" | custom-call | tf_op jit(solution)/shard_map/middle_pass/pallas_call | solution.py:474
  103.5 1.5 collective-permute-start.6
  105.0 19.9 %collective-permute-done.7.above = f32[288,384]{1,0:T(8,128)S(1)} collective-permute-done((f32[288,384]{1,0:T(8,128)}, f32[288,384]{1,0:T(8,128)S(1)}, u32[]{:S(2)}, u32[]{:S(2)}) %collective-permute-start.7) | collective-permute-done | bytes 442400 | tf_op jit(solution)/shard_map/ppermute | solution.py:33
  126.4 3.0 lend_env.3
  129.5 2.0 collective-permute-done.8.across
  132.2 61.7 %last_pass.1 = (f32[1,384]{1,0:T(1,128)}, f32[128,12288]{1,0:T(8,128)}, f32[32,12288]{1,0:T(8,128)}, f32[9,32,384]{2,1,0:T(8,128)}, f32[288,384]{1,0:T(8,128)}, ...) custom-call(f32[18,32,384]{2,1,0:T(8,128)} %get-tuple-element.58.geo, ...), custom_call_target="tpu_custom_call" | custom-call | tf_op jit(solution)/shard_map/last_pass/pallas_call | solution.py:568
  194.1 1.9 collective-permute-done.9.returned
  196.8 3.2 take_back.3
  199.9 2.0 collective-permute-start.11
  202.0 19.9 %collective-permute-done.10.low = f32[288,384]{1,0:T(8,128)S(1)} collective-permute-done((f32[288,384]{1,0:T(8,128)}, f32[288,384]{1,0:T(8,128)S(1)}, u32[]{:S(2)}, u32[]{:S(2)}) %collective-permute-start.10) | collective-permute-done | bytes 442400 | tf_op jit(solution)/shard_map/ppermute | solution.py:33
  222.8 38.7 %middle_back.1 = (f32[128,12288]{1,0:T(8,128)}, f32[32,12288]{1,0:T(8,128)}, f32[9,32,384]{2,1,0:T(8,128)}, f32[288,384]{1,0:T(8,128)}, f32[288,384]{1,0:T(8,128...) custom-call(f32[18,32,384]{2,1,0:T(8,128)} %get-tuple-element.58.geo, s32[32,384]{1,0:T(8,128)} %get-tuple-element.59.nbrs, ...), custom_call_target="tpu_custom_call" | custom-call | tf_op jit(solution)/shard_map/middle_back/pallas_call | solution.py:643
  261.5 2.0 collective-permute-done.12.returned
  264.3 3.2 take_back.4
  267.9 1.6 collective-permute-start.14
  269.5 19.9 %collective-permute-done.13.low = f32[288,384]{1,0:T(8,128)S(1)} collective-permute-done((f32[288,384]{1,0:T(8,128)}, f32[288,384]{1,0:T(8,128)S(1)}, u32[]{:S(2)}, u32[]{:S(2)}) %collective-permute-start.13) | collective-permute-done | bytes 442400 | tf_op jit(solution)/shard_map/ppermute | solution.py:33
  290.3 12.5 %first_back.1.dgeo = f32[17,32,384]{2,1,0:T(8,128)} custom-call(f32[18,32,384]{2,1,0:T(8,128)} %get-tuple-element.58.geo, f32[288,384]{1,0:T(8,128)} %get-tuple-element.95.own, f32[288,384]{1,0:T(8,128)} %copy-done.4, f32[288,384]{1,0:T(8,128)} %copy-done.5, f32[9,32,384]{2,1,0:T(8,128)} %get-tuple-element.98.dgeo_in, f32[128,12288]{1,0:T(8,128)} %get-tuple-element.99.dx, ...), custom_call_target="tpu_custom_call" | custom-call | tf_op jit(solution)/shard_map/first_back/pallas_call | solution.py:686
  302.8 3.7 %geometry_back.1 = (f32[8,384]{1,0:T(8,128)}, f32[8,384]{1,0:T(8,128)}, f32[8,384]{1,0:T(8,128)}, f32[8,384]{1,0:T(8,128)}) custom-call(f32[3,32,384]{2,1,0:T(8,128)} %get-tuple-element.76.vec, f32[17,32,384]{2,1,0:T(8,128)} %first_back.1.dgeo, s32[32,384]{1,0:T(8,128)} %get-tuple-element.59.nbrs), custom_call_target="tpu_custom_call" | custom-call | tf_op jit(solution)/shard_map/geometry_back/pallas_call | solution.py:759
  308.6 1.8 take_back.5
  310.8 1.6 collective-permute-start.17
  313.0 32.4 %psum.7 = f32[]{:T(128)} all-reduce(f32[]{:T(128)} %reduce_sum.9), channel_id=1, replica_groups=mesh['groups'=2,'gx'=8,'gy'=2] {'gx','gy'}, use_global_device_ids=true, to_apply=%region_1.0 | all-reduce | flops 1 | bytes 8 | tf_op jit(solution)/shard_map/psum | solution.py:851
  (70 shorter events, 18.5 us)
Async XLA Ops:
  2.8 12.4 %copy-start.12 = (f32[8,384]{1,0:T(8,128)}, f32[8,384]{1,0:T(8,128)S(1)}, u32[]{:S(2)}) copy-start(f32[8,384]{1,0:T(8,128)S(1)} %maximum_maximum_fusion.own) | copy-start | bytes 36868
  2.8 7.4 %collective-permute-start.1 = (f32[8,384]{1,0:T(8,128)S(1)}, f32[8,384]{1,0:T(8,128)S(1)}, u32[]{:S(2)}, u32[]{:S(2)}) collective-permute-start(f32[8,384]{1,0:T(8,128)S(1)} %maximum_maximum_fusion.own), channel_id=1, source_target_pairs={{0,14},{2,0},{4,2},{6,4},{8,6},{10,8},{12,10},{14,12},{1,15},{3,1}... | collective-permute-start | bytes 36872 | tf_op jit(solution)/shard_map/ppermute | solution.py:33
  8.8 6.4 %collective-permute-start = (f32[8,384]{1,0:T(8,128)S(1)}, f32[8,384]{1,0:T(8,128)S(1)}, u32[]{:S(2)}, u32[]{:S(2)}) collective-permute-start(f32[8,384]{1,0:T(8,128)S(1)} %maximum_maximum_fusion.own), channel_id=1, source_target_pairs={{0,2},{2,4},{4,6},{6,8},{8,10},{10,12},{12,14},{14,0},{1,3},{3,5},... | collective-permute-start | bytes 36872 | tf_op jit(solution)/shard_map/ppermute | solution.py:33
  10.2 5.0 %copy-start.13 = (f32[8,384]{1,0:T(8,128)}, f32[8,384]{1,0:T(8,128)S(1)}, u32[]{:S(2)}) copy-start(f32[8,384]{1,0:T(8,128)S(1)} %collective-permute-done.1.above) | copy-start | bytes 36868
  17.4 5.4 %collective-permute-start.2 = (f32[8,384]{1,0:T(8,128)}, f32[8,384]{1,0:T(8,128)S(1)}, u32[]{:S(2)}, u32[]{:S(2)}) collective-permute-start(f32[8,384]{1,0:T(8,128)} %get-tuple-element.57), channel_id=1, source_target_pairs={{0,1},{1,0},{2,3},{3,2},{4,5},{5,4},{6,7},{7,6},{8,9},{9,8},{10,11... | collective-permute-start | bytes 36872 | tf_op jit(solution)/shard_map/ppermute | solution.py:33
  39.0 22.3 %collective-permute-start.4 = (f32[288,384]{1,0:T(8,128)}, f32[288,384]{1,0:T(8,128)S(1)}, u32[]{:S(2)}, u32[]{:S(2)}) collective-permute-start(f32[288,384]{1,0:T(8,128)} %get-tuple-element.63.own), channel_id=1, source_target_pairs={{0,14},{2,0},{4,2},{6,4},{8,6},{10,8},{12,10},{14,12},{1,15},{3,1}... | collective-permute-start | bytes 1327112 | tf_op jit(solution)/shard_map/ppermute | solution.py:33
  39.6 21.7 %collective-permute-start.3 = (f32[288,384]{1,0:T(8,128)}, f32[288,384]{1,0:T(8,128)S(1)}, u32[]{:S(2)}, u32[]{:S(2)}) collective-permute-start(f32[288,384]{1,0:T(8,128)} %get-tuple-element.63.own), channel_id=1, source_target_pairs={{0,2},{2,4},{4,6},{6,8},{8,10},{10,12},{12,14},{14,0},{1,3},{3,5},... | collective-permute-start | bytes 1327112 | tf_op jit(solution)/shard_map/ppermute | solution.py:33
  61.3 0.8 copy-start
  61.3 0.9 copy-start.1
  65.3 2.0 collective-permute-start.5
  102.9 22.0 %collective-permute-start.7 = (f32[288,384]{1,0:T(8,128)}, f32[288,384]{1,0:T(8,128)S(1)}, u32[]{:S(2)}, u32[]{:S(2)}) collective-permute-start(f32[288,384]{1,0:T(8,128)} %get-tuple-element.69.own), channel_id=1, source_target_pairs={{0,14},{2,0},{4,2},{6,4},{8,6},{10,8},{12,10},{14,12},{1,15},{3,1}... | collective-permute-start | bytes 1327112 | tf_op jit(solution)/shard_map/ppermute | solution.py:33
  103.5 21.4 %collective-permute-start.6 = (f32[288,384]{1,0:T(8,128)}, f32[288,384]{1,0:T(8,128)S(1)}, u32[]{:S(2)}, u32[]{:S(2)}) collective-permute-start(f32[288,384]{1,0:T(8,128)} %get-tuple-element.69.own), channel_id=1, source_target_pairs={{0,2},{2,4},{4,6},{6,8},{8,10},{10,12},{12,14},{14,0},{1,3},{3,5},... | collective-permute-start | bytes 1327112 | tf_op jit(solution)/shard_map/ppermute | solution.py:33
  124.9 0.8 copy-start.2
  125.7 0.8 copy-start.3
  129.5 2.0 collective-permute-start.8
  131.5 0.8 copy-start.9
  193.9 2.1 collective-permute-start.9
  196.0 0.8 copy-start.7
  199.9 21.9 %collective-permute-start.10 = (f32[288,384]{1,0:T(8,128)}, f32[288,384]{1,0:T(8,128)S(1)}, u32[]{:S(2)}, u32[]{:S(2)}) collective-permute-start(f32[288,384]{1,0:T(8,128)} %get-tuple-element.82), channel_id=1, source_target_pairs={{0,14},{2,0},{4,2},{6,4},{8,6},{10,8},{12,10},{14,12},{1,15},{3,1}... | collective-permute-start | bytes 1327112 | tf_op jit(solution)/shard_map/ppermute | solution.py:33
  199.9 21.9 %collective-permute-start.11 = (f32[288,384]{1,0:T(8,128)}, f32[288,384]{1,0:T(8,128)S(1)}, u32[]{:S(2)}, u32[]{:S(2)}) collective-permute-start(f32[288,384]{1,0:T(8,128)} %get-tuple-element.83), channel_id=1, source_target_pairs={{0,2},{2,4},{4,6},{6,8},{8,10},{10,12},{12,14},{14,0},{1,3},{3,5},... | collective-permute-start | bytes 1327112 | tf_op jit(solution)/shard_map/ppermute | solution.py:33
  221.9 0.8 copy-start.10
  221.9 0.9 copy-start.11
  261.5 2.1 collective-permute-start.12
  263.5 0.8 copy-start.8
  267.5 21.9 %collective-permute-start.13 = (f32[288,384]{1,0:T(8,128)}, f32[288,384]{1,0:T(8,128)S(1)}, u32[]{:S(2)}, u32[]{:S(2)}) collective-permute-start(f32[288,384]{1,0:T(8,128)} %get-tuple-element.96), channel_id=1, source_target_pairs={{0,14},{2,0},{4,2},{6,4},{8,6},{10,8},{12,10},{14,12},{1,15},{3,1}... | collective-permute-start | bytes 1327112 | tf_op jit(solution)/shard_map/ppermute | solution.py:33
  267.9 21.5 %collective-permute-start.14 = (f32[288,384]{1,0:T(8,128)}, f32[288,384]{1,0:T(8,128)S(1)}, u32[]{:S(2)}, u32[]{:S(2)}) collective-permute-start(f32[288,384]{1,0:T(8,128)} %get-tuple-element.97), channel_id=1, source_target_pairs={{0,2},{2,4},{4,6},{6,8},{8,10},{10,12},{12,14},{14,0},{1,3},{3,5},... | collective-permute-start | bytes 1327112 | tf_op jit(solution)/shard_map/ppermute | solution.py:33
  289.4 0.8 copy-start.4
  289.4 0.9 copy-start.5
  290.3 22.0 %copy-start.17 = (f32[1,384]{1,0:T(1,128)S(1)}, f32[1,384]{1,0:T(1,128)}, u32[]{:S(2)}) copy-start(f32[1,384]{1,0:T(1,128)} %get-tuple-element.75) | copy-start | bytes 4612
  306.6 1.4 collective-permute-start.15
  310.3 35.7 %collective-permute-start.16 = (f32[8,384]{1,0:T(8,128)}, f32[8,384]{1,0:T(8,128)S(1)}, u32[]{:S(2)}, u32[]{:S(2)}) collective-permute-start(f32[8,384]{1,0:T(8,128)} %get-tuple-element.109), channel_id=1, source_target_pairs={{0,14},{2,0},{4,2},{6,4},{8,6},{10,8},{12,10},{14,12},{1,15},{3,1}... | collective-permute-start | bytes 36872 | tf_op jit(solution)/shard_map/ppermute | solution.py:33
  310.8 35.3 %collective-permute-start.17 = (f32[8,384]{1,0:T(8,128)}, f32[8,384]{1,0:T(8,128)S(1)}, u32[]{:S(2)}, u32[]{:S(2)}) collective-permute-start(f32[8,384]{1,0:T(8,128)} %get-tuple-element.110), channel_id=1, source_target_pairs={{0,2},{2,4},{4,6},{6,8},{8,10},{10,12},{12,14},{14,0},{1,3},{3,5},... | collective-permute-start | bytes 36872 | tf_op jit(solution)/shard_map/ppermute | solution.py:33
  (4 other events, 2.6 us)

commit v2 on v1

--- a/solution.py
+++ b/solution.py
@@ -396,32 +396,64 @@
     )(returned, wanted, below, above, own)
 
 
-def chosen_columns(nbrs, step, group, columns):
+def chosen_columns(nbrs, step, group, start, columns):
     parts = []
     for q in range(group):
-        index = nbrs[pl.ds(step * group + q, 1), :]
+        index = nbrs[pl.ds(step * group + q, 1), :] - start
         rows = lax.broadcasted_iota(jnp.int32, (columns, index.shape[1]), 0)
         parts.append((rows == index).astype(F32).astype(BF16))
     return jnp.concatenate(parts, 1)
 
 
-def fill_split(own, below, above, across, split):
-    atoms = own.shape[1]
-    rows = own.shape[0]
-    for number, block in enumerate((own, below, above, across)):
+def fill_split(blocks, split):
+    rows, atoms = blocks[0].shape
+    for number, block in enumerate(blocks):
         span = slice(number * atoms, (number + 1) * atoms)
         high, low = halves(block[...])
         split[:rows, span] = high
         split[rows:, span] = low
 
 
-def gathered(split, chosen, own, g, group):
-    rows = HARM * TENSORS
-    atoms = own.shape[1]
-    both = dot(split[...], chosen)
+def gather_kernel(nbrs, block, before, out, split, *, group, place):
+    step = pl.program_id(0)
+    rows, atoms = block.shape
+
+    @pl.when(step == 0)
+    def _():
+        fill_split((block,), split)
+
+    both = dot(split[...], chosen_columns(nbrs, step, group, place * atoms, atoms))
     for q in range(group):
         span = slice(q * atoms, (q + 1) * atoms)
-        g[:, span] = both[:rows, span] + both[rows:, span] + own[...]
+        added = before[...] if place == 0 else before[:, span]
+        out[:, span] = both[:rows, span] + both[rows:, span] + added
+
+
+def gather_block(nbrs, block, before, place, group):
+    slots, atoms = nbrs.shape
+    rows = block.shape[0]
+    width = group * atoms
+    return pl.pallas_call(
+        partial(gather_kernel, group=group, place=place),
+        grid=(slots // group,),
+        out_shape=edge_shape(rows, slots * atoms),
+        in_specs=[WHOLE, WHOLE, WHOLE if place == 0 else edge_spec(rows, width)],
+        out_specs=edge_spec(rows, width),
+        scratch_shapes=[pltpu.VMEM((2 * rows, atoms), BF16)],
+        compiler_params=params(),
+        cost_estimate=effort(4 * rows * atoms * slots * atoms),
+        name="gather_block",
+    )(nbrs, block, before)
+
+
+def effort(flops):
+    return pl.CostEstimate(flops=flops, transcendentals=0, bytes_accessed=flops // 512)
+
+
+def add_rest(split, chosen, before, g):
+    rows = g.shape[0]
+    both = dot(split[...], chosen)
+    g[...] = both[:rows] + both[rows:] + before[...]
 
 
 def contracted(geo, step, group, g, value, atoms):
@@ -440,20 +472,19 @@
 
 
 def middle_kernel(
-    geo, nbrs, own, below, above, across, x, lx, val, s_w, mix_w, cols,
+    geo, nbrs, above, across, before, x, lx, val, s_w, mix_w, cols,
     g, slope_out, x_out, emb_out, val_out, lx_out, env_out, split, *, group,
 ):
     step = pl.program_id(0)
-    atoms = own.shape[1]
+    atoms = above.shape[1]
     norm = 1.0 / math.sqrt(geo.shape[1])
 
     @pl.when(step == 0)
     def _():
-        fill_split(own, below, above, across, split)
+        fill_split((above, across), split)
         env_out[...] = jnp.zeros_like(env_out)
 
-    chosen = chosen_columns(nbrs, step, group, split.shape[1])
-    gathered(split, chosen, own, g, group)
+    add_rest(split, chosen_columns(nbrs, step, group, 2 * atoms, 2 * atoms), before, g)
     _, s = contracted(geo, step, group, g, val[...], atoms)
     update, slope = silu_pair(lx[...] + product(s_w[0], s))
     slope_out[...] = slope
@@ -475,17 +506,18 @@
         partial(middle_kernel, group=group),
         grid=(slots // group,),
         out_shape=[edge_shape(r, edges) for r in rows] + [edge_shape(HARM * TENSORS, atoms)],
-        in_specs=[WHOLE] * 6
-        + [edge_spec(r, width) for r in (LATENT, LATENT, TENSORS)]
+        in_specs=[WHOLE] * 4
+        + [edge_spec(r, width) for r in (HARM * TENSORS, LATENT, LATENT, TENSORS)]
         + [WHOLE] * 3,
         out_specs=[edge_spec(r, width) for r in rows] + [WHOLE],
-        scratch_shapes=[pltpu.VMEM((2 * HARM * TENSORS, 4 * atoms), BF16)],
-        compiler_params=params(),
+        scratch_shapes=[pltpu.VMEM((2 * HARM * TENSORS, 2 * atoms), BF16)],
+        compiler_params=params(),
+        cost_estimate=effort(8 * HARM * TENSORS * atoms * edges),
         name="middle_pass",
     )(geo, nbrs, *blocks, x, lx, val, s_w, mix_w, cols)
 
 
-def pull_mixed(geo, step, group, g, value, ds, chosen, dgeo, d_own, d_wide, dg, atoms):
+def pull_mixed(geo, step, group, g, value, ds, dgeo, d_own, dg, atoms):
     columns = []
     for q in range(group):
         k = step * group + q
@@ -511,32 +543,25 @@
             dg[rows, span] = high
             dg[slice(HARM * TENSORS + m * TENSORS, HARM * TENSORS + (m + 1) * TENSORS), span] = low
         columns.append(total)
-    both = dot_nt(dg[...], chosen)
-    rows = HARM * TENSORS
-    for number, out in enumerate(d_wide):
-        span = slice(number * atoms, (number + 1) * atoms)
-        out[...] += both[:rows, span] + both[rows:, span]
     return jnp.concatenate(columns, 1)
 
 
 def last_kernel(
-    geo, nbrs, own, below, above, across, x, lx, val, s_w, back_w, cols, base,
-    energy, dx_out, dval_out, dgeo, d_own, d_below, d_above, d_across, split, g, dg, *, group,
+    geo, nbrs, above, across, before, x, lx, val, s_w, back_w, cols, base,
+    energy, dx_out, dval_out, dgeo, d_own, dg, split, g, *, group,
 ):
     step = pl.program_id(0)
-    atoms = own.shape[1]
+    atoms = above.shape[1]
     norm = 1.0 / math.sqrt(geo.shape[1])
 
     @pl.when(step == 0)
     def _():
-        fill_split(own, below, above, across, split)
+        fill_split((above, across), split)
         energy[...] = base[...]
         dgeo[...] = jnp.zeros_like(dgeo)
-        for out in (d_own, d_below, d_above, d_across):
-            out[...] = jnp.zeros_like(out)
-
-    chosen = chosen_columns(nbrs, step, group, split.shape[1])
-    gathered(split, chosen, own, g, group)
+        d_own[...] = jnp.zeros_like(d_own)
+
+    add_rest(split, chosen_columns(nbrs, step, group, 2 * atoms, 2 * atoms), before, g)
     value = val[...]
     _, s = contracted(geo, step, group, g, value, atoms)
     update, slope = silu_pair(lx[...] + product(s_w[1], s))
@@ -555,8 +580,7 @@
     pulled = product(back_w[1], d_fresh * slope)
     dx_out[...] = d_fresh + pulled[:LATENT]
     dval_out[...] = pull_mixed(
-        geo, step, group, g, value, pulled[LATENT:], chosen, dgeo, d_own,
-        (d_own, d_below, d_above, d_across), dg, atoms,
+        geo, step, group, g, value, pulled[LATENT:], dgeo, d_own, dg, atoms
     )
 
 
@@ -573,18 +597,20 @@
             edge_shape(LATENT, edges),
             edge_shape(TENSORS, edges),
             jax.ShapeDtypeStruct((HARM, slots, atoms), F32),
-        ]
-        + [edge_shape(rows, atoms)] * 4,
-        in_specs=[WHOLE] * 6
-        + [edge_spec(r, width) for r in (LATENT, LATENT, TENSORS)]
+            edge_shape(rows, atoms),
+            jax.ShapeDtypeStruct((2 * rows, edges), BF16),
+        ],
+        in_specs=[WHOLE] * 4
+        + [edge_spec(r, width) for r in (rows, LATENT, LATENT, TENSORS)]
         + [WHOLE] * 4,
-        out_specs=[WHOLE, edge_spec(LATENT, width), edge_spec(TENSORS, width)] + [WHOLE] * 5,
+        out_specs=[WHOLE, edge_spec(LATENT, width), edge_spec(TENSORS, width), WHOLE, WHOLE]
+        + [edge_spec(2 * rows, width)],
         scratch_shapes=[
-            pltpu.VMEM((2 * rows, 4 * atoms), BF16),
+            pltpu.VMEM((2 * rows, 2 * atoms), BF16),
             pltpu.VMEM((rows, width), F32),
-            pltpu.VMEM((2 * rows, width), BF16),
         ],
         compiler_params=params(),
+        cost_estimate=effort(8 * rows * atoms * edges),
         name="last_pass",
     )(geo, nbrs, *blocks, x, lx, val, s_w, back_w, cols, base)
 
@@ -610,8 +636,8 @@
 
 
 def middle_back_kernel(
-    geo, nbrs, own, low, high, dgeo_in, dx, dval, emb, g, slope, val, ev_w, back_w,
-    dx_out, dval_out, dgeo, d_own, d_below, d_above, d_across, total, dg, *, group,
+    geo, own, low, high, dgeo_in, dx, dval, emb, g, slope, val, ev_w, back_w,
+    dx_out, dval_out, dgeo, d_own, dg, total, *, group,
 ):
     step = pl.program_id(0)
     atoms = own.shape[1]
@@ -621,21 +647,18 @@
     def _():
         total[...] = own[...] + low[...] + high[...]
         dgeo[...] = dgeo_in[...]
-        for out in (d_own, d_below, d_above, d_across):
-            out[...] = jnp.zeros_like(out)
-
-    chosen = chosen_columns(nbrs, step, group, 4 * atoms)
+        d_own[...] = jnp.zeros_like(d_own)
+
     demb = pull_env(geo, step, group, total, emb, dgeo, atoms, norm)
     d_fresh = dx[...] + product(ev_w[1], jnp.concatenate([demb, dval[...]], 0))
     pulled = product(back_w[0], d_fresh * slope[...])
     dx_out[...] = d_fresh + pulled[:LATENT]
     dval_out[...] = pull_mixed(
-        geo, step, group, g, val[...], pulled[LATENT:], chosen, dgeo, d_own,
-        (d_own, d_below, d_above, d_across), dg, atoms,
-    )
-
-
-def middle_back(geo, nbrs, grads, dgeo, dx, dval, emb, g, slope, val, ev_w, back_w, group):
+        geo, step, group, g, val[...], pulled[LATENT:], dgeo, d_own, dg, atoms
+    )
+
+
+def middle_back(geo, grads, dgeo, dx, dval, emb, g, slope, val, ev_w, back_w, group):
     _, slots, atoms = geo.shape
     width = group * atoms
     edges = slots * atoms
@@ -647,16 +670,19 @@
             edge_shape(LATENT, edges),
             edge_shape(TENSORS, edges),
             jax.ShapeDtypeStruct((HARM, slots, atoms), F32),
-        ]
-        + [edge_shape(rows, atoms)] * 4,
-        in_specs=[WHOLE] * 6
+            edge_shape(rows, atoms),
+            jax.ShapeDtypeStruct((2 * rows, edges), BF16),
+        ],
+        in_specs=[WHOLE] * 5
         + [edge_spec(r, width) for r in (LATENT, TENSORS, TENSORS, rows, LATENT, TENSORS)]
         + [WHOLE] * 2,
-        out_specs=[edge_spec(LATENT, width), edge_spec(TENSORS, width)] + [WHOLE] * 5,
-        scratch_shapes=[pltpu.VMEM((rows, atoms), F32), pltpu.VMEM((2 * rows, width), BF16)],
-        compiler_params=params(),
+        out_specs=[edge_spec(LATENT, width), edge_spec(TENSORS, width), WHOLE, WHOLE]
+        + [edge_spec(2 * rows, width)],
+        scratch_shapes=[pltpu.VMEM((rows, atoms), F32)],
+        compiler_params=params(),
+        cost_estimate=effort(2 * rows * atoms * edges),
         name="middle_back",
-    )(geo, nbrs, *grads, dgeo, dx, dval, emb, g, slope, val, ev_w, back_w)
+    )(geo, *grads, dgeo, dx, dval, emb, g, slope, val, ev_w, back_w)
 
 
 def first_back_kernel(
@@ -783,17 +809,105 @@
     return jnp.concatenate([up, down], 1)
 
 
-def ghost_env(env, wanted, face):
+def picked(returned, wanted, place, atoms):
+    rows = lax.broadcasted_iota(jnp.int32, (atoms, wanted.shape[1]), 0) + place * atoms
+    chosen = (rows == wanted[...]).astype(F32).astype(BF16)
+    both = dot_nt(stacked(returned[...]), chosen)
+    half = both.shape[0] // 2
+    return both[:half] + both[half:]
+
+
+def scatter_kernel(nbrs, dg, *rest, group, place, returning):
+    out = rest[-1]
+    step = pl.program_id(0)
+    rows, atoms = out.shape
+
+    @pl.when(step == 0)
+    def _():
+        start = picked(rest[0], rest[1], place, atoms) if returning else jnp.zeros(out.shape, F32)
+        out[...] = start + rest[2][...] if place == 0 else start
+
+    both = dot_nt(dg[...], chosen_columns(nbrs, step, group, place * atoms, atoms))
+    out[...] += both[:rows] + both[rows:]
+
+
+def scatter_block(nbrs, dg, place, group, *rest):
+    slots, atoms = nbrs.shape
+    rows = dg.shape[0] // 2
+    return pl.pallas_call(
+        partial(scatter_kernel, group=group, place=place, returning=len(rest) > 1),
+        grid=(slots // group,),
+        out_shape=edge_shape(rows, atoms),
+        in_specs=[WHOLE, edge_spec(2 * rows, group * atoms)] + [WHOLE] * len(rest),
+        out_specs=WHOLE,
+        compiler_params=params(),
+        cost_estimate=effort(4 * rows * atoms * slots * atoms),
+        name="scatter_block",
+    )(nbrs, dg, *rest)
+
+
+def add_picked_kernel(returned, wanted, block, out, *, place):
+    out[...] = block[...] + picked(returned, wanted, place, block.shape[1])
+
+
+def add_picked(returned, wanted, block, place):
+    return pl.pallas_call(
+        partial(add_picked_kernel, place=place),
+        out_shape=jax.ShapeDtypeStruct(block.shape, F32),
+        in_specs=[WHOLE] * 3,
+        out_specs=WHOLE,
+        compiler_params=params(),
+        name="add_picked",
+    )(returned, wanted, block)
+
+
+def spread_env(env, nbrs, wanted, face, group):
     below = passed_along(env, "gx", 1)
-    above = passed_along(env, "gx", -1)
+    part = gather_block(nbrs, env, env, 0, group)
+    env_up, below, part = lax.optimization_barrier((env, below, part))
+    above = passed_along(env_up, "gx", -1)
+    part = gather_block(nbrs, below, part, 1, group)
+    below, part = lax.optimization_barrier((below, part))
     across = swap_y(lend_env(env, below, above, wanted), face)
-    return env, below, above, across
+    return above, across, part
+
+
+def env_grads(d_own, dg, nbrs, wanted, face, group, total, steps):
+    total = sum_step(total, steps)
+    across = scatter_block(nbrs, dg, 3, group)
+    returned = return_y(across, face)
+    dg, across = lax.optimization_barrier((dg, across))
+    below = scatter_block(nbrs, dg, 1, group)
+    returned, below, total = lax.optimization_barrier((returned, below, total))
+    total = sum_step(total, steps)
+    below = add_picked(returned, wanted, below, 1)
+    from_above = passed_along(below, "gx", -1)
+    dg, below = lax.optimization_barrier((dg, below))
+    above = scatter_block(nbrs, dg, 2, group, returned, wanted)
+    dg, above, from_above, total = lax.optimization_barrier((dg, above, from_above, total))
+    from_below = passed_along(above, "gx", 1)
+    own = scatter_block(nbrs, dg, 0, group, returned, wanted, d_own)
+    return (own, from_above, from_below), total
 
 
 def owned_grads(own, below, above, across, wanted, face):
     returned = return_y(across, face)
     own, below, above = take_back(returned, wanted, own, below, above)
     return own, passed_along(below, "gx", -1), passed_along(above, "gx", 1)
+
+
+def sum_steps():
+    count = lax.axis_size("gx")
+    if count & (count - 1) or lax.axis_size("gy") != 2:
+        return None
+    return [("gy", 1)] + [("gx", 1 << n) for n in range(count.bit_length() - 1)]
+
+
+def sum_step(total, steps):
+    if steps:
+        axis, by = steps.pop(0)
+        total = total + passed_along(total, axis, by)
+    return total
 
 
 def per_device(
@@ -840,22 +954,28 @@
     across = swap_y(lent, face)
     vec, geo, nbrs, base = geometry(rows, below, above, across, nbrs, species_shift, face)
     x0, slope_a, emb0, val0, lx0, env0 = first_pass(geo, rows, two_w, mix_w, cols, group)
-    blocks = ghost_env(env0, wanted, face)
+    blocks = spread_env(env0, nbrs, wanted, face, group)
     g0, slope0, x1, emb1, val1, lx1, env1 = middle_pass(
         geo, nbrs, blocks, x0, lx0, val0, s_w, mix_w, cols, group
     )
-    blocks = ghost_env(env1, wanted, face)
-    energy, dx, dval, dgeo, *grads = last_pass(
+    blocks = spread_env(env1, nbrs, wanted, face, group)
+    energy, dx, dval, dgeo, d_own, dg = last_pass(
         geo, nbrs, blocks, x1, lx1, val1, s_w, back_w, cols, base, group
     )
-    total = lax.psum(jnp.sum(energy), ("gx", "gy"))
-    mean_energy = total / (atoms * lax.axis_size("gx") * lax.axis_size("gy"))
-    grads = owned_grads(*grads, wanted, face)
-    dx, dval, dgeo, *grads = middle_back(
-        geo, nbrs, grads, dgeo, dx, dval, emb1, g0, slope0, val0, ev_w, back_w, group
-    )
-    grads = owned_grads(*grads, wanted, face)
+    total = jnp.sum(energy)
+    steps = sum_steps()
+    if steps is None:
+        total = lax.psum(total, ("gx", "gy"))
+    total = jnp.full((8, 128), total, F32)
+    grads, total = env_grads(d_own, dg, nbrs, wanted, face, group, total, steps)
+    dx, dval, dgeo, d_own, dg = middle_back(
+        geo, grads, dgeo, dx, dval, emb1, g0, slope0, val0, ev_w, back_w, group
+    )
+    grads, total = env_grads(d_own, dg, nbrs, wanted, face, group, total, steps)
     dgeo = first_back(geo, grads, dgeo, dx, dval, emb0, slope_a, ev_w, rad_w, group)
+    while steps:
+        total = sum_step(total, steps)
+    mean_energy = total[0, 0] / (atoms * lax.axis_size("gx") * lax.axis_size("gy"))
     grads = owned_grads(*geometry_back(vec, dgeo, nbrs), wanted, face)
     forces = -(grads[0] + grads[1] + grads[2])[:3]
     return (energy[None], forces[None, None], mean_energy.reshape(1))

time: 349 us -> 356 us (1.020)
  Pallas kernels: 185 us -> 289 us
  waiting for transfers between devices: 94.1 us -> 22.6 us
  blocking collectives: 32.4 us -> 0 us
  starting transfers between devices: 16.5 us -> 21.5 us
    pallas_call x0 -> x14, Pallas kernels: none -> 162 us  [the longest x8 103 us: scatter_block(): pl.pallas_call(partial(scatter_kernel, group=group, place=place, returnin...]
    ppermute x18 -> x22, waiting for transfers between devices: 94.1 us -> 22.6 us  [passed_along(): lax.ppermute(value, axis, [(i, (i + by) % count) for i in range(count)])]
    psum x1 -> x0, blocking collectives: 32.4 us -> none  [per_device(): total = lax.psum(jnp.sum(energy), ('gx', 'gy'))]
    pallas_call x1, Pallas kernels: 61.7 us -> 29.7 us  [last_pass(): pl.pallas_call(partial(last_kernel, group=group), grid=(slots // group,),...]
    pallas_call x1, Pallas kernels: 38.7 us -> 24.9 us  [middle_back(): pl.pallas_call(partial(middle_back_kernel, group=group), grid=(slots // g...]
    pallas_call x3 -> x1, Pallas kernels: 8.16 us -> 1.76 us  [take_back(): pl.pallas_call(take_back_kernel, out_shape=[jax.ShapeDtypeStruct(own.shap...]
    pallas_call x1, Pallas kernels: 34.9 us -> 29 us  [middle_pass(): pl.pallas_call(partial(middle_kernel, group=group), grid=(slots // group,...]
    ppermute x18 -> x22, starting transfers between devices: 16.5 us -> 21.5 us  [passed_along(): lax.ppermute(value, axis, [(i, (i + by) % count) for i in range(count)])]
  transfers between devices with their start and end apart: 18 -> 22, of which waited for: 10 -> 10; matrix products, arithmetic and copies ran while one was open for 1% -> 2% of each run, Pallas kernels for 1% -> 38%
where the time goes in v2:
time: 356 us; the launch traced here: 354 us
  Pallas kernels  289 us (81%)
  waiting for transfers between devices  22.6 us (6%)
  starting transfers between devices  21.5 us (6%)
  local copies, waits for them, and re-layouts  14.9 us (4%)
    pallas_call x8, Pallas kernels, scatter_block(): pl.pallas_call(partial(scatter_kernel, group=group, place=place, returnin...  103 us
    pallas_call x4, Pallas kernels, gather_block(): pl.pallas_call(partial(gather_kernel, group=group, place=place), grid=(sl...  54 us
    pallas_call x1, Pallas kernels, last_pass(): pl.pallas_call(partial(last_kernel, group=group), grid=(slots // group,),...  29.7 us
    pallas_call x1, Pallas kernels, middle_pass(): pl.pallas_call(partial(middle_kernel, group=group), grid=(slots // group,...  29 us
    pallas_call x1, Pallas kernels, middle_back(): pl.pallas_call(partial(middle_back_kernel, group=group), grid=(slots // g...  24.9 us
    ppermute x22, waiting for transfers between devices, passed_along(): lax.ppermute(value, axis, [(i, (i + by) % count) for i in range(count)])  22.6 us
    ppermute x22, starting transfers between devices, passed_along(): lax.ppermute(value, axis, [(i, (i + by) % count) for i in range(count)])  21.5 us
    pallas_call x1, Pallas kernels, first_back(): pl.pallas_call(partial(first_back_kernel, group=group), grid=(slots // gr...  12.5 us
  transfers between devices with their start and end apart: 22, of which 10 were waited for; matrix products, arithmetic and copies ran while one was open for 2% of the time, Pallas kernels for 38%

profile of v2, /device:TPU:0, one launch (start us, length us, event | category | flops | bytes accessed | tf_op | source)
XLA Modules:
  0.0 353.6 jit_solution(846822175828190332)
XLA Ops:
  2.8 6.0 %collective-permute-start.1 = (f32[8,384]{1,0:T(8,128)S(1)}, f32[8,384]{1,0:T(8,128)S(1)}, u32[]{:S(2)}, u32[]{:S(2)}) collective-permute-start(f32[8,384]{1,0:T(8,128)S(1)} %maximum_maximum_fusion.own), channel_id=1, source_target_pairs={{0,14},{2,0},{4,2},{6,4},{8,6},{10,8},{12,10},{14,12},{1,15},{3,1}... | collective-permute-start | bytes 36872 | tf_op jit(solution)/shard_map/ppermute | solution.py:33
  10.2 5.0 %collective-permute-done.below = f32[8,384]{1,0:T(8,128)S(1)} collective-permute-done((f32[8,384]{1,0:T(8,128)S(1)}, f32[8,384]{1,0:T(8,128)S(1)}, u32[]{:S(2)}, u32[]{:S(2)}) %collective-permute-start) | collective-permute-done | bytes 12320 | tf_op jit(solution)/shard_map/ppermute | solution.py:33
  20.4 2.4 prepare_weights.1
  23.4 3.5 %geometry.1 = (f32[3,32,384]{2,1,0:T(8,128)}, f32[18,32,384]{2,1,0:T(8,128)}, s32[32,384]{1,0:T(8,128)}, f32[1,384]{1,0:T(1,128)}) custom-call(f32[8,384]{1,0:T(8,128)} %copy-done.12, f32[8,384]{1,0:T(8,128)} %copy-done.14, f32[8,384]{1,0:T(8,128)} %copy-done.13, f32[8,384]{1,0:T(8,128)} %copy-done.15, s32[32,384]{1,0:T(8,128)} %bitcast.16, f32[5]{0:T(128)} %shift.1), custom_call_target="tpu_custom_call" | custom-call | tf_op jit(solution)/shard_map/geometry/pallas_call | solution.py:266
  26.9 11.9 %first_pass.1 = (f32[128,12288]{1,0:T(8,128)}, f32[128,12288]{1,0:T(8,128)}, f32[32,12288]{1,0:T(8,128)}, f32[32,12288]{1,0:T(8,128)}, f32[128,12288]{1,0:T(8,128)}, /*index=5*/f32[288,384]{1,0:T(8,128)}) custom-call(f32[18,32,384]{2,1,0:T(8,128)} %get-tuple-element.76.geo, f32[8,384]{1,0:T(8,128)} %copy-done.12, bf16[256,48]{1,0:T(8,128)(2,1)} %get-tuple-element.78.two_w, ...), custom_call_target="tpu_custom_call" | custom-call | tf_op jit(solution)/shard_map/first_pass/pallas_call | solution.py:344
  38.9 11.9 %gather_block.4.before = f32[288,12288]{1,0:T(8,128)} custom-call(s32[32,384]{1,0:T(8,128)} %get-tuple-element.77.nbrs, f32[288,384]{1,0:T(8,128)} %get-tuple-element.82.block.before.own, f32[288,384]{1,0:T(8,128)} %get-tuple-element.82.block.before.own), custom_call_target="tpu_custom_call" | custom-call | flops 5435817984 | bytes 10616832 | tf_op jit(solution)/shard_map/gather_block/pallas_call | solution.py:436
  50.8 3.6 %collective-permute-done.3.block.below = f32[288,384]{1,0:T(8,128)S(1)} collective-permute-done((f32[288,384]{1,0:T(8,128)}, f32[288,384]{1,0:T(8,128)S(1)}, u32[]{:S(2)}, u32[]{:S(2)}) %collective-permute-start.3) | collective-permute-done | bytes 442400 | tf_op jit(solution)/shard_map/ppermute | solution.py:33
  55.5 15.2 %gather_block.5.before = f32[288,12288]{1,0:T(8,128)} custom-call(s32[32,384]{1,0:T(8,128)} %get-tuple-element.77.nbrs, f32[288,384]{1,0:T(8,128)} %copy-done, f32[288,12288]{1,0:T(8,128)} %gather_block.4.before), custom_call_target="tpu_custom_call" | custom-call | flops 5435817984 | bytes 10616832 | tf_op jit(solution)/shard_map/gather_block/pallas_call | solution.py:436
  71.5 3.0 lend_env.2
  74.5 2.0 collective-permute-done.5.across
  77.3 29.0 %middle_pass.1 = (f32[288,12288]{1,0:T(8,128)}, f32[128,12288]{1,0:T(8,128)}, f32[128,12288]{1,0:T(8,128)}, f32[32,12288]{1,0:T(8,128)}, f32[32,12288]{1,0:T(8,1...) custom-call(f32[18,32,384]{2,1,0:T(8,128)} %get-tuple-element.76.geo, s32[32,384]{1,0:T(8,128)} %get-tuple-element.77.nbrs, ...), custom_call_target="tpu_custom_call" | custom-call | flops 10871635968 | bytes 21233664 | tf_op jit(solution)/shard_map/middle_pass/pallas_call | solution.py:505
  107.2 11.8 %gather_block.6.before = f32[288,12288]{1,0:T(8,128)} custom-call(s32[32,384]{1,0:T(8,128)} %get-tuple-element.77.nbrs, f32[288,384]{1,0:T(8,128)} %get-tuple-element.93.block.before.own, f32[288,384]{1,0:T(8,128)} %get-tuple-element.93.block.before.own), custom_call_target="tpu_custom_call" | custom-call | flops 5435817984 | bytes 10616832 | tf_op jit(solution)/shard_map/gather_block/pallas_call | solution.py:436
  118.9 2.5 collective-permute-done.6.block.below
  123.1 15.2 %gather_block.7.before = f32[288,12288]{1,0:T(8,128)} custom-call(s32[32,384]{1,0:T(8,128)} %get-tuple-element.77.nbrs, f32[288,384]{1,0:T(8,128)} %copy-done.1, f32[288,12288]{1,0:T(8,128)} %gather_block.6.before), custom_call_target="tpu_custom_call" | custom-call | flops 5435817984 | bytes 10616832 | tf_op jit(solution)/shard_map/gather_block/pallas_call | solution.py:436
  139.0 3.0 lend_env.3
  144.8 29.7 %last_pass.1 = (f32[1,384]{1,0:T(1,128)}, f32[128,12288]{1,0:T(8,128)}, f32[32,12288]{1,0:T(8,128)}, f32[9,32,384]{2,1,0:T(8,128)}, f32[288,384]{1,0:T(8,128)}, /*index=5*/bf16[576,12288]{1,0:T(8,128)(2,1)}) custom-call(f32[18,32,384]{2,1,0:T(8,128)} %get-tuple-element.76.geo, s32[32,384]{1,0:T(8,128)} %get-tuple-element.77.nbrs, f32[288,384]{1,0:T(8,128)} %copy-done.7, ...), custom_call_target="tpu_custom_call" | custom-call | flops 10871635968 | bytes 21233664 | tf_op jit(solution)/shard_map/last_pass/pallas_call | solution.py:592
  174.5 12.6 %scatter_block.8 = f32[288,384]{1,0:T(8,128)} custom-call(s32[32,384]{1,0:T(8,128)} %get-tuple-element.77.nbrs, bf16[576,12288]{1,0:T(8,128)(2,1)} %get-tuple-element.111.dg), custom_call_target="tpu_custom_call" | custom-call | flops 5435817984 | bytes 10616832 | tf_op jit(solution)/shard_map/scatter_block/pallas_call | solution.py:837
  189.0 12.5 %scatter_block.9.block = f32[288,384]{1,0:T(8,128)} custom-call(s32[32,384]{1,0:T(8,128)} %get-tuple-element.77.nbrs, bf16[576,12288]{1,0:T(8,128)(2,1)} %get-tuple-element.111.dg), custom_call_target="tpu_custom_call" | custom-call | flops 5435817984 | bytes 10616832 | tf_op jit(solution)/shard_map/scatter_block/pallas_call | solution.py:837
  202.9 2.4 add_picked.2
  207.4 13.0 %scatter_block.10 = f32[288,384]{1,0:T(8,128)} custom-call(s32[32,384]{1,0:T(8,128)} %get-tuple-element.77.nbrs, bf16[576,12288]{1,0:T(8,128)(2,1)} %get-tuple-element.111.dg, f32[288,384]{1,0:T(8,128)} %copy-done.10, s32[1,384]{1,0:T(1,128)} %get-tuple-element.86.wanted.rest_1_), custom_call_target="tpu_custom_call" | custom-call | flops 5435817984 | bytes 10616832 | tf_op jit(solution)/shard_map/scatter_block/pallas_call | solution.py:837
  222.1 13.2 %scatter_block.11.own = f32[288,384]{1,0:T(8,128)} custom-call(s32[32,384]{1,0:T(8,128)} %get-tuple-element.77.nbrs, bf16[576,12288]{1,0:T(8,128)(2,1)} %get-tuple-element.111.dg, f32[288,384]{1,0:T(8,128)} %copy-done.10, s32[1,384]{1,0:T(1,128)} %get-tuple-element.86.wanted.rest_1_, f32[288,384]{1,0:T(8,128)} %get-tuple-element.112.rest_2_), custom_call_target="tpu_custom_call" | custom-call | flops 5435817984 | bytes 10616832 | tf_op jit(solution)/shard_map/scatter_block/pallas_call | solution.py:837
  236.1 24.9 %middle_back.1 = (f32[128,12288]{1,0:T(8,128)}, f32[32,12288]{1,0:T(8,128)}, f32[9,32,384]{2,1,0:T(8,128)}, f32[288,384]{1,0:T(8,128)}, bf16[576,12288]{1,0:T(8,128)(2,1)}) custom-call(f32[18,32,384]{2,1,0:T(8,128)} %get-tuple-element.76.geo, f32[288,384]{1,0:T(8,128)} %scatter_block.11.own, f32[288,384]{1,0:T(8,128)} %copy-done.2, f32[288,384]{1,0:T(8,128)} %copy-done.4, ...), custom_call_target="tpu_custom_call" | custom-call | flops 2717908992 | bytes 5308416 | tf_op jit(solution)/shard_map/middle_back/pallas_call | solution.py:666
  261.0 12.6 %scatter_block.12 = f32[288,384]{1,0:T(8,128)} custom-call(s32[32,384]{1,0:T(8,128)} %get-tuple-element.77.nbrs, bf16[576,12288]{1,0:T(8,128)(2,1)} %get-tuple-element.129.dg), custom_call_target="tpu_custom_call" | custom-call | flops 5435817984 | bytes 10616832 | tf_op jit(solution)/shard_map/scatter_block/pallas_call | solution.py:837
  273.6 12.6 %scatter_block.13.block = f32[288,384]{1,0:T(8,128)} custom-call(s32[32,384]{1,0:T(8,128)} %get-tuple-element.77.nbrs, bf16[576,12288]{1,0:T(8,128)(2,1)} %get-tuple-element.129.dg), custom_call_target="tpu_custom_call" | custom-call | flops 5435817984 | bytes 10616832 | tf_op jit(solution)/shard_map/scatter_block/pallas_call | solution.py:837
  286.9 2.4 add_picked.3
  289.3 3.4 collective-permute-start.16
  292.7 13.0 %scatter_block.14 = f32[288,384]{1,0:T(8,128)} custom-call(s32[32,384]{1,0:T(8,128)} %get-tuple-element.77.nbrs, bf16[576,12288]{1,0:T(8,128)(2,1)} %get-tuple-element.129.dg, f32[288,384]{1,0:T(8,128)} %copy-done.11, s32[1,384]{1,0:T(1,128)} %get-tuple-element.86.wanted.rest_1_), custom_call_target="tpu_custom_call" | custom-call | flops 5435817984 | bytes 10616832 | tf_op jit(solution)/shard_map/scatter_block/pallas_call | solution.py:837
  307.2 13.2 %scatter_block.15.own = f32[288,384]{1,0:T(8,128)} custom-call(s32[32,384]{1,0:T(8,128)} %get-tuple-element.77.nbrs, bf16[576,12288]{1,0:T(8,128)(2,1)} %get-tuple-element.129.dg, f32[288,384]{1,0:T(8,128)} %copy-done.11, s32[1,384]{1,0:T(1,128)} %get-tuple-element.86.wanted.rest_1_, f32[288,384]{1,0:T(8,128)} %get-tuple-element.130.rest_2_), custom_call_target="tpu_custom_call" | custom-call | flops 5435817984 | bytes 10616832 | tf_op jit(solution)/shard_map/scatter_block/pallas_call | solution.py:837
  321.8 12.5 %first_back.1.dgeo = f32[17,32,384]{2,1,0:T(8,128)} custom-call(f32[18,32,384]{2,1,0:T(8,128)} %get-tuple-element.76.geo, f32[288,384]{1,0:T(8,128)} %scatter_block.15.own, f32[288,384]{1,0:T(8,128)} %copy-done.3, f32[288,384]{1,0:T(8,128)} %copy-done.5, f32[9,32,384]{2,1,0:T(8,128)} %get-tuple-element.133.dgeo_in, f32[128,12288]{1,0:T(8,128)} %get-tuple-element.134.dx, ...), custom_call_target="tpu_custom_call" | custom-call | tf_op jit(solution)/shard_map/first_back/pallas_call | solution.py:712
  334.3 3.7 %geometry_back.1 = (f32[8,384]{1,0:T(8,128)}, f32[8,384]{1,0:T(8,128)}, f32[8,384]{1,0:T(8,128)}, f32[8,384]{1,0:T(8,128)}) custom-call(f32[3,32,384]{2,1,0:T(8,128)} %get-tuple-element.104.vec, f32[17,32,384]{2,1,0:T(8,128)} %first_back.1.dgeo, s32[32,384]{1,0:T(8,128)} %get-tuple-element.77.nbrs), custom_call_target="tpu_custom_call" | custom-call | tf_op jit(solution)/shard_map/geometry_back/pallas_call | solution.py:785
  341.8 2.7 collective-permute-start.20
  346.1 5.0 %collective-permute-done.21 = f32[8,384]{1,0:T(8,128)S(1)} collective-permute-done((f32[8,384]{1,0:T(8,128)}, f32[8,384]{1,0:T(8,128)S(1)}, u32[]{:S(2)}, u32[]{:S(2)}) %collective-permute-start.21) | collective-permute-done | bytes 12320 | tf_op jit(solution)/shard_map/ppermute | solution.py:33
  (99 shorter events, 35.7 us)
Async XLA Ops:
  2.8 12.4 %copy-start.12 = (f32[8,384]{1,0:T(8,128)}, f32[8,384]{1,0:T(8,128)S(1)}, u32[]{:S(2)}) copy-start(f32[8,384]{1,0:T(8,128)S(1)} %maximum_maximum_fusion.own) | copy-start | bytes 36868
  2.8 7.4 %collective-permute-start.1 = (f32[8,384]{1,0:T(8,128)S(1)}, f32[8,384]{1,0:T(8,128)S(1)}, u32[]{:S(2)}, u32[]{:S(2)}) collective-permute-start(f32[8,384]{1,0:T(8,128)S(1)} %maximum_maximum_fusion.own), channel_id=1, source_target_pairs={{0,14},{2,0},{4,2},{6,4},{8,6},{10,8},{12,10},{14,12},{1,15},{3,1}... | collective-permute-start | bytes 36872 | tf_op jit(solution)/shard_map/ppermute | solution.py:33
  8.8 6.4 %collective-permute-start = (f32[8,384]{1,0:T(8,128)S(1)}, f32[8,384]{1,0:T(8,128)S(1)}, u32[]{:S(2)}, u32[]{:S(2)}) collective-permute-start(f32[8,384]{1,0:T(8,128)S(1)} %maximum_maximum_fusion.own), channel_id=1, source_target_pairs={{0,2},{2,4},{4,6},{6,8},{8,10},{10,12},{12,14},{14,0},{1,3},{3,5},... | collective-permute-start | bytes 36872 | tf_op jit(solution)/shard_map/ppermute | solution.py:33
  10.2 5.0 %copy-start.13 = (f32[8,384]{1,0:T(8,128)}, f32[8,384]{1,0:T(8,128)S(1)}, u32[]{:S(2)}) copy-start(f32[8,384]{1,0:T(8,128)S(1)} %collective-permute-done.1.above) | copy-start | bytes 36868
  17.4 5.4 %collective-permute-start.2 = (f32[8,384]{1,0:T(8,128)}, f32[8,384]{1,0:T(8,128)S(1)}, u32[]{:S(2)}, u32[]{:S(2)}) collective-permute-start(f32[8,384]{1,0:T(8,128)} %get-tuple-element.75), channel_id=1, source_target_pairs={{0,1},{1,0},{2,3},{3,2},{4,5},{5,4},{6,7},{7,6},{8,9},{9,8},{10,11... | collective-permute-start | bytes 36872 | tf_op jit(solution)/shard_map/ppermute | solution.py:33
  38.8 15.6 %collective-permute-start.3 = (f32[288,384]{1,0:T(8,128)}, f32[288,384]{1,0:T(8,128)S(1)}, u32[]{:S(2)}, u32[]{:S(2)}) collective-permute-start(f32[288,384]{1,0:T(8,128)} %get-tuple-element.82.block.before.own), channel_id=1, source_target_pairs={{0,2},{2,4},{4,6},{6,8},{8,10},{10,12},{12,14},{14,0},{1,3},{3,5},... | collective-permute-start | bytes 1327112 | tf_op jit(solution)/shard_map/ppermute | solution.py:33
  38.9 15.5 %copy-start.9 = (f32[288,384]{1,0:T(8,128)S(1)}, f32[288,384]{1,0:T(8,128)}, u32[]{:S(2)}) copy-start(f32[288,384]{1,0:T(8,128)} %get-tuple-element.82.block.before.own) | copy-start | bytes 1327108
  54.4 1.1 copy-start
  54.4 16.3 %collective-permute-start.4 = (f32[288,384]{1,0:T(8,128)S(1)}, f32[288,384]{1,0:T(8,128)S(1)}, u32[]{:S(2)}, u32[]{:S(2)}) collective-permute-start(f32[288,384]{1,0:T(8,128)S(1)} %copy-done.9), channel_id=1, source_target_pairs={{0,14},{2,0},{4,2},{6,4},{8,6},{10,8},{12,10},{14,12},{1,15},{3,1}... | collective-permute-start | bytes 1327112 | tf_op jit(solution)/shard_map/ppermute | solution.py:33
  74.5 2.0 collective-permute-start.5
  76.5 0.8 copy-start.19
  106.3 15.2 %copy-start.6 = (f32[288,384]{1,0:T(8,128)S(1)}, f32[288,384]{1,0:T(8,128)}, u32[]{:S(2)}) copy-start(f32[288,384]{1,0:T(8,128)} %get-tuple-element.93.block.before.own) | copy-start | bytes 1327108
  106.3 15.1 %collective-permute-start.6 = (f32[288,384]{1,0:T(8,128)}, f32[288,384]{1,0:T(8,128)S(1)}, u32[]{:S(2)}, u32[]{:S(2)}) collective-permute-start(f32[288,384]{1,0:T(8,128)} %get-tuple-element.93.block.before.own), channel_id=1, source_target_pairs={{0,2},{2,4},{4,6},{6,8},{8,10},{10,12},{12,14},{14,0},{1,3},{3,5},... | collective-permute-start | bytes 1327112 | tf_op jit(solution)/shard_map/ppermute | solution.py:33
  121.4 1.6 copy-start.1
  121.4 16.8 %collective-permute-start.7 = (f32[288,384]{1,0:T(8,128)S(1)}, f32[288,384]{1,0:T(8,128)S(1)}, u32[]{:S(2)}, u32[]{:S(2)}) collective-permute-start(f32[288,384]{1,0:T(8,128)S(1)} %copy-done.6), channel_id=1, source_target_pairs={{0,14},{2,0},{4,2},{6,4},{8,6},{10,8},{12,10},{14,12},{1,15},{3,1}... | collective-permute-start | bytes 1327112 | tf_op jit(solution)/shard_map/ppermute | solution.py:33
  142.0 2.0 collective-permute-start.8
  174.5 12.7 %copy-start.17 = (f32[1,384]{1,0:T(1,128)S(1)}, f32[1,384]{1,0:T(1,128)}, u32[]{:S(2)}) copy-start(f32[1,384]{1,0:T(1,128)} %get-tuple-element.103) | copy-start | bytes 4612
  187.1 15.0 %collective-permute-start.9 = (f32[288,384]{1,0:T(8,128)}, f32[288,384]{1,0:T(8,128)S(1)}, u32[]{:S(2)}, u32[]{:S(2)}) collective-permute-start(f32[288,384]{1,0:T(8,128)} %scatter_block.8), channel_id=1, source_target_pairs={{0,1},{1,0},{2,3},{3,2},{4,5},{5,4},{6,7},{7,6},{8,9},{9,8},{10,11... | collective-permute-start | bytes 1327112 | tf_op jit(solution)/shard_map/ppermute | solution.py:33
  188.5 13.0 %collective-permute-start.10 = (f32[8,128]{1,0:T(8,128)S(1)}, f32[8,128]{1,0:T(8,128)S(1)}, u32[]{:S(2)}, u32[]{:S(2)}) collective-permute-start(f32[8,128]{1,0:T(8,128)S(1)} %broadcast_in_dim.30), channel_id=1, source_target_pairs={{0,1},{1,0},{2,3},{3,2},{4,5},{5,4},{6,7},{7,6},{8,9},{9,8},{10,11... | collective-permute-start | bytes 12296 | tf_op jit(solution)/shard_map/ppermute | solution.py:33
  205.3 15.1 %collective-permute-start.11 = (f32[288,384]{1,0:T(8,128)}, f32[288,384]{1,0:T(8,128)S(1)}, u32[]{:S(2)}, u32[]{:S(2)}) collective-permute-start(f32[288,384]{1,0:T(8,128)} %add_picked.2), channel_id=1, source_target_pairs={{0,14},{2,0},{4,2},{6,4},{8,6},{10,8},{12,10},{14,12},{1,15},{3,1}... | collective-permute-start | bytes 1327112 | tf_op jit(solution)/shard_map/ppermute | solution.py:33
  205.9 14.5 %collective-permute-start.12 = (f32[8,128]{1,0:T(8,128)S(1)}, f32[8,128]{1,0:T(8,128)S(1)}, u32[]{:S(2)}, u32[]{:S(2)}) collective-permute-start(f32[8,128]{1,0:T(8,128)S(1)} %broadcast_add_fusion), channel_id=1, source_target_pairs={{0,2},{2,4},{4,6},{6,8},{8,10},{10,12},{12,14},{14,0},{1,3},{3,5},... | collective-permute-start | bytes 12296 | tf_op jit(solution)/shard_map/ppermute | solution.py:33
  220.4 14.9 %copy-start.2 = (f32[288,384]{1,0:T(8,128)}, f32[288,384]{1,0:T(8,128)S(1)}, u32[]{:S(2)}) copy-start(f32[288,384]{1,0:T(8,128)S(1)} %collective-permute-done.11.low) | copy-start | bytes 1327108
  220.4 14.9 %collective-permute-start.15 = (f32[8,128]{1,0:T(8,128)S(1)}, f32[8,128]{1,0:T(8,128)S(1)}, u32[]{:S(2)}, u32[]{:S(2)}) collective-permute-start(f32[8,128]{1,0:T(8,128)S(1)} %add.19), channel_id=1, source_target_pairs={{0,4},{2,6},{4,8},{6,10},{8,12},{10,14},{12,0},{14,2},{1,5},{3,7},... | collective-permute-start | bytes 12296 | tf_op jit(solution)/shard_map/ppermute | solution.py:33
  220.5 14.9 %collective-permute-start.13 = (f32[288,384]{1,0:T(8,128)}, f32[288,384]{1,0:T(8,128)S(1)}, u32[]{:S(2)}, u32[]{:S(2)}) collective-permute-start(f32[288,384]{1,0:T(8,128)} %scatter_block.10), channel_id=1, source_target_pairs={{0,2},{2,4},{4,6},{6,8},{8,10},{10,12},{12,14},{14,0},{1,3},{3,5},... | collective-permute-start | bytes 1327112 | tf_op jit(solution)/shard_map/ppermute | solution.py:33
  273.6 12.6 %collective-permute-start.14 = (f32[288,384]{1,0:T(8,128)}, f32[288,384]{1,0:T(8,128)S(1)}, u32[]{:S(2)}, u32[]{:S(2)}) collective-permute-start(f32[288,384]{1,0:T(8,128)} %scatter_block.12), channel_id=1, source_target_pairs={{0,1},{1,0},{2,3},{3,2},{4,5},{5,4},{6,7},{7,6},{8,9},{9,8},{10,11... | collective-permute-start | bytes 1327112 | tf_op jit(solution)/shard_map/ppermute | solution.py:33
  289.3 16.4 %collective-permute-start.16 = (f32[288,384]{1,0:T(8,128)}, f32[288,384]{1,0:T(8,128)S(1)}, u32[]{:S(2)}, u32[]{:S(2)}) collective-permute-start(f32[288,384]{1,0:T(8,128)} %add_picked.3), channel_id=1, source_target_pairs={{0,14},{2,0},{4,2},{6,4},{8,6},{10,8},{12,10},{14,12},{1,15},{3,1}... | collective-permute-start | bytes 1327112 | tf_op jit(solution)/shard_map/ppermute | solution.py:33
  292.7 13.0 %collective-permute-start.17 = (f32[8,128]{1,0:T(8,128)S(1)}, f32[8,128]{1,0:T(8,128)S(1)}, u32[]{:S(2)}, u32[]{:S(2)}) collective-permute-start(f32[8,128]{1,0:T(8,128)S(1)} %add.20), channel_id=1, source_target_pairs={{0,8},{2,10},{4,12},{6,14},{8,0},{10,2},{12,4},{14,6},{1,9},{3,11}... | collective-permute-start | bytes 12296 | tf_op jit(solution)/shard_map/ppermute | solution.py:33
  305.7 14.7 %copy-start.3 = (f32[288,384]{1,0:T(8,128)}, f32[288,384]{1,0:T(8,128)S(1)}, u32[]{:S(2)}) copy-start(f32[288,384]{1,0:T(8,128)S(1)} %collective-permute-done.16.low) | copy-start | bytes 1327108
  305.8 15.3 %collective-permute-start.18 = (f32[288,384]{1,0:T(8,128)}, f32[288,384]{1,0:T(8,128)S(1)}, u32[]{:S(2)}, u32[]{:S(2)}) collective-permute-start(f32[288,384]{1,0:T(8,128)} %scatter_block.14), channel_id=1, source_target_pairs={{0,2},{2,4},{4,6},{6,8},{8,10},{10,12},{12,14},{14,0},{1,3},{3,5},... | collective-permute-start | bytes 1327112 | tf_op jit(solution)/shard_map/ppermute | solution.py:33
  338.0 1.4 collective-permute-start.19
  341.8 4.4 %collective-permute-start.20 = (f32[8,384]{1,0:T(8,128)}, f32[8,384]{1,0:T(8,128)S(1)}, u32[]{:S(2)}, u32[]{:S(2)}) collective-permute-start(f32[8,384]{1,0:T(8,128)} %get-tuple-element.144), channel_id=1, source_target_pairs={{0,14},{2,0},{4,2},{6,4},{8,6},{10,8},{12,10},{14,12},{1,15},{3,1}... | collective-permute-start | bytes 36872 | tf_op jit(solution)/shard_map/ppermute | solution.py:33
  344.5 6.6 %collective-permute-start.21 = (f32[8,384]{1,0:T(8,128)}, f32[8,384]{1,0:T(8,128)S(1)}, u32[]{:S(2)}, u32[]{:S(2)}) collective-permute-start(f32[8,384]{1,0:T(8,128)} %get-tuple-element.145), channel_id=1, source_target_pairs={{0,2},{2,4},{4,6},{6,8},{8,10},{10,12},{12,14},{14,0},{1,3},{3,5},... | collective-permute-start | bytes 36872 | tf_op jit(solution)/shard_map/ppermute | solution.py:33
  (10 other events, 7.2 us)

commit v3 on v1

v3 whole, which is shorter than its diff:
```python
from functools import partial
import math

import jax
import jax.numpy as jnp
from jax import lax
from jax.experimental import pallas as pl
from jax.experimental.pallas import tpu as pltpu
from jax.sharding import PartitionSpec as P

BASIS = 8
SPECIES = 5
SITES_X = 2
SITES_Y = 16
CUTOFF = 2.5
LATENT = 128
TENSORS = 32
HARM = 9
UNIT = 128
ROOT3 = math.sqrt(3.0)
DEGREE = (0, 1, 1, 1, 2, 2, 2, 2, 2)
F32 = jnp.float32
BF16 = jnp.bfloat16
WHOLE = pl.BlockSpec(memory_space=pltpu.VMEM)
SCALARS = pl.BlockSpec(memory_space=pltpu.SMEM)


def params():
    return pltpu.CompilerParams(vmem_limit_bytes=60 << 20)


def passed_along(value, axis, by):
    count = lax.axis_size(axis)
    return lax.ppermute(value, axis, [(i, (i + by) % count) for i in range(count)])


def dot(a, b):
    return jnp.dot(a, b, preferred_element_type=F32)


def dot_nt(a, b):
    return lax.dot_general(a, b, (((1,), (1,)), ((), ())), preferred_element_type=F32)


def halves(value):
    high = value.astype(BF16)
    return high, (value - high.astype(F32)).astype(BF16)


def stacked(value):
    return jnp.concatenate(halves(value), 0)


def product(weights, value):
    rows = weights.shape[0] // 2
    both = dot(weights, stacked(value))
    return both[:rows] + both[rows:]


def rounded(value):
    high = value.astype(BF16).astype(F32)
    return high, value - high


def weights_kernel(two, bias, env, val, lat, lat_bias, out_w, *outs):
    two_out, mix_out, s_out, back_out, ev_out, rad_out, cols = outs

    def depth_stack(piece):
        high, low = rounded(piece)
        top = jnp.concatenate([high, high], 0)
        bottom = jnp.concatenate([low, jnp.zeros_like(low)], 0)
        return top.T, bottom.T

    def join(pieces):
        tops, bottoms = zip(*[depth_stack(p) for p in pieces])
        return jnp.concatenate(list(tops) + list(bottoms), 0).astype(BF16)

    def wide_stack(piece):
        high, low = rounded(piece)
        top = jnp.concatenate([high, high], 1)
        bottom = jnp.concatenate([low, jnp.zeros_like(low)], 1)
        return jnp.concatenate([top, bottom], 0).astype(BF16)

    width = two.shape[1]
    first = jnp.concatenate(
        [
            two[0:SPECIES, :],
            bias[...],
            jnp.zeros((2, width), F32),
            two[SPECIES : 2 * SPECIES, :],
            jnp.zeros((3, width), F32),
            two[2 * SPECIES :, :],
        ],
        0,
    )
    two_out[...] = join([first])
    rad_out[...] = wide_stack(two[2 * SPECIES :, :])
    for layer in range(env.shape[0]):
        latent = lat[layer]
        mix_out[layer] = join([env[layer], val[layer], latent[:width]])
        s_out[layer] = join([latent[width:]])
        back_out[layer] = wide_stack(latent)
        high = [rounded(env[layer].T), rounded(val[layer].T)]
        top = jnp.concatenate([high[0][0], high[1][0]] * 2, 0).T
        bottom = jnp.concatenate([high[0][1], high[1][1]] + [jnp.zeros_like(high[0][1])] * 2, 0).T
        ev_out[layer] = jnp.concatenate([top, bottom], 0).astype(BF16)
    columns = jnp.concatenate(
        [lat_bias[...], out_w[...], jnp.zeros((8 - lat_bias.shape[0] - 1, width), F32)], 0
    )
    cols[...] = columns.T


def prepare_weights(two, bias, env, val, lat, lat_bias, out_w):
    layers = env.shape[0]
    shapes = [
        (2 * LATENT, 48),
        (layers, 2 * (LATENT + 2 * TENSORS), 2 * LATENT),
        (layers, 2 * LATENT, 6 * TENSORS),
        (layers, 2 * (LATENT + 3 * TENSORS), 2 * LATENT),
        (layers, 2 * LATENT, 4 * TENSORS),
        (2 * BASIS, 2 * LATENT),
    ]
    out_shape = [jax.ShapeDtypeStruct(s, BF16) for s in shapes]
    out_shape.append(jax.ShapeDtypeStruct((LATENT, 8), F32))
    return pl.pallas_call(
        weights_kernel,
        out_shape=out_shape,
        in_specs=[WHOLE] * 7,
        out_specs=[WHOLE] * 7,
        compiler_params=params(),
        name="prepare_weights",
    )(two, bias[None], env, val, lat, lat_bias, out_w[None])


def shifted(rows, by_x, by_y):
    lane_row = lax.broadcasted_iota(jnp.int32, rows.shape, 0)
    return rows + jnp.where(lane_row == 0, by_x, jnp.where(lane_row == 1, by_y, 0.0))


def lane_pick(table, row, index, blocks):
    low = index & 127
    high = lax.shift_right_arithmetic(index, 7)
    found = jnp.zeros(index.shape, F32)
    for block in range(blocks):
        span = slice(block * 128, block * 128 + 128)
        source = table[...][:, span] if row is None else table[row : row + 1, span]
        source = jnp.broadcast_to(source, index.shape)
        taken = jnp.take_along_axis(source, low, axis=1)
        found = jnp.where(high == block, taken, found)
    return found


def fill_wide(own, below, above, table, remap):
    atoms = own.shape[1]
    table[:, 0:atoms] = own[...]
    table[:, atoms : 2 * atoms] = shifted(below[...], -float(SITES_X), 0.0)
    table[:, 2 * atoms : 3 * atoms] = shifted(above[...], float(SITES_X), 0.0)
    lanes = lax.broadcasted_iota(jnp.int32, (1, atoms), 1).astype(F32)
    remap[:, 0:atoms] = lanes
    remap[:, atoms : 2 * atoms] = below[5:6, :] + float(atoms)
    remap[:, 2 * atoms : 3 * atoms] = above[4:5, :] + float(2 * atoms)


def lend_kernel(own, below, above, wanted, rows_out, wanted_out, table, remap):
    atoms = own.shape[1]
    blocks = 3 * atoms // 128
    fill_wide(own, below, above, table, remap)
    for tile in range(wanted.shape[1] // 128):
        span = slice(tile * 128, tile * 128 + 128)
        index = jnp.broadcast_to(wanted[:, span], (8, 128))
        place = lane_pick(remap, 0, index, blocks).astype(jnp.int32)
        place = jnp.where(index < 0, -1, place)
        wanted_out[:, span] = place[0:1]
        rows_out[:, span] = lane_pick(table, None, place, blocks)


def lend_rows(own, below, above, wanted):
    atoms = own.shape[1]
    return pl.pallas_call(
        lend_kernel,
        out_shape=[
            jax.ShapeDtypeStruct(wanted.shape[:0] + (8, wanted.shape[1]), F32),
            jax.ShapeDtypeStruct(wanted.shape, jnp.int32),
        ],
        in_specs=[WHOLE] * 4,
        out_specs=[WHOLE] * 2,
        scratch_shapes=[pltpu.VMEM((8, 3 * atoms), F32), pltpu.VMEM((1, 3 * atoms), F32)],
        compiler_params=params(),
        name="lend_rows",
    )(own, below, above, wanted)


def distances(vx, vy, vz):
    dist = jnp.sqrt(vx * vx + vy * vy + vz * vz)
    inverse = 1.0 / dist
    scaled = jnp.minimum(dist * (1.0 / CUTOFF), 1.0)
    second = scaled * scaled
    fourth = second * second
    sixth = fourth * second
    cut = 1.0 - 28.0 * sixth + 48.0 * (sixth * scaled) - 21.0 * (sixth * second)
    rest = 1.0 - scaled
    slope = (-168.0 / CUTOFF) * (fourth * scaled) * (rest * rest)
    angle = scaled * math.pi
    return inverse, cut, slope, jnp.sin(angle), jnp.cos(angle)


def geometry_kernel(
    own, below, above, across, nbrs, shift, vec_out, geo_out, nbr_out, base_out, table, remap, face
):
    atoms = own.shape[1]
    slots = nbrs.shape[0]
    blocks = table.shape[1] // 128
    fill_wide(own, below, above, table, remap)
    lanes = lax.broadcasted_iota(jnp.int32, (8, atoms), 1)
    rows = lax.broadcasted_iota(jnp.int32, (8, atoms), 0)
    moved = across[...] + jnp.where(
        rows == 1, jnp.where(lanes < face, -float(SITES_Y), float(SITES_Y)), 0.0
    )
    empty = jnp.where(rows == 2, -1000.0, jnp.where(rows == 3, -1.0, 0.0))
    table[:, 3 * atoms : 4 * atoms] = jnp.where(lanes < 2 * face, moved, empty)
    remap[:, 3 * atoms : 4 * atoms] = (
        lax.broadcasted_iota(jnp.int32, (1, atoms), 1) + 3 * atoms
    ).astype(F32)
    base = jnp.zeros((1, atoms), F32)
    for kind in range(SPECIES):
        base = base + jnp.where(own[3:4, :] == float(kind), shift[kind], 0.0)
    base_out[...] = base
    for group in range(slots // 8):
        for tile in range(atoms // UNIT):
            span = slice(tile * UNIT, tile * UNIT + UNIT)
            index = nbrs[group * 8 : group * 8 + 8, span]
            up = slice(tile * slots + group * 8, tile * slots + group * 8 + 8)
            index = lane_pick(remap, 0, index, blocks).astype(jnp.int32)
            nbr_out[up, :] = index
            vx = lane_pick(table, 0, index, blocks) - own[0:1, span]
            vy = lane_pick(table, 1, index, blocks) - own[1:2, span]
            vz = lane_pick(table, 2, index, blocks) - own[2:3, span]
            kind = lane_pick(table, 3, index, blocks)
            vec_out[0, up, :] = vx
            vec_out[1, up, :] = vy
            vec_out[2, up, :] = vz
            inverse, cut, _, sine, cosine = distances(vx, vy, vz)
            ux, uy, uz = vx * inverse, vy * inverse, vz * inverse
            harm = [
                ux,
                uy,
                uz,
                ROOT3 * ux * uy,
                ROOT3 * uy * uz,
                0.5 * (3.0 * uz * uz - 1.0),
                ROOT3 * ux * uz,
                0.5 * ROOT3 * (ux * ux - uy * uy),
            ]
            geo_out[0, up, :] = cut
            for number, value in enumerate(harm):
                geo_out[1 + number, up, :] = value
            scale = math.sqrt(2.0 / CUTOFF) * inverse * cut
            before, now = jnp.zeros_like(sine), sine
            for number in range(BASIS):
                geo_out[9 + number, up, :] = now * scale
                before, now = now, 2.0 * cosine * now - before
            geo_out[17, up, :] = kind


def geometry(own, below, above, across, nbrs, shift, face):
    slots, atoms = nbrs.shape
    return pl.pallas_call(
        partial(geometry_kernel, face=face),
        out_shape=[
            jax.ShapeDtypeStruct((3, slots * atoms // UNIT, UNIT), F32),
            jax.ShapeDtypeStruct((18, slots * atoms // UNIT, UNIT), F32),
            jax.ShapeDtypeStruct((slots * atoms // UNIT, UNIT), jnp.int32),
            jax.ShapeDtypeStruct((1, atoms), F32),
        ],
        in_specs=[WHOLE] * 5 + [SCALARS],
        out_specs=[WHOLE] * 4,
        scratch_shapes=[pltpu.VMEM((8, 4 * atoms), F32), pltpu.VMEM((1, 4 * atoms), F32)],
        compiler_params=params(),
        name="geometry",
    )(own, below, above, across, nbrs, shift)


def silu_pair(pre):
    gate = 1.0 / (1.0 + jnp.exp(-pre))
    value = pre * gate
    return value, gate + value * (1.0 - gate)


def row_spec(count, group, first):
    return pl.BlockSpec((count, group, UNIT), lambda i: (0, first + i, 0))


def index_spec(group, first):
    return pl.BlockSpec((group, UNIT), lambda i: (first + i, 0))


def edge_spec(rows, group, first):
    return pl.BlockSpec((rows, group * UNIT), lambda i: (0, first + i))


def unit_spec(rows, per):
    return pl.BlockSpec((rows, UNIT), lambda i: (0, i // per))


def edge_shape(rows, edges):
    return jax.ShapeDtypeStruct((rows, edges), F32)


def lanes_of(q):
    return slice(q * UNIT, (q + 1) * UNIT)


def rows_of(m):
    return slice(m * TENSORS, (m + 1) * TENSORS)


def add_env(geo, step, per, group, embed, env_out, norm):
    @pl.when(step % per == 0)
    def _():
        env_out[...] = jnp.zeros_like(env_out)

    cuts = [geo[0, q : q + 1, :] * norm for q in range(group)]
    for m in range(HARM):
        total = env_out[rows_of(m), :]
        for q in range(group):
            factor = cuts[q] if m == 0 else cuts[q] * geo[m, q : q + 1, :]
            total = total + embed[:TENSORS, lanes_of(q)] * factor
        env_out[rows_of(m), :] = total


def first_kernel(
    geo, own, two_w, mix_w, cols, x_out, slope_out, emb_out, val_out, lx_out, env_out,
    *, group, per, norm,
):
    step = pl.program_id(0)
    kinds = lax.broadcasted_iota(jnp.int32, (8, UNIT), 0)
    kinds_f = kinds.astype(F32)
    centre = jnp.where((own[3:4, :] == kinds_f) & (kinds < SPECIES), 1.0, 0.0)
    centre = jnp.where(kinds == SPECIES, 1.0, centre)
    parts = []
    for q in range(group):
        other = jnp.where(geo[17, q : q + 1, :] == kinds_f, 1.0, 0.0)
        radial = [geo[9 + n, q : q + 1, :] for n in range(BASIS)]
        parts.append(jnp.concatenate([centre, other] + radial, 0))
    features = jnp.concatenate(parts, 1)
    x, slope = silu_pair(product(two_w[...], features))
    x_out[...] = x
    slope_out[...] = slope
    mixed = product(mix_w[0], x)
    emb_out[...] = mixed[:TENSORS]
    val_out[...] = mixed[TENSORS : 2 * TENSORS]
    lx_out[...] = mixed[2 * TENSORS :] + cols[:, 0:1]
    add_env(geo, step, per, group, mixed, env_out, norm)


def first_pass(geo, own, two_w, mix_w, cols, slots, group):
    edges = geo.shape[1] * UNIT
    per = slots // group
    rows = (LATENT, LATENT, TENSORS, TENSORS, LATENT)
    return pl.pallas_call(
        partial(first_kernel, group=group, per=per, norm=1.0 / math.sqrt(slots)),
        grid=(geo.shape[1] // group,),
        out_shape=[edge_shape(r, edges) for r in rows]
        + [edge_shape(HARM * TENSORS, own.shape[1])],
        in_specs=[row_spec(18, group, 0), unit_spec(8, per)] + [WHOLE] * 3,
        out_specs=[edge_spec(r, group, 0) for r in rows] + [unit_spec(HARM * TENSORS, per)],
        compiler_params=params(),
        name="first_pass",
    )(geo, own, two_w, mix_w, cols)


def chosen_rows(index, columns, start):
    rows = lax.broadcasted_iota(jnp.int32, (columns, index.shape[1]), 0) + start
    return (rows == index).astype(F32).astype(BF16)


def chosen_columns(nbrs, group, columns):
    return jnp.concatenate(
        [chosen_rows(nbrs[q : q + 1, :], columns, 0) for q in range(group)], 1
    )


def lend_env_kernel(wanted, *refs):
    out = refs[-1]
    rows = out.shape[0]
    total = jnp.zeros((2 * rows, out.shape[1]), F32)
    start = 0
    for block in refs[:-1]:
        chosen = chosen_rows(wanted[...], block.shape[1], start)
        total = total + dot(stacked(block[...]), chosen)
        start += block.shape[1]
    out[...] = total[:rows] + total[rows:]


def lend_env(wanted, pieces):
    return pl.pallas_call(
        lend_env_kernel,
        out_shape=jax.ShapeDtypeStruct((HARM * TENSORS, wanted.shape[1]), F32),
        in_specs=[WHOLE] * (1 + len(pieces)),
        out_specs=WHOLE,
        compiler_params=params(),
        name="lend_env",
    )(wanted, *pieces)


def take_back_kernel(returned, wanted, centre, wide, *outs, widths):
    atoms = centre.shape[1]
    rows = returned.shape[0]
    value = stacked(returned[...])
    for place in range(3):
        chosen = chosen_rows(wanted[...], atoms, place * atoms)
        both = dot_nt(value, chosen)
        total = wide[:, place * atoms : (place + 1) * atoms] + both[:rows] + both[rows:]
        if place == 0:
            total = total + centre[...]
        start = 0
        for number, width in enumerate(widths):
            outs[place * len(widths) + number][...] = total[:, start : start + width]
            start += width


def take_back(returned, wanted, centre, wide, widths):
    outs = pl.pallas_call(
        partial(take_back_kernel, widths=widths),
        out_shape=[edge_shape(centre.shape[0], w) for w in widths] * 3,
        in_specs=[WHOLE] * 4,
        out_specs=[WHOLE] * (3 * len(widths)),
        compiler_params=params(),
        name="take_back",
    )(returned, wanted, centre, wide)
    count = len(widths)
    return [outs[place * count : (place + 1) * count] for place in range(3)]


def fill_split(pieces, split):
    rows = pieces[0].shape[0]
    start = 0
    for block in pieces:
        span = slice(start, start + block.shape[1])
        high, low = halves(block[...])
        split[:rows, span] = high
        split[rows:, span] = low
        start += block.shape[1]


def gathered(split, chosen, own, g, group):
    rows = HARM * TENSORS
    both = dot(split[...], chosen)
    for q in range(group):
        g[:, lanes_of(q)] = both[:rows, lanes_of(q)] + both[rows:, lanes_of(q)] + own[...]


def contracted(geo, group, g, value):
    columns = []
    for q in range(group):
        span = lanes_of(q)
        sums = [g[0:TENSORS, span], None, None]
        for m in range(1, HARM):
            term = g[rows_of(m), span] * geo[m, q : q + 1, :]
            d = DEGREE[m]
            sums[d] = term if sums[d] is None else sums[d] + term
        columns.append(jnp.concatenate([part * value[:, span] for part in sums], 0))
    return jnp.concatenate(columns, 1)


def middle_kernel(*refs, group, per, norm, count, aliased):
    geo, nbrs, own, x, lx, val, s_w, mix_w, cols = refs[:9]
    pieces = refs[9 : 9 + count]
    g, slope_out, x_out, emb_out, val_out, lx_out, env_out, split = refs[9 + count + aliased :]
    step = pl.program_id(0)

    @pl.when(step == 0)
    def _():
        fill_split(pieces, split)

    chosen = chosen_columns(nbrs, group, split.shape[1])
    gathered(split, chosen, own, g, group)
    s = contracted(geo, group, g, val[...])
    update, slope = silu_pair(lx[...] + product(s_w[0], s))
    slope_out[...] = slope
    fresh = x[...] + update
    x_out[...] = fresh
    mixed = product(mix_w[1], fresh)
    emb_out[...] = mixed[:TENSORS]
    val_out[...] = mixed[TENSORS : 2 * TENSORS]
    lx_out[...] = mixed[2 * TENSORS :] + cols[:, 1:2]
    add_env(geo, step, per, group, mixed, env_out, norm)


def middle_pass(geo, nbrs, own, pieces, x, lx, val, s_w, mix_w, cols, slots, group, span, before):
    edges = x.shape[1]
    per = slots // group
    first = span[0] * per
    rows = (HARM * TENSORS, LATENT, LATENT, TENSORS, TENSORS, LATENT)
    ins = 9 + len(pieces)
    return pl.pallas_call(
        partial(
            middle_kernel, group=group, per=per, norm=1.0 / math.sqrt(slots),
            count=len(pieces), aliased=len(before),
        ),
        grid=((span[1] - span[0]) * per,),
        out_shape=[edge_shape(r, edges) for r in rows]
        + [edge_shape(HARM * TENSORS, (span[1] - span[0]) * UNIT)],
        in_specs=[
            row_spec(18, group, first),
            index_spec(group, first),
            pl.BlockSpec((HARM * TENSORS, UNIT), lambda i: (0, span[0] + i // per)),
        ]
        + [edge_spec(r, group, first) for r in (LATENT, LATENT, TENSORS)]
        + [WHOLE] * (3 + len(pieces))
        + [pl.BlockSpec(memory_space=pl.ANY)] * len(before),
        out_specs=[edge_spec(r, group, first) for r in rows] + [unit_spec(HARM * TENSORS, per)],
        scratch_shapes=[
            pltpu.VMEM((2 * HARM * TENSORS, sum(p.shape[1] for p in pieces)), BF16)
        ],
        input_output_aliases={ins + n: n for n in range(len(before))},
        compiler_params=params(),
        cost_estimate=effort(8 * HARM * TENSORS * edges * edges // slots),
        name="middle_pass",
    )(geo, nbrs, own, x, lx, val, s_w, mix_w, cols, *pieces, *before)


def effort(flops):
    return pl.CostEstimate(flops=flops, transcendentals=0, bytes_accessed=flops // 512)


def pull_mixed(geo, group, g, value, ds, chosen, dgeo, centre, wide, dg):
    columns = []
    for q in range(group):
        span = lanes_of(q)
        part = value[:, span]
        pulled = [ds[rows_of(d), span] for d in range(3)]
        scaled = [p * part for p in pulled]
        total = None
        for m in range(HARM):
            d = DEGREE[m]
            source = g[rows_of(m), span]
            if m == 0:
                total = source * pulled[0]
                grad = scaled[0]
            else:
                harm = geo[m, q : q + 1, :]
                total = total + source * pulled[d] * harm
                dgeo[m, q : q + 1, :] += jnp.sum(source * scaled[d], axis=0, keepdims=True)
                grad = scaled[d] * harm
            centre[rows_of(m), :] += grad
            high, low = halves(grad)
            dg[rows_of(m), span] = high
            dg[rows_of(HARM + m), span] = low
        columns.append(total)
    both = dot_nt(dg[...], chosen)
    rows = HARM * TENSORS
    wide[...] += both[:rows] + both[rows:]
    return jnp.concatenate(columns, 1)


def last_kernel(*refs, group, per, norm, count):
    geo, nbrs, own, x, lx, val, s_w, back_w, cols, base = refs[:10]
    pieces = refs[10 : 10 + count]
    energy, dx_out, dval_out, dgeo, centre, wide, split, g, dg = refs[10 + count :]
    step = pl.program_id(0)

    @pl.when(step == 0)
    def _():
        fill_split(pieces, split)
        wide[...] = jnp.zeros_like(wide)

    @pl.when(step % per == 0)
    def _():
        energy[...] = base[...]
        centre[...] = jnp.zeros_like(centre)

    chosen = chosen_columns(nbrs, group, split.shape[1])
    gathered(split, chosen, own, g, group)
    value = val[...]
    s = contracted(geo, group, g, value)
    update, slope = silu_pair(lx[...] + product(s_w[1], s))
    fresh = x[...] + update
    weight = cols[:, 2:3]
    read = jnp.sum(fresh * weight, axis=0, keepdims=True) * norm
    cuts = []
    dgeo[...] = jnp.zeros_like(dgeo)
    for q in range(group):
        cut = geo[0, q : q + 1, :]
        cuts.append(cut)
        energy[...] += read[:, lanes_of(q)] * cut
        dgeo[0, q : q + 1, :] = read[:, lanes_of(q)]
    d_fresh = weight * (jnp.concatenate(cuts, 1) * norm)
    pulled = product(back_w[1], d_fresh * slope)
    dx_out[...] = d_fresh + pulled[:LATENT]
    dval_out[...] = pull_mixed(
        geo, group, g, value, pulled[LATENT:], chosen, dgeo, centre, wide, dg
    )


def last_pass(geo, nbrs, own, pieces, x, lx, val, s_w, back_w, cols, base, slots, group):
    edges = x.shape[1]
    per = slots // group
    rows = HARM * TENSORS
    columns = sum(p.shape[1] for p in pieces)
    return pl.pallas_call(
        partial(
            last_kernel, group=group, per=per, norm=1.0 / math.sqrt(slots), count=len(pieces)
        ),
        grid=(geo.shape[1] // group,),
        out_shape=[
            jax.ShapeDtypeStruct(base.shape, F32),
            edge_shape(LATENT, edges),
            edge_shape(TENSORS, edges),
            jax.ShapeDtypeStruct((HARM,) + geo.shape[1:], F32),
            edge_shape(rows, base.shape[1]),
            edge_shape(rows, columns),
        ],
        in_specs=[row_spec(18, group, 0), index_spec(group, 0), unit_spec(rows, per)]
        + [edge_spec(r, group, 0) for r in (LATENT, LATENT, TENSORS)]
        + [WHOLE] * 3
        + [unit_spec(1, per)]
        + [WHOLE] * len(pieces),
        out_specs=[
            unit_spec(1, per),
            edge_spec(LATENT, group, 0),
            edge_spec(TENSORS, group, 0),
            row_spec(HARM, group, 0),
            unit_spec(rows, per),
            WHOLE,
        ],
        scratch_shapes=[
            pltpu.VMEM((2 * rows, columns), BF16),
            pltpu.VMEM((rows, group * UNIT), F32),
            pltpu.VMEM((2 * rows, group * UNIT), BF16),
        ],
        compiler_params=params(),
        cost_estimate=effort(16 * rows * edges * edges // slots),
        name="last_pass",
    )(geo, nbrs, own, x, lx, val, s_w, back_w, cols, base, *pieces)


def pull_env(geo, group, total, emb, dgeo, norm):
    columns = []
    for q in range(group):
        part = emb[:, lanes_of(q)]
        cut = geo[0, q : q + 1, :] * norm
        grad = None
        for m in range(HARM):
            source = total[rows_of(m), :]
            if m == 0:
                grad = source
            else:
                grad = grad + source * geo[m, q : q + 1, :]
                dgeo[m, q : q + 1, :] += cut * jnp.sum(source * part, axis=0, keepdims=True)
        dgeo[0, q : q + 1, :] += norm * jnp.sum(grad * part, axis=0, keepdims=True)
        columns.append(grad * cut)
    return jnp.concatenate(columns, 1)


def middle_back_kernel(*refs, group, per, norm, aliased):
    geo, nbrs, own, low, high, dgeo_in, dx, dval, emb, g, slope, val, ev_w, back_w = refs[:14]
    wide_in = refs[14] if aliased else None
    dx_out, dval_out, dgeo, centre, wide, total, dg = refs[14 + aliased :]
    step = pl.program_id(0)

    @pl.when(step == 0)
    def _():
        wide[...] = wide_in[...] if aliased else jnp.zeros_like(wide)

    @pl.when(step % per == 0)
    def _():
        total[...] = own[...] + low[...] + high[...]
        centre[...] = jnp.zeros_like(centre)

    chosen = chosen_columns(nbrs, group, wide.shape[1])
    dgeo[...] = dgeo_in[...]
    demb = pull_env(geo, group, total, emb, dgeo, norm)
    d_fresh = dx[...] + product(ev_w[1], jnp.concatenate([demb, dval[...]], 0))
    pulled = product(back_w[0], d_fresh * slope[...])
    dx_out[...] = d_fresh + pulled[:LATENT]
    dval_out[...] = pull_mixed(
        geo, group, g, val[...], pulled[LATENT:], chosen, dgeo, centre, wide, dg
    )


def middle_back(
    geo, nbrs, grads, dgeo, dx, dval, emb, g, slope, val, ev_w, back_w, slots, group, span, before
):
    edges = dx.shape[1]
    per = slots // group
    first = span[0] * per
    rows = HARM * TENSORS
    atoms = geo.shape[1] // slots * UNIT
    columns = 4 * atoms
    aliased = len(before)
    shapes = [
        edge_shape(LATENT, edges),
        edge_shape(TENSORS, edges),
        jax.ShapeDtypeStruct((HARM,) + geo.shape[1:], F32),
        edge_shape(rows, atoms),
        edge_shape(rows, columns),
    ]
    extra = [before[4], *before[:4]] if before else []
    return pl.pallas_call(
        partial(
            middle_back_kernel, group=group, per=per, norm=1.0 / math.sqrt(slots), aliased=aliased
        ),
        grid=((span[1] - span[0]) * per,),
        out_shape=shapes,
        in_specs=[row_spec(18, group, first), index_spec(group, first)]
        + [unit_spec(rows, per)] * 3
        + [row_spec(HARM, group, first)]
        + [
            edge_spec(r, group, first)
            for r in (LATENT, TENSORS, TENSORS, rows, LATENT, TENSORS)
        ]
        + [WHOLE] * 2
        + ([WHOLE] + [pl.BlockSpec(memory_space=pl.ANY)] * 4 if before else []),
        out_specs=[
            edge_spec(LATENT, group, first),
            edge_spec(TENSORS, group, first),
            row_spec(HARM, group, first),
            pl.BlockSpec((rows, UNIT), lambda i: (0, span[0] + i // per)),
            WHOLE,
        ],
        scratch_shapes=[
            pltpu.VMEM((rows, UNIT), F32),
            pltpu.VMEM((2 * rows, group * UNIT), BF16),
        ],
        input_output_aliases={15 + n: n for n in range(4)} if before else {},
        compiler_params=params(),
        cost_estimate=effort(8 * rows * edges * edges // slots),
        name="middle_back",
    )(geo, nbrs, *grads, dgeo, dx, dval, emb, g, slope, val, ev_w, back_w, *extra)


def first_back_kernel(
    geo, own, low, high, dgeo_in, dx, dval, emb, slope, ev_w, rad_w, dgeo, total,
    *, group, per, norm,
):
    step = pl.program_id(0)

    @pl.when(step % per == 0)
    def _():
        total[...] = own[...] + low[...] + high[...]

    dgeo[0:HARM] = dgeo_in[...]
    demb = pull_env(geo, group, total, emb, dgeo, norm)
    d_fresh = dx[...] + product(ev_w[0], jnp.concatenate([demb, dval[...]], 0))
    radial = product(rad_w[...], d_fresh * slope[...])
    for q in range(group):
        for n in range(BASIS):
            dgeo[HARM + n, q : q + 1, :] = radial[n : n + 1, lanes_of(q)]


def first_back(geo, grads, dgeo, dx, dval, emb, slope, ev_w, rad_w, slots, group):
    per = slots // group
    rows = HARM * TENSORS
    return pl.pallas_call(
        partial(first_back_kernel, group=group, per=per, norm=1.0 / math.sqrt(slots)),
        grid=(geo.shape[1] // group,),
        out_shape=jax.ShapeDtypeStruct((HARM + BASIS,) + geo.shape[1:], F32),
        in_specs=[row_spec(18, group, 0)]
        + [unit_spec(rows, per)] * 3
        + [row_spec(HARM, group, 0)]
        + [edge_spec(r, group, 0) for r in (LATENT, TENSORS, TENSORS, LATENT)]
        + [WHOLE] * 2,
        out_specs=row_spec(HARM + BASIS, group, 0),
        scratch_shapes=[pltpu.VMEM((rows, UNIT), F32)],
        compiler_params=params(),
        name="first_back",
    )(geo, *grads, dgeo, dx, dval, emb, slope, ev_w, rad_w)


def geometry_back_kernel(vec, dgeo, nbrs, centre_out, wide_out, dvec, *, slots):
    rows_total = vec.shape[1]
    units = rows_total // slots
    for group in range(rows_total // 8):
        up = slice(group * 8, group * 8 + 8)
        vx, vy, vz = (vec[axis, up, :] for axis in range(3))
        inverse, cut, slope, sine, cosine = distances(vx, vy, vz)
        ux, uy, uz = vx * inverse, vy * inverse, vz * inverse
        _, h1, h2, h3, h4, h5, h6, h7, h8 = (dgeo[m, up, :] for m in range(HARM))
        dux = h1 + ROOT3 * (uy * h4 + uz * h7 + ux * h8)
        duy = h2 + ROOT3 * (ux * h4 + uz * h5 - uy * h8)
        duz = h3 + ROOT3 * (uy * h5 + ux * h7) + 3.0 * uz * h6
        along = ux * dux + uy * duy + uz * duz
        scale = math.sqrt(2.0 / CUTOFF) * inverse
        by_wave = jnp.zeros_like(sine)
        by_angle = jnp.zeros_like(sine)
        before, now = jnp.zeros_like(sine), sine
        before_c, now_c = jnp.ones_like(sine), cosine
        for n in range(BASIS):
            pulled = dgeo[HARM + n, up, :]
            by_wave = by_wave + pulled * now
            by_angle = by_angle + (n + 1.0) * (pulled * now_c)
            before, now = now, 2.0 * cosine * now - before
            before_c, now_c = now_c, 2.0 * cosine * now_c - before_c
        d_dist = slope * dgeo[0, up, :] + scale * (
            (math.pi / CUTOFF) * by_angle * cut + by_wave * (slope - inverse * cut)
        )
        dvec[0, up, :] = (dux - ux * along) * inverse + ux * d_dist
        dvec[1, up, :] = (duy - uy * along) * inverse + uy * d_dist
        dvec[2, up, :] = (duz - uz * along) * inverse + uz * d_dist
    total = jnp.zeros((2 * 48, UNIT), F32)
    rows = lax.broadcasted_iota(jnp.int32, (16, UNIT), 0)
    lane = lax.broadcasted_iota(jnp.int32, (UNIT, UNIT), 0)
    for group in range(rows_total // 4):
        spreads, picks = [], []
        for k in range(group * 4, group * 4 + 4):
            index = nbrs[k : k + 1, :]
            here = rows == lax.shift_right_arithmetic(index, 7)
            spreads.append(
                jnp.concatenate(
                    [jnp.where(here, dvec[axis, k : k + 1, :], 0.0) for axis in range(3)], 0
                )
            )
            picks.append((lane == (index & 127)).astype(F32).astype(BF16))
        spread = jnp.concatenate(spreads, 1)
        total = total + dot_nt(stacked(spread), jnp.concatenate(picks, 1))
    total = total[:48] + total[48:]
    wide_out[...] = jnp.zeros_like(wide_out)
    centre_out[...] = jnp.zeros_like(centre_out)
    for axis in range(3):
        for block in range(wide_out.shape[1] // UNIT):
            row = axis * 16 + block
            wide_out[axis : axis + 1, lanes_of(block)] = total[row : row + 1]
        for unit in range(units):
            part = dvec[axis, unit * slots : (unit + 1) * slots, :]
            centre_out[axis : axis + 1, lanes_of(unit)] = -jnp.sum(part, axis=0, keepdims=True)


def geometry_back(vec, dgeo, nbrs, slots):
    atoms = vec.shape[1] // slots * UNIT
    return pl.pallas_call(
        partial(geometry_back_kernel, slots=slots),
        out_shape=[edge_shape(8, atoms), edge_shape(8, 4 * atoms)],
        in_specs=[WHOLE] * 3,
        out_specs=[WHOLE] * 2,
        scratch_shapes=[pltpu.VMEM(vec.shape, F32)],
        compiler_params=params(),
        name="geometry_back",
    )(vec, dgeo, nbrs)


def swap_y(rows, face):
    if lax.axis_size("gy") == 2:
        return passed_along(rows, "gy", 1)
    up = passed_along(rows[:, :face], "gy", 1)
    down = passed_along(rows[:, face:], "gy", -1)
    return jnp.concatenate([up, down], 1)


def return_y(rows, face):
    if lax.axis_size("gy") == 2:
        return passed_along(rows, "gy", 1)
    up = passed_along(rows[:, :face], "gy", -1)
    down = passed_along(rows[:, face:], "gy", 1)
    return jnp.concatenate([up, down], 1)


def across_part(wide):
    return wide[:, wide.shape[1] // 4 * 3 :]


def ghost_rows(parts, wanted, face):
    below = [passed_along(part, "gx", 1) for part in parts]
    above = [passed_along(part, "gx", -1) for part in parts]
    pieces = [*parts, *below, *above]
    return pieces + [swap_y(lend_env(wanted, pieces), face)]


def owned_grads(centre, wide, wanted, face, widths):
    returned = return_y(across_part(wide), face)
    own, below, above = take_back(returned, wanted, centre, wide, widths)
    found = []
    for number in range(len(widths)):
        send = below[number], above[number]
        if found:
            send, found[-1] = lax.optimization_barrier((send, found[-1]))
        found.append(
            [own[number], passed_along(send[0], "gx", -1), passed_along(send[1], "gx", 1)]
        )
    return found


def sum_steps():
    count = lax.axis_size("gx")
    if count & (count - 1) or lax.axis_size("gy") != 2:
        return None
    return [("gy", 1)] + [("gx", 1 << n) for n in range(count.bit_length() - 1)]


def sum_step(total, steps):
    if steps:
        axis, by = steps.pop(0)
        total = total + passed_along(total, axis, by)
    return total


def per_device(
    positions,
    species,
    neighbours,
    send_x,
    send_y,
    two_weight,
    two_bias,
    env_weight,
    value_weight,
    latent_weight,
    latent_bias,
    out_weight,
    species_shift,
):
    group = 8
    nbrs = neighbours[0, 0]
    atoms = nbrs.shape[1]
    face = send_y.shape[3]
    rows = jnp.concatenate(
        [
            positions[0, 0],
            species[0, 0][None].astype(F32),
            send_x[0, 0].astype(F32),
            jnp.zeros((2, atoms), F32),
        ],
        0,
    )
    wanted = jnp.concatenate(
        [
            send_y[0, 0, 1],
            send_y[0, 0, 0],
            jnp.full((atoms - 2 * face,), -1, jnp.int32),
        ]
    )[None]
    below = passed_along(rows, "gx", 1)
    above = passed_along(rows, "gx", -1)
    two_w, mix_w, s_w, back_w, ev_w, rad_w, cols = prepare_weights(
        two_weight, two_bias, env_weight, value_weight, latent_weight, latent_bias, out_weight
    )
    lent, wanted = lend_rows(rows, below, above, wanted)
    across = swap_y(lent, face)
    slots = nbrs.shape[0]
    units = atoms // UNIT
    vec, geo, nbrs, base = geometry(rows, below, above, across, nbrs, species_shift, face)
    x0, slope_a, emb0, val0, lx0, env0 = first_pass(
        geo, rows, two_w, mix_w, cols, slots, group
    )
    pieces = ghost_rows([env0], wanted, face)
    parts, before = [], []
    for span in ((0, units - 1), (units - 1, units)):
        *before, part = middle_pass(
            geo, nbrs, env0, pieces, x0, lx0, val0, s_w, mix_w, cols, slots, group, span, before
        )
        parts.append(part)
    g0, slope0, x1, emb1, val1, lx1 = before
    pieces = ghost_rows(parts, wanted, face)
    env1 = jnp.concatenate(parts, 1)
    energy, dx, dval, dgeo, centre, wide = last_pass(
        geo, nbrs, env1, pieces, x1, lx1, val1, s_w, back_w, cols, base, slots, group
    )
    total = jnp.sum(energy)
    steps = sum_steps()
    if steps is None:
        total = lax.psum(total, ("gx", "gy"))
    total = sum_step(jnp.full((8, 128), total, F32), steps)
    widths = (UNIT, atoms - UNIT)
    grads = owned_grads(centre, wide, wanted, face, widths)
    before = []
    for number, span in enumerate(((0, 1), (1, units))):
        grads[number][0], total = lax.optimization_barrier((grads[number][0], total))
        total = sum_step(total, steps)
        before = middle_back(
            geo, nbrs, grads[number], dgeo, dx, dval, emb1, g0, slope0, val0, ev_w, back_w,
            slots, group, span, before,
        )
    dx, dval, dgeo, centre, wide = before
    (grads,) = owned_grads(centre, wide, wanted, face, (atoms,))
    grads[0], total = lax.optimization_barrier((grads[0], total))
    total = sum_step(total, steps)
    dgeo = first_back(geo, grads, dgeo, dx, dval, emb0, slope_a, ev_w, rad_w, slots, group)
    while steps:
        total = sum_step(total, steps)
    mean_energy = total[0, 0] / (atoms * lax.axis_size("gx") * lax.axis_size("gy"))
    (grads,) = owned_grads(*geometry_back(vec, dgeo, nbrs, slots), wanted, face, (atoms,))
    forces = -(grads[0] + grads[1] + grads[2])[:3]
    return (energy[None], forces[None, None], mean_energy.reshape(1))


def solution(mesh):
    placed = (
        P(("groups", "gx"), "gy", None, None),
        P(("groups", "gx"), "gy", None),
        P(("groups", "gx"), "gy", None, None),
        P(("groups", "gx"), "gy", None, None),
        P(("groups", "gx"), "gy", None, None),
        P(),
        P(),
        P(),
        P(),
        P(),
        P(),
        P(),
        P(),
    )
    return jax.shard_map(
        per_device,
        mesh=mesh,
        in_specs=placed,
        out_specs=(
            P(("groups", "gx"), "gy", None),
            P(("groups", "gx"), "gy", None, None),
            P("groups"),
        ),
        check_vma=False,
    )
```

time: 349 us -> 334 us (0.957)
  blocking collectives: 32.4 us -> 0 us
  waiting for transfers between devices: 94.1 us -> 68 us
  Pallas kernels: 185 us -> 207 us
  starting transfers between devices: 16.5 us -> 30.1 us
  local copies, waits for them, and re-layouts: 14.9 us -> 18.6 us
    psum x1 -> x0, blocking collectives: 32.4 us -> none  [per_device(): total = lax.psum(jnp.sum(energy), ('gx', 'gy'))]
    ppermute x18 -> x26, waiting for transfers between devices: 94.1 us -> 68 us  [passed_along(): lax.ppermute(value, axis, [(i, (i + by) % count) for i in range(count)])]
    pallas_call x11 -> x13, Pallas kernels: 178 us -> 199 us  [the longest x1 65.5 us: last_pass(): pl.pallas_call(partial(last_kernel, group=group, per=per, norm=1.0 / math...]
    ppermute x18 -> x26, starting transfers between devices: 16.5 us -> 30.1 us  [passed_along(): lax.ppermute(value, axis, [(i, (i + by) % count) for i in range(count)])]
    unnamed x40 -> x48, local copies, waits for them, and re-layouts: 13.5 us -> 13.2 us
  transfers between devices with their start and end apart: 18 -> 26, of which waited for: 10 -> 14; matrix products, arithmetic and copies ran while one was open for 1% -> 3% of each run, Pallas kernels for 1% -> 11%
where the time goes in v3:
time: 334 us; the launch traced here: 332 us
  Pallas kernels  207 us (62%)
  waiting for transfers between devices  68 us (20%)
  starting transfers between devices  30.1 us (9%)
  local copies, waits for them, and re-layouts  18.6 us (6%)
  other arithmetic  5.92 us (2%)
    ppermute x26, waiting for transfers between devices, passed_along(): lax.ppermute(value, axis, [(i, (i + by) % count) for i in range(count)])  68 us
    pallas_call x1, Pallas kernels, last_pass(): pl.pallas_call(partial(last_kernel, group=group, per=per, norm=1.0 / math...  65.5 us
    pallas_call x2, Pallas kernels, middle_back(): pl.pallas_call(partial(middle_back_kernel, group=group, per=per, norm=1.0...  45.4 us
    pallas_call x2, Pallas kernels, middle_pass(): pl.pallas_call(partial(middle_kernel, group=group, per=per, norm=1.0 / ma...  42.2 us
    ppermute x26, starting transfers between devices, passed_along(): lax.ppermute(value, axis, [(i, (i + by) % count) for i in range(count)])  30.1 us
    pallas_call x1, Pallas kernels, first_back(): pl.pallas_call(partial(first_back_kernel, group=group, per=per, norm=1.0...  14.3 us
    pallas_call x1, Pallas kernels, first_pass(): pl.pallas_call(partial(first_kernel, group=group, per=per, norm=1.0 / mat...  13.7 us
    unnamed x48, local copies, waits for them, and re-layouts  13.2 us
  transfers between devices with their start and end apart: 26, of which 14 were waited for; matrix products, arithmetic and copies ran while one was open for 3% of the time, Pallas kernels for 11%

profile of v3, /device:TPU:0, one launch (start us, length us, event | category | flops | bytes accessed | tf_op | source)
XLA Modules:
  0.0 332.0 jit_solution(13671325930907993161)
XLA Ops:
  2.8 6.0 %collective-permute-start.1 = (f32[8,384]{1,0:T(8,128)S(1)}, f32[8,384]{1,0:T(8,128)S(1)}, u32[]{:S(2)}, u32[]{:S(2)}) collective-permute-start(f32[8,384]{1,0:T(8,128)S(1)} %maximum_maximum_fusion.own), channel_id=1, source_target_pairs={{0,14},{2,0},{4,2},{6,4},{8,6},{10,8},{12,10},{14,12},{1,15},{3,1}... | collective-permute-start | bytes 36872 | tf_op jit(solution)/shard_map/ppermute | solution.py:34
  10.2 5.0 %collective-permute-done.below = f32[8,384]{1,0:T(8,128)S(1)} collective-permute-done((f32[8,384]{1,0:T(8,128)S(1)}, f32[8,384]{1,0:T(8,128)S(1)}, u32[]{:S(2)}, u32[]{:S(2)}) %collective-permute-start) | collective-permute-done | bytes 12320 | tf_op jit(solution)/shard_map/ppermute | solution.py:34
  20.4 2.4 prepare_weights.1
  23.4 3.5 %geometry.1 = (f32[3,96,128]{2,1,0:T(8,128)}, f32[18,96,128]{2,1,0:T(8,128)}, s32[96,128]{1,0:T(8,128)}, f32[1,384]{1,0:T(1,128)}) custom-call(f32[8,384]{1,0:T(8,128)} %copy-done.12, f32[8,384]{1,0:T(8,128)} %copy-done.16, f32[8,384]{1,0:T(8,128)} %copy-done.15, f32[8,384]{1,0:T(8,128)} %copy-done.17, s32[32,384]{1,0:T(8,128)} %bitcast.16, f32[5]{0:T(128)} %shift.1), custom_call_target="tpu_custom_call" | custom-call | tf_op jit(solution)/shard_map/geometry/pallas_call | solution.py:267
  26.9 13.7 %first_pass.1 = (f32[128,12288]{1,0:T(8,128)}, f32[128,12288]{1,0:T(8,128)}, f32[32,12288]{1,0:T(8,128)}, f32[32,12288]{1,0:T(8,128)}, f32[128,12288]{1,0:T(8,128)}, /*index=5*/f32[288,384]{1,0:T(8,128)}) custom-call(f32[18,96,128]{2,1,0:T(8,128)} %get-tuple-element.78.geo.refs_0_, f32[8,384]{1,0:T(8,128)} %copy-done.12, ...), custom_call_target="tpu_custom_call" | custom-call | tf_op jit(solution)/shard_map/first_pass/pallas_call | solution.py:360
  42.7 20.2 %collective-permute-done.4.refs_2_.refs_11_ = f32[288,384]{1,0:T(8,128)S(1)} collective-permute-done((f32[288,384]{1,0:T(8,128)}, f32[288,384]{1,0:T(8,128)S(1)}, u32[]{:S(2)}, u32[]{:S(2)}) %collective-permute-start.4) | collective-permute-done | bytes 442400 | tf_op jit(solution)/shard_map/ppermute | solution.py:34
  63.8 3.0 lend_env.2
  66.8 2.0 collective-permute-done.5.refs_12_
  69.6 26.7 %middle_pass.2 = (f32[288,12288]{1,0:T(8,128)}, f32[128,12288]{1,0:T(8,128)}, f32[128,12288]{1,0:T(8,128)}, f32[32,12288]{1,0:T(8,128)}, f32[32,12288]{1,0:T(8,1...) custom-call(f32[18,96,128]{2,1,0:T(8,128)} %get-tuple-element.78.geo.refs_0_, s32[96,128]{1,0:T(8,128)} %get-tuple-element.79.refs_1_.nbrs, ...), custom_call_target="tpu_custom_call" | custom-call | flops 10871635968 | bytes 21233664 | tf_op jit(solution)/shard_map/middle_pass/pallas_call | solution.py:496
  98.4 15.4 %middle_pass.3 = (f32[288,12288]{1,0:T(8,128)}, f32[128,12288]{1,0:T(8,128)}, f32[128,12288]{1,0:T(8,128)}, f32[32,12288]{1,0:T(8,128)}, f32[32,12288]{1,0:T(8,1...) custom-call(f32[18,96,128]{2,1,0:T(8,128)} %get-tuple-element.78.geo, ...), custom_call_target="tpu_custom_call", output_to_operand_aliasing={{0}: (13, {}), {1}: (14, {}), {2}: (15, {}), {3}: (16, {}),... | custom-call | flops 10871635968 | bytes 21233664 | tf_op jit(solution)/shard_map/middle_pass/pallas_call | solution.py:496
  113.8 3.3 collective-permute-start.9
  117.1 3.2 collective-permute-done.9.refs_5_.refs_15_
  120.3 4.9 %collective-permute-done.7.refs_3_.refs_13_ = f32[288,128]{1,0:T(8,128)S(1)} collective-permute-done((f32[288,128]{1,0:T(8,128)}, f32[288,128]{1,0:T(8,128)S(1)}, u32[]{:S(2)}, u32[]{:S(2)}) %collective-permute-start.7) | collective-permute-done | bytes 147488 | tf_op jit(solution)/shard_map/ppermute | solution.py:34
  126.7 3.0 lend_env.3
  129.7 1.7 pad_maximum_fusion.refs_2_
  132.4 65.5 %last_pass.1 = (f32[1,384]{1,0:T(1,128)}, f32[128,12288]{1,0:T(8,128)}, f32[32,12288]{1,0:T(8,128)}, f32[9,96,128]{2,1,0:T(8,128)}, f32[288,384]{1,0:T(8,128)}, /*index=5*/f32[288,1536]{1,0:T(8,128)}) custom-call(f32[18,96,128]{2,1,0:T(8,128)} %get-tuple-element.78.geo.refs_0_, s32[96,128]{1,0:T(8,128)} %get-tuple-element.79.refs_1_.nbrs, ...), custom_call_target="tpu_custom_call" | custom-call | flops 21743271936 | bytes 42467328 | tf_op jit(solution)/shard_map/last_pass/pallas_call | solution.py:601
  202.3 3.5 %take_back.3 = (f32[288,128]{1,0:T(8,128)}, f32[288,256]{1,0:T(8,128)}, f32[288,128]{1,0:T(8,128)}, f32[288,256]{1,0:T(8,128)}, f32[288,128]{1,0:T(8,128)}, /*index=5*/f32[288,256]{1,0:T(8,128)}) custom-call(f32[288,384]{1,0:T(8,128)} %copy-done.6, s32[1,384]{1,0:T(1,128)} %get-tuple-element.88.wanted, f32[288,384]{1,0:T(8,128)} %get-tuple-element.105.centre, ...), custom_call_target="tpu_custom_call" | custom-call | tf_op jit(solution)/shard_map/take_back/pallas_call | solution.py:423
  208.5 3.5 %collective-permute-done.12.refs_3_ = f32[288,128]{1,0:T(8,128)S(1)} collective-permute-done((f32[288,128]{1,0:T(8,128)}, f32[288,128]{1,0:T(8,128)S(1)}, u32[]{:S(2)}, u32[]{:S(2)}) %collective-permute-start.12) | collective-permute-done | bytes 147488 | tf_op jit(solution)/shard_map/ppermute | solution.py:34
  212.1 3.3 %collective-permute-done.13.refs_4_ = f32[288,128]{1,0:T(8,128)S(1)} collective-permute-done((f32[288,128]{1,0:T(8,128)}, f32[288,128]{1,0:T(8,128)S(1)}, u32[]{:S(2)}, u32[]{:S(2)}) %collective-permute-start.13) | collective-permute-done | bytes 147488 | tf_op jit(solution)/shard_map/ppermute | solution.py:34
  215.4 4.7 %collective-permute-start.16 = (f32[288,256]{1,0:T(8,128)}, f32[288,256]{1,0:T(8,128)S(1)}, u32[]{:S(2)}, u32[]{:S(2)}) collective-permute-start(f32[288,256]{1,0:T(8,128)} %get-tuple-element.115), channel_id=1, source_target_pairs={{0,14},{2,0},{4,2},{6,4},{8,6},{10,8},{12,10},{14,12},{1,15},{3,1}... | collective-permute-start | bytes 884744 | tf_op jit(solution)/shard_map/ppermute | solution.py:34
  220.1 16.3 %middle_back.2 = (f32[128,12288]{1,0:T(8,128)}, f32[32,12288]{1,0:T(8,128)}, f32[9,96,128]{2,1,0:T(8,128)}, f32[288,384]{1,0:T(8,128)}, f32[288,1536]{1,0:T(8,128)}) custom-call(f32[18,96,128]{2,1,0:T(8,128)} %get-tuple-element.78.geo.refs_0_, s32[96,128]{1,0:T(8,128)} %get-tuple-element.79.refs_1_.nbrs, f32[288,128]{1,0:T(8,128)} %get-tuple-element.124.refs_2_, ...), custom_call_target="tpu_custom_call" | custom-call | flops 10871635968 | bytes 21233664 | tf_op jit(solution)/shard_map/middle_back/pallas_call | solution.py:700
  237.3 29.1 %middle_back.3 = (f32[128,12288]{1,0:T(8,128)}, f32[32,12288]{1,0:T(8,128)}, f32[9,96,128]{2,1,0:T(8,128)}, f32[288,384]{1,0:T(8,128)}, f32[288,1536]{1,0:T(8,128)}) custom-call(f32[18,96,128]{2,1,0:T(8,128)} %get-tuple-element.78.geo.refs_0_, ...), custom_call_target="tpu_custom_call", output_to_operand_aliasing={{0}: (15, {}), {1}: (16, {}), {2}: (17, {}), {3}: (18, {})} | custom-call | flops 10871635968 | bytes 21233664 | tf_op jit(solution)/shard_map/middle_back/pallas_call | solution.py:700
  267.5 1.8 collective-permute-done.18.returned
  270.1 3.5 %take_back.4 = (f32[288,384]{1,0:T(8,128)}, f32[288,384]{1,0:T(8,128)}, f32[288,384]{1,0:T(8,128)}) custom-call(f32[288,384]{1,0:T(8,128)} %copy-done.7, s32[1,384]{1,0:T(1,128)} %get-tuple-element.88.wanted, f32[288,384]{1,0:T(8,128)} %get-tuple-element.133.centre, f32[288,1536]{1,0:T(8,128)} %get-tuple-element.132.wide), custom_call_target="tpu_custom_call" | custom-call | tf_op jit(solution)/shard_map/take_back/pallas_call | solution.py:423
  273.6 4.7 %collective-permute-start.20 = (f32[288,384]{1,0:T(8,128)}, f32[288,384]{1,0:T(8,128)S(1)}, u32[]{:S(2)}, u32[]{:S(2)}) collective-permute-start(f32[288,384]{1,0:T(8,128)} %get-tuple-element.137), channel_id=1, source_target_pairs={{0,14},{2,0},{4,2},{6,4},{8,6},{10,8},{12,10},{14,12},{1,15},{3,1}... | collective-permute-start | bytes 1327112 | tf_op jit(solution)/shard_map/ppermute | solution.py:34
  278.3 10.1 %collective-permute-done.19 = f32[8,128]{1,0:T(8,128)S(1)} collective-permute-done((f32[8,128]{1,0:T(8,128)S(1)}, f32[8,128]{1,0:T(8,128)S(1)}, u32[]{:S(2)}, u32[]{:S(2)}) %collective-permute-start.19) | collective-permute-done | bytes 4128 | tf_op jit(solution)/shard_map/ppermute | solution.py:34
  288.4 7.1 %collective-permute-done.20.low = f32[288,384]{1,0:T(8,128)S(1)} collective-permute-done((f32[288,384]{1,0:T(8,128)}, f32[288,384]{1,0:T(8,128)S(1)}, u32[]{:S(2)}, u32[]{:S(2)}) %collective-permute-start.20) | collective-permute-done | bytes 442400 | tf_op jit(solution)/shard_map/ppermute | solution.py:34
  296.4 14.3 %first_back.1.dgeo = f32[17,96,128]{2,1,0:T(8,128)} custom-call(f32[18,96,128]{2,1,0:T(8,128)} %get-tuple-element.78.geo.refs_0_, f32[288,384]{1,0:T(8,128)} %get-tuple-element.136.own, f32[288,384]{1,0:T(8,128)} %copy-done.3, f32[288,384]{1,0:T(8,128)} %copy-done.5, f32[9,96,128]{2,1,0:T(8,128)} %get-tuple-element.139.dgeo_in, ...), custom_call_target="tpu_custom_call" | custom-call | tf_op jit(solution)/shard_map/first_back/pallas_call | solution.py:755
  310.7 3.4 %geometry_back.1 = (f32[8,384]{1,0:T(8,128)}, f32[8,1536]{1,0:T(8,128)}) custom-call(f32[3,96,128]{2,1,0:T(8,128)} %get-tuple-element.103.vec, f32[17,96,128]{2,1,0:T(8,128)} %first_back.1.dgeo, s32[96,128]{1,0:T(8,128)} %get-tuple-element.79.refs_1_.nbrs), custom_call_target="tpu_custom_call" | custom-call | tf_op jit(solution)/shard_map/geometry_back/pallas_call | solution.py:831
  316.6 1.8 take_back.5
  318.4 4.5 %collective-permute-start.23 = (f32[8,384]{1,0:T(8,128)}, f32[8,384]{1,0:T(8,128)S(1)}, u32[]{:S(2)}, u32[]{:S(2)}) collective-permute-start(f32[8,384]{1,0:T(8,128)} %get-tuple-element.148), channel_id=1, source_target_pairs={{0,14},{2,0},{4,2},{6,4},{8,6},{10,8},{12,10},{14,12},{1,15},{3,1}... | collective-permute-start | bytes 36872 | tf_op jit(solution)/shard_map/ppermute | solution.py:34
  323.0 4.5 %collective-permute-done.25 = f32[8,128]{1,0:T(8,128)S(1)} collective-permute-done((f32[8,128]{1,0:T(8,128)S(1)}, f32[8,128]{1,0:T(8,128)S(1)}, u32[]{:S(2)}, u32[]{:S(2)}) %collective-permute-start.25) | collective-permute-done | bytes 4128 | tf_op jit(solution)/shard_map/ppermute | solution.py:34
  (105 shorter events, 33.6 us)
Async XLA Ops:
  2.8 12.4 %copy-start.12 = (f32[8,384]{1,0:T(8,128)}, f32[8,384]{1,0:T(8,128)S(1)}, u32[]{:S(2)}) copy-start(f32[8,384]{1,0:T(8,128)S(1)} %maximum_maximum_fusion.own) | copy-start | bytes 36868
  2.8 7.4 %collective-permute-start.1 = (f32[8,384]{1,0:T(8,128)S(1)}, f32[8,384]{1,0:T(8,128)S(1)}, u32[]{:S(2)}, u32[]{:S(2)}) collective-permute-start(f32[8,384]{1,0:T(8,128)S(1)} %maximum_maximum_fusion.own), channel_id=1, source_target_pairs={{0,14},{2,0},{4,2},{6,4},{8,6},{10,8},{12,10},{14,12},{1,15},{3,1}... | collective-permute-start | bytes 36872 | tf_op jit(solution)/shard_map/ppermute | solution.py:34
  8.8 6.4 %collective-permute-start = (f32[8,384]{1,0:T(8,128)S(1)}, f32[8,384]{1,0:T(8,128)S(1)}, u32[]{:S(2)}, u32[]{:S(2)}) collective-permute-start(f32[8,384]{1,0:T(8,128)S(1)} %maximum_maximum_fusion.own), channel_id=1, source_target_pairs={{0,2},{2,4},{4,6},{6,8},{8,10},{10,12},{12,14},{14,0},{1,3},{3,5},... | collective-permute-start | bytes 36872 | tf_op jit(solution)/shard_map/ppermute | solution.py:34
  10.2 5.0 %copy-start.15 = (f32[8,384]{1,0:T(8,128)}, f32[8,384]{1,0:T(8,128)S(1)}, u32[]{:S(2)}) copy-start(f32[8,384]{1,0:T(8,128)S(1)} %collective-permute-done.1.above) | copy-start | bytes 36868
  17.4 5.4 %collective-permute-start.2 = (f32[8,384]{1,0:T(8,128)}, f32[8,384]{1,0:T(8,128)S(1)}, u32[]{:S(2)}, u32[]{:S(2)}) collective-permute-start(f32[8,384]{1,0:T(8,128)} %get-tuple-element.77), channel_id=1, source_target_pairs={{0,1},{1,0},{2,3},{3,2},{4,5},{5,4},{6,7},{7,6},{8,9},{9,8},{10,11... | collective-permute-start | bytes 36872 | tf_op jit(solution)/shard_map/ppermute | solution.py:34
  40.6 22.3 %collective-permute-start.4 = (f32[288,384]{1,0:T(8,128)}, f32[288,384]{1,0:T(8,128)S(1)}, u32[]{:S(2)}, u32[]{:S(2)}) collective-permute-start(f32[288,384]{1,0:T(8,128)} %get-tuple-element.83.refs_0_.refs_2_.refs_9_), channel_id=1, source_target_pairs={{0,14},{2,0},{4,2},{6,4},{8,6},{10,8},{12,10},{14,12},{1,15},{3,1}... | collective-permute-start | bytes 1327112 | tf_op jit(solution)/shard_map/ppermute | solution.py:34
  41.2 21.7 %collective-permute-start.3 = (f32[288,384]{1,0:T(8,128)}, f32[288,384]{1,0:T(8,128)S(1)}, u32[]{:S(2)}, u32[]{:S(2)}) collective-permute-start(f32[288,384]{1,0:T(8,128)} %get-tuple-element.83.refs_0_.refs_2_.refs_9_), channel_id=1, source_target_pairs={{0,2},{2,4},{4,6},{6,8},{8,10},{10,12},{12,14},{14,0},{1,3},{3,5},... | collective-permute-start | bytes 1327112 | tf_op jit(solution)/shard_map/ppermute | solution.py:34
  66.8 2.0 collective-permute-start.5
  96.3 28.8 %collective-permute-start.8 = (f32[288,256]{1,0:T(8,128)}, f32[288,256]{1,0:T(8,128)S(1)}, u32[]{:S(2)}, u32[]{:S(2)}) collective-permute-start(f32[288,256]{1,0:T(8,128)} %get-tuple-element.89.refs_0_.refs_10_), channel_id=1, source_target_pairs={{0,14},{2,0},{4,2},{6,4},{8,6},{10,8},{12,10},{14,12},{1,15},{3,1}... | collective-permute-start | bytes 884744 | tf_op jit(solution)/shard_map/ppermute | solution.py:34
  96.9 28.3 %collective-permute-start.6 = (f32[288,256]{1,0:T(8,128)}, f32[288,256]{1,0:T(8,128)S(1)}, u32[]{:S(2)}, u32[]{:S(2)}) collective-permute-start(f32[288,256]{1,0:T(8,128)} %get-tuple-element.89.refs_0_.refs_10_), channel_id=1, source_target_pairs={{0,2},{2,4},{4,6},{6,8},{8,10},{10,12},{12,14},{14,0},{1,3},{3,5},... | collective-permute-start | bytes 884744 | tf_op jit(solution)/shard_map/ppermute | solution.py:34
  98.4 31.2 %copy-start.2 = (f32[288,256]{1,0:T(8,128)S(1)}, f32[288,256]{1,0:T(8,128)}, u32[]{:S(2)}) copy-start(f32[288,256]{1,0:T(8,128)} %get-tuple-element.89.refs_0_.refs_10_) | copy-start | bytes 884740
  113.8 6.4 %collective-permute-start.9 = (f32[288,128]{1,0:T(8,128)}, f32[288,128]{1,0:T(8,128)S(1)}, u32[]{:S(2)}, u32[]{:S(2)}) collective-permute-start(f32[288,128]{1,0:T(8,128)} %get-tuple-element.96.refs_1_.refs_11_), channel_id=1, source_target_pairs={{0,14},{2,0},{4,2},{6,4},{8,6},{10,8},{12,10},{14,12},{1,15},{3,1}... | collective-permute-start | bytes 442376 | tf_op jit(solution)/shard_map/ppermute | solution.py:34
  117.1 8.1 %collective-permute-start.7 = (f32[288,128]{1,0:T(8,128)}, f32[288,128]{1,0:T(8,128)S(1)}, u32[]{:S(2)}, u32[]{:S(2)}) collective-permute-start(f32[288,128]{1,0:T(8,128)} %get-tuple-element.96.refs_1_.refs_11_), channel_id=1, source_target_pairs={{0,2},{2,4},{4,6},{6,8},{8,10},{10,12},{12,14},{14,0},{1,3},{3,5},... | collective-permute-start | bytes 442376 | tf_op jit(solution)/shard_map/ppermute | solution.py:34
  120.3 4.9 %copy-start.13 = (f32[288,128]{1,0:T(8,128)}, f32[288,128]{1,0:T(8,128)S(1)}, u32[]{:S(2)}) copy-start(f32[288,128]{1,0:T(8,128)S(1)} %collective-permute-done.9.refs_5_.refs_15_) | copy-start | bytes 442372
  129.7 2.0 collective-permute-start.10
  198.9 2.6 collective-permute-start.11
  201.2 6.6 %collective-permute-start.14 = (f32[8,128]{1,0:T(8,128)S(1)}, f32[8,128]{1,0:T(8,128)S(1)}, u32[]{:S(2)}, u32[]{:S(2)}) collective-permute-start(f32[8,128]{1,0:T(8,128)S(1)} %broadcast_in_dim.30), channel_id=1, source_target_pairs={{0,1},{1,0},{2,3},{3,2},{4,5},{5,4},{6,7},{7,6},{8,9},{9,8},{10,11... | collective-permute-start | bytes 12296 | tf_op jit(solution)/shard_map/ppermute | solution.py:34
  205.8 6.2 %collective-permute-start.12 = (f32[288,128]{1,0:T(8,128)}, f32[288,128]{1,0:T(8,128)S(1)}, u32[]{:S(2)}, u32[]{:S(2)}) collective-permute-start(f32[288,128]{1,0:T(8,128)} %get-tuple-element.110), channel_id=1, source_target_pairs={{0,14},{2,0},{4,2},{6,4},{8,6},{10,8},{12,10},{14,12},{1,15},{3,1}... | collective-permute-start | bytes 442376 | tf_op jit(solution)/shard_map/ppermute | solution.py:34
  206.7 8.6 %collective-permute-start.13 = (f32[288,128]{1,0:T(8,128)}, f32[288,128]{1,0:T(8,128)S(1)}, u32[]{:S(2)}, u32[]{:S(2)}) collective-permute-start(f32[288,128]{1,0:T(8,128)} %get-tuple-element.111), channel_id=1, source_target_pairs={{0,2},{2,4},{4,6},{6,8},{8,10},{10,12},{12,14},{14,0},{1,3},{3,5},... | collective-permute-start | bytes 442376 | tf_op jit(solution)/shard_map/ppermute | solution.py:34
  212.1 8.1 %copy-start.20 = (f32[288,128]{1,0:T(8,128)}, f32[288,128]{1,0:T(8,128)S(1)}, u32[]{:S(2)}) copy-start(f32[288,128]{1,0:T(8,128)S(1)} %collective-permute-done.12.refs_3_) | copy-start | bytes 442372
  215.4 4.7 %copy-start.21 = (f32[288,128]{1,0:T(8,128)}, f32[288,128]{1,0:T(8,128)S(1)}, u32[]{:S(2)}) copy-start(f32[288,128]{1,0:T(8,128)S(1)} %collective-permute-done.13.refs_4_) | copy-start | bytes 442372
  215.4 21.1 %collective-permute-start.15 = (f32[8,128]{1,0:T(8,128)S(1)}, f32[8,128]{1,0:T(8,128)S(1)}, u32[]{:S(2)}, u32[]{:S(2)}) collective-permute-start(f32[8,128]{1,0:T(8,128)S(1)} %broadcast_add_fusion), channel_id=1, source_target_pairs={{0,2},{2,4},{4,6},{6,8},{8,10},{10,12},{12,14},{14,0},{1,3},{3,5},... | collective-permute-start | bytes 12296 | tf_op jit(solution)/shard_map/ppermute | solution.py:34
  215.4 21.1 %collective-permute-start.16 = (f32[288,256]{1,0:T(8,128)}, f32[288,256]{1,0:T(8,128)S(1)}, u32[]{:S(2)}, u32[]{:S(2)}) collective-permute-start(f32[288,256]{1,0:T(8,128)} %get-tuple-element.115), channel_id=1, source_target_pairs={{0,14},{2,0},{4,2},{6,4},{8,6},{10,8},{12,10},{14,12},{1,15},{3,1}... | collective-permute-start | bytes 884744 | tf_op jit(solution)/shard_map/ppermute | solution.py:34
  220.1 16.4 %collective-permute-start.17 = (f32[288,256]{1,0:T(8,128)}, f32[288,256]{1,0:T(8,128)S(1)}, u32[]{:S(2)}, u32[]{:S(2)}) collective-permute-start(f32[288,256]{1,0:T(8,128)} %get-tuple-element.116), channel_id=1, source_target_pairs={{0,2},{2,4},{4,6},{6,8},{8,10},{10,12},{12,14},{14,0},{1,3},{3,5},... | collective-permute-start | bytes 884744 | tf_op jit(solution)/shard_map/ppermute | solution.py:34
  267.4 1.9 collective-permute-start.18
  273.6 21.9 %collective-permute-start.20 = (f32[288,384]{1,0:T(8,128)}, f32[288,384]{1,0:T(8,128)S(1)}, u32[]{:S(2)}, u32[]{:S(2)}) collective-permute-start(f32[288,384]{1,0:T(8,128)} %get-tuple-element.137), channel_id=1, source_target_pairs={{0,14},{2,0},{4,2},{6,4},{8,6},{10,8},{12,10},{14,12},{1,15},{3,1}... | collective-permute-start | bytes 1327112 | tf_op jit(solution)/shard_map/ppermute | solution.py:34
  278.3 17.2 %collective-permute-start.21 = (f32[288,384]{1,0:T(8,128)}, f32[288,384]{1,0:T(8,128)S(1)}, u32[]{:S(2)}, u32[]{:S(2)}) collective-permute-start(f32[288,384]{1,0:T(8,128)} %get-tuple-element.138), channel_id=1, source_target_pairs={{0,2},{2,4},{4,6},{6,8},{8,10},{10,12},{12,14},{14,0},{1,3},{3,5},... | collective-permute-start | bytes 1327112 | tf_op jit(solution)/shard_map/ppermute | solution.py:34
  278.3 10.1 %collective-permute-start.19 = (f32[8,128]{1,0:T(8,128)S(1)}, f32[8,128]{1,0:T(8,128)S(1)}, u32[]{:S(2)}, u32[]{:S(2)}) collective-permute-start(f32[8,128]{1,0:T(8,128)S(1)} %add.19), channel_id=1, source_target_pairs={{0,4},{2,6},{4,8},{6,10},{8,12},{10,14},{12,0},{14,2},{1,5},{3,7},... | collective-permute-start | bytes 12296 | tf_op jit(solution)/shard_map/ppermute | solution.py:34
  314.8 1.2 collective-permute-start.22
  318.4 10.2 %collective-permute-start.23 = (f32[8,384]{1,0:T(8,128)}, f32[8,384]{1,0:T(8,128)S(1)}, u32[]{:S(2)}, u32[]{:S(2)}) collective-permute-start(f32[8,384]{1,0:T(8,128)} %get-tuple-element.148), channel_id=1, source_target_pairs={{0,14},{2,0},{4,2},{6,4},{8,6},{10,8},{12,10},{14,12},{1,15},{3,1}... | collective-permute-start | bytes 36872 | tf_op jit(solution)/shard_map/ppermute | solution.py:34
  323.0 6.6 %collective-permute-start.24 = (f32[8,384]{1,0:T(8,128)}, f32[8,384]{1,0:T(8,128)S(1)}, u32[]{:S(2)}, u32[]{:S(2)}) collective-permute-start(f32[8,384]{1,0:T(8,128)} %get-tuple-element.149), channel_id=1, source_target_pairs={{0,2},{2,4},{4,6},{6,8},{8,10},{10,12},{12,14},{14,0},{1,3},{3,5},... | collective-permute-start | bytes 36872 | tf_op jit(solution)/shard_map/ppermute | solution.py:34
  323.0 4.5 %collective-permute-start.25 = (f32[8,128]{1,0:T(8,128)S(1)}, f32[8,128]{1,0:T(8,128)S(1)}, u32[]{:S(2)}, u32[]{:S(2)}) collective-permute-start(f32[8,128]{1,0:T(8,128)S(1)} %add.20), channel_id=1, source_target_pairs={{0,8},{2,10},{4,12},{6,14},{8,0},{10,2},{12,4},{14,6},{1,9},{3,11}... | collective-permute-start | bytes 12296 | tf_op jit(solution)/shard_map/ppermute | solution.py:34
  (16 other events, 11.9 us)
